TPU v7x, 512 devices: a whole 4x4x16 slice. The times are simulated.
512 devices in a mesh: tile: 64 (over x, z), head: 8 (over y, core).
Axes of the slice: x: 4, y: 4, z: 16, core: 2. Of those that a mesh axis runs over, the one named last changes fastest.
Arguments:
- queries: bfloat16 [16384, 2048], P('tile', 'head'), may hold values from -26.5 to 26.5
- keys: bfloat16 [16384, 2048], P('tile', 'head'), may hold values from -26.5 to 26.5
- values: bfloat16 [16384, 2048], P('tile', 'head'), may hold values from -36 to 36
- out_weight: bfloat16 [2048, 2048], P('head'), may hold values from -0.1875 to 0.1875
- teacher: bfloat16 [16384, 2048], P('tile', 'head'), may hold values from -3 to 3
- block_lists: int32 [16, 64, 27], P('head', 'tile'), may hold values from -1 to 63, as said below
Outputs:
- student: bfloat16 [16384, 2048], P('tile', 'head')
- grad_queries: bfloat16 [16384, 2048], P('tile', 'head')
- grad_keys: bfloat16 [16384, 2048], P('tile', 'head')
- grad_values: bfloat16 [16384, 2048], P('tile', 'head')
Inputs may be any that keep to these rules, and one draw needn't show every extreme that they name: `block_lists`: tile c has grid coordinates (c // 32, (c // 8) % 4, c % 8) in a 2 x 4 x 8 grid. Row (h, c) lists, each at most once, tiles within one step of tile c along each of the three grid dimensions; tile c itself is always listed; the other slots hold -1.
All inputs are finite; a program needn't handle non-finite values.
Results may differ from a plain program's by a relative error of at most 0.035.
Values may be sent and summed in bfloat16 or wider, within the bound.
No kernel may reach another device: no remote copies, remote signals or barrier semaphores. Data moves between devices by JAX's collectives and lax.ppermute only.
A program may use at most 64 MiB of HBM per device.

v0:
```python
import jax
import jax.numpy as jnp
from jax import lax
from jax.sharding import PartitionSpec as P

HD = 128
TW = 8


neighbour_steps = ((-1, -1), (-1, 0), (-1, 1), (0, -1), (0, 0), (0, 1), (1, -1), (1, 0), (1, 1))
centre_slot = 4


def shifted(value, axis, steps):
    count = lax.axis_size(axis)
    first, last = (max(0, -steps), min(count, count - steps))
    return lax.ppermute(value, axis, [(source, source + steps) for source in range(first, last)])


def shifted_2(shard, axis, by):
    peers = lax.axis_size(axis)
    return lax.ppermute(shard, axis, [(i, (i + by) % peers) for i in range(peers)])


def window_mask(block_lists, position, half):
    rows_total = half // TW
    within = position % half
    grid_row = within // TW
    grid_col = within % TW
    partner = jnp.where(position < half, position + half, position - half)
    step_rows = jnp.array([offset_pair[0] for offset_pair in neighbour_steps], jnp.int32)
    step_cols = jnp.array([offset_pair[1] for offset_pair in neighbour_steps], jnp.int32)
    inside = (grid_row + step_rows >= 0) & (grid_row + step_rows < rows_total)
    inside = inside & (grid_col + step_cols >= 0) & (grid_col + step_cols < TW)
    moved = step_rows * TW + step_cols
    wanted = jnp.concatenate([position + moved, partner + moved])
    usable = jnp.concatenate([inside, inside])
    listed = jnp.any(block_lists[:, 0, :, None] == wanted[None, None, :], axis=1)
    return listed & usable[None, :]


def fetch_window(keys, values, half):
    near_keys = []
    near_values = []
    for offset_pair in neighbour_steps:
        moved = offset_pair[0] * TW + offset_pair[1]
        if moved == 0:
            near_keys.append(keys)
            near_values.append(values)
        else:
            got_keys, got_values = shifted((keys, values), "tile", -moved)
            near_keys.append(got_keys)
            near_values.append(got_values)
    near_keys = jnp.stack(near_keys)
    near_values = jnp.stack(near_values)
    far_key_list = []
    far_value_list = []
    for offset_pair in neighbour_steps:
        moved = offset_pair[0] * TW + offset_pair[1]
        got_keys, got_values = shifted_2((keys, values), "tile", -(half + moved))
        far_key_list.append(got_keys)
        far_value_list.append(got_values)
    far_keys = jnp.stack(far_key_list)
    far_values = jnp.stack(far_value_list)
    return (jnp.concatenate([near_keys, far_keys]), jnp.concatenate([near_values, far_values]))


def return_parts(key_parts, value_parts, half):
    rows_total = half // TW
    far_base = len(neighbour_steps)
    own_keys = key_parts[centre_slot].astype(jnp.float32)
    own_values = value_parts[centre_slot].astype(jnp.float32)
    for slot_index, offset_pair in enumerate(neighbour_steps):
        moved = offset_pair[0] * TW + offset_pair[1]
        if moved == 0 or (offset_pair[0] != 0 and rows_total == 1):
            continue
        got_keys, got_values = shifted(
            (key_parts[slot_index], value_parts[slot_index]), "tile", moved
        )
        own_keys = own_keys + got_keys.astype(jnp.float32)
        own_values = own_values + got_values.astype(jnp.float32)
    for slot_index, offset_pair in enumerate(neighbour_steps):
        moved = offset_pair[0] * TW + offset_pair[1]
        got_keys, got_values = shifted_2(
            (key_parts[far_base + slot_index], value_parts[far_base + slot_index]),
            "tile",
            half + moved,
        )
        own_keys = own_keys + got_keys.astype(jnp.float32)
        own_values = own_values + got_values.astype(jnp.float32)
    return (own_keys, own_values)


def contract_rows(left, right):
    return lax.dot_general(
        left, right, (((0,), (0,)), ((), ())), preferred_element_type=jnp.float32
    )


def contract_cols(left, right):
    return lax.dot_general(
        left, right, (((1,), (1,)), ((), ())), preferred_element_type=jnp.float32
    )


def body(queries, keys, values, out_weight, teacher, block_lists):
    half = lax.axis_size("tile") // 2
    position = lax.axis_index("tile")
    allowed = window_mask(block_lists, position, half)
    all_keys, all_values = fetch_window(keys, values, half)
    slot_count = all_keys.shape[0]
    tile_rows = queries.shape[0]
    local_width = queries.shape[1]
    key_flat = all_keys.reshape(slot_count * tile_rows, local_width)
    value_flat = all_values.reshape(slot_count * tile_rows, local_width)
    score_scale = HD ** (-0.5)
    head_count = local_width // HD
    outputs = []
    kept_probs = []
    for head_index in range(head_count):
        first = head_index * HD
        query_head = queries[:, first : first + HD]
        column_live = jnp.repeat(allowed[head_index], tile_rows)
        scores = contract_cols(query_head, key_flat[:, first : first + HD]) * score_scale
        scores = jnp.where(column_live[None, :], scores, -jnp.inf)
        highest = jnp.max(scores, axis=1, keepdims=True)
        weights = jnp.exp(scores - highest)
        probs = (weights / jnp.sum(weights, axis=1, keepdims=True)).astype(jnp.bfloat16)
        kept_probs.append(probs)
        outputs.append(
            jnp.dot(
                probs, value_flat[:, first : first + HD], preferred_element_type=jnp.float32
            ).astype(jnp.bfloat16)
        )
    attended = jnp.concatenate(outputs, axis=1)
    partial_rows = jnp.dot(attended, out_weight, preferred_element_type=jnp.float32)
    student = lax.psum_scatter(
        partial_rows.astype(jnp.bfloat16), "head", scatter_dimension=1, tiled=True
    )
    residue = (student.astype(jnp.float32) - teacher.astype(jnp.float32)).astype(jnp.bfloat16)
    grad_attended = contract_cols(
        lax.all_gather(residue, "head", axis=1, tiled=True), out_weight
    ).astype(jnp.bfloat16)
    query_grads = []
    key_pieces = []
    value_pieces = []
    for head_index in range(head_count):
        first = head_index * HD
        query_head = queries[:, first : first + HD]
        grad_head = grad_attended[:, first : first + HD]
        probs = kept_probs[head_index]
        delta = jnp.sum(
            grad_head.astype(jnp.float32) * outputs[head_index].astype(jnp.float32), axis=1
        )
        dprob = contract_cols(grad_head, value_flat[:, first : first + HD])
        dscore = (probs.astype(jnp.float32) * (dprob - delta[:, None])).astype(jnp.bfloat16)
        query_grads.append(
            (
                jnp.dot(dscore, key_flat[:, first : first + HD], preferred_element_type=jnp.float32)
                * score_scale
            ).astype(jnp.bfloat16)
        )
        key_pieces.append((contract_rows(dscore, query_head) * score_scale).astype(jnp.bfloat16))
        value_pieces.append(contract_rows(probs, grad_head).astype(jnp.bfloat16))
    grad_queries = jnp.concatenate(query_grads, axis=1)
    key_parts = jnp.concatenate(key_pieces, axis=1).reshape(slot_count, tile_rows, local_width)
    value_parts = jnp.concatenate(value_pieces, axis=1).reshape(slot_count, tile_rows, local_width)
    grad_keys, grad_values = return_parts(key_parts, value_parts, half)
    return (student, grad_queries, grad_keys.astype(jnp.bfloat16), grad_values.astype(jnp.bfloat16))


def solution(mesh):
    return jax.shard_map(
        body,
        mesh=mesh,
        in_specs=(
            P("tile", "head"),
            P("tile", "head"),
            P("tile", "head"),
            P("head", None),
            P("tile", "head"),
            P("head", "tile", None),
        ),
        out_specs=(P("tile", "head"), P("tile", "head"), P("tile", "head"), P("tile", "head")),
        check_vma=False,
    )
```

profile of v0, /device:TPU:5, one launch (start us, length us, event | category | flops | bytes accessed | tf_op | source)
XLA Modules:
  0.0 1010.7 jit_solution(17084340704729399102)
XLA Ops:
  7.2 15.8 %collective-permute-start.14 = (bf16[256,256]{1,0:T(8,128)(2,1)}, bf16[256,256]{1,0:T(8,128)(2,1)S(1)}, u32[]{:S(2)}, u32[]{:S(2)}) collective-permute-start(bf16[256,256]{1,0:T(8,128)(2,1)} %param.9), channel_id=1, source_target_pairs={{0,200},{8,208},{16,216},{24,224},{32,232},{40,240},{48,248},{56,2... | collective-permute-start | bytes 393224 | tf_op jit(solution)/shard_map/ppermute | solution.py:22
  37.7 27.6 %collective-permute-done = bf16[256,256]{1,0:T(8,128)(2,1)S(1)} collective-permute-done((bf16[256,256]{1,0:T(8,128)(2,1)}, bf16[256,256]{1,0:T(8,128)(2,1)S(1)}, u32[]{:S(2)}, u32[]{:S(2)}) %collective-permute-start) | collective-permute-done | bytes 131104 | tf_op jit(solution)/shard_map/ppermute | solution.py:17
  68.3 14.0 %collective-permute-done.1 = bf16[256,256]{1,0:T(8,128)(2,1)S(1)} collective-permute-done((bf16[256,256]{1,0:T(8,128)(2,1)}, bf16[256,256]{1,0:T(8,128)(2,1)S(1)}, u32[]{:S(2)}, u32[]{:S(2)}) %collective-permute-start.1) | collective-permute-done | bytes 131104 | tf_op jit(solution)/shard_map/ppermute | solution.py:17
  84.3 19.7 %collective-permute-done.2 = bf16[256,256]{1,0:T(8,128)(2,1)S(1)} collective-permute-done((bf16[256,256]{1,0:T(8,128)(2,1)}, bf16[256,256]{1,0:T(8,128)(2,1)S(1)}, u32[]{:S(2)}, u32[]{:S(2)}) %collective-permute-start.2) | collective-permute-done | bytes 131104 | tf_op jit(solution)/shard_map/ppermute | solution.py:17
  138.4 18.0 %collective-permute-start.6 = (bf16[256,256]{1,0:T(8,128)(2,1)}, bf16[256,256]{1,0:T(8,128)(2,1)S(1)}, u32[]{:S(2)}, u32[]{:S(2)}) collective-permute-start(bf16[256,256]{1,0:T(8,128)(2,1)} %param.9), channel_id=1, source_target_pairs={{64,0},{72,8},{80,16},{88,24},{96,32},{104,40},{112,48},{120,56},{... | collective-permute-start | bytes 393224 | tf_op jit(solution)/shard_map/ppermute | solution.py:17
  163.5 21.1 %collective-permute-done.7 = bf16[256,256]{1,0:T(8,128)(2,1)S(1)} collective-permute-done((bf16[256,256]{1,0:T(8,128)(2,1)}, bf16[256,256]{1,0:T(8,128)(2,1)S(1)}, u32[]{:S(2)}, u32[]{:S(2)}) %collective-permute-start.7) | collective-permute-done | bytes 131104 | tf_op jit(solution)/shard_map/ppermute | solution.py:17
  207.3 14.5 %collective-permute-done.9 = bf16[256,256]{1,0:T(8,128)(2,1)S(1)} collective-permute-done((bf16[256,256]{1,0:T(8,128)(2,1)S(1)}, bf16[256,256]{1,0:T(8,128)(2,1)S(1)}, u32[]{:S(2)}, u32[]{:S(2)}) %collective-permute-start.9) | collective-permute-done | bytes 131104 | tf_op jit(solution)/shard_map/ppermute | solution.py:22
  223.7 19.4 %collective-permute-done.10 = bf16[256,256]{1,0:T(8,128)(2,1)S(1)} collective-permute-done((bf16[256,256]{1,0:T(8,128)(2,1)S(1)}, bf16[256,256]{1,0:T(8,128)(2,1)S(1)}, u32[]{:S(2)}, u32[]{:S(2)}) %collective-permute-start.10) | collective-permute-done | bytes 131104 | tf_op jit(solution)/shard_map/ppermute | solution.py:22
  256.4 19.2 %collective-permute-start.31 = (bf16[256,256]{1,0:T(8,128)(2,1)S(1)}, bf16[256,256]{1,0:T(8,128)(2,1)S(1)}, u32[]{:S(2)}, u32[]{:S(2)}) collective-permute-start(bf16[256,256]{1,0:T(8,128)(2,1)S(1)} %copy-done.43), channel_id=1, source_target_pairs={{0,200},{8,208},{16,216},{24,224},{32,232},{40,240},{48,248},{56,2... | collective-permute-start | bytes 393224 | tf_op jit(solution)/shard_map/ppermute | solution.py:22
  285.4 13.8 %collective-permute-start.17 = (bf16[256,256]{1,0:T(8,128)(2,1)S(1)}, bf16[256,256]{1,0:T(8,128)(2,1)S(1)}, u32[]{:S(2)}, u32[]{:S(2)}) collective-permute-start(bf16[256,256]{1,0:T(8,128)(2,1)S(1)} %copy-done.43), channel_id=1, source_target_pairs={{0,72},{8,80},{16,88},{24,96},{32,104},{40,112},{48,120},{56,128},... | collective-permute-start | bytes 393224 | tf_op jit(solution)/shard_map/ppermute | solution.py:17
  304.1 14.0 %collective-permute-done.17 = bf16[256,256]{1,0:T(8,128)(2,1)S(1)} collective-permute-done((bf16[256,256]{1,0:T(8,128)(2,1)S(1)}, bf16[256,256]{1,0:T(8,128)(2,1)S(1)}, u32[]{:S(2)}, u32[]{:S(2)}) %collective-permute-start.17) | collective-permute-done | bytes 131104 | tf_op jit(solution)/shard_map/ppermute | solution.py:17
  320.0 13.4 %collective-permute-done.18 = bf16[256,256]{1,0:T(8,128)(2,1)S(1)} collective-permute-done((bf16[256,256]{1,0:T(8,128)(2,1)S(1)}, bf16[256,256]{1,0:T(8,128)(2,1)S(1)}, u32[]{:S(2)}, u32[]{:S(2)}) %collective-permute-start.18) | collective-permute-done | bytes 131104 | tf_op jit(solution)/shard_map/ppermute | solution.py:17
  343.0 13.8 %collective-permute-done.19 = bf16[256,256]{1,0:T(8,128)(2,1)S(1)} collective-permute-done((bf16[256,256]{1,0:T(8,128)(2,1)S(1)}, bf16[256,256]{1,0:T(8,128)(2,1)S(1)}, u32[]{:S(2)}, u32[]{:S(2)}) %collective-permute-start.19) | collective-permute-done | bytes 131104 | tf_op jit(solution)/shard_map/ppermute | solution.py:17
  381.3 12.3 %collective-permute-done.22 = bf16[256,256]{1,0:T(8,128)(2,1)S(1)} collective-permute-done((bf16[256,256]{1,0:T(8,128)(2,1)S(1)}, bf16[256,256]{1,0:T(8,128)(2,1)S(1)}, u32[]{:S(2)}, u32[]{:S(2)}) %collective-permute-start.22) | collective-permute-done | bytes 131104 | tf_op jit(solution)/shard_map/ppermute | solution.py:17
  409.4 12.6 %collective-permute-start.24 = (bf16[256,256]{1,0:T(8,128)(2,1)S(1)}, bf16[256,256]{1,0:T(8,128)(2,1)S(1)}, u32[]{:S(2)}, u32[]{:S(2)}) collective-permute-start(bf16[256,256]{1,0:T(8,128)(2,1)S(1)} %copy-done.43), channel_id=1, source_target_pairs={{72,0},{80,8},{88,16},{96,24},{104,32},{112,40},{120,48},{128,56},... | collective-permute-start | bytes 393224 | tf_op jit(solution)/shard_map/ppermute | solution.py:17
  428.7 17.6 %collective-permute-start.25 = (bf16[256,256]{1,0:T(8,128)(2,1)S(1)}, bf16[256,256]{1,0:T(8,128)(2,1)S(1)}, u32[]{:S(2)}, u32[]{:S(2)}) collective-permute-start(bf16[256,256]{1,0:T(8,128)(2,1)S(1)} %copy-done.43), channel_id=1, source_target_pairs={{0,328},{8,336},{16,344},{24,352},{32,360},{40,368},{48,376},{56,3... | collective-permute-start | bytes 393224 | tf_op jit(solution)/shard_map/ppermute | solution.py:22
  478.3 17.1 %collective-permute-start.33 = (bf16[256,256]{1,0:T(8,128)(2,1)S(1)}, bf16[256,256]{1,0:T(8,128)(2,1)S(1)}, u32[]{:S(2)}, u32[]{:S(2)}) collective-permute-start(bf16[256,256]{1,0:T(8,128)(2,1)S(1)} %copy-done.43), channel_id=1, source_target_pairs={{0,184},{8,192},{16,200},{24,208},{32,216},{40,224},{48,232},{56,2... | collective-permute-start | bytes 393224 | tf_op jit(solution)/shard_map/ppermute | solution.py:22
  495.4 11.8 %collective-permute-start.32 = (bf16[256,256]{1,0:T(8,128)(2,1)S(1)}, bf16[256,256]{1,0:T(8,128)(2,1)S(1)}, u32[]{:S(2)}, u32[]{:S(2)}) collective-permute-start(bf16[256,256]{1,0:T(8,128)(2,1)S(1)} %copy-done.43), channel_id=1, source_target_pairs={{0,192},{8,200},{16,208},{24,216},{32,224},{40,232},{48,240},{56,2... | collective-permute-start | bytes 393224 | tf_op jit(solution)/shard_map/ppermute | solution.py:22
  507.3 16.2 %collective-permute-done.32 = bf16[256,256]{1,0:T(8,128)(2,1)S(1)} collective-permute-done((bf16[256,256]{1,0:T(8,128)(2,1)S(1)}, bf16[256,256]{1,0:T(8,128)(2,1)S(1)}, u32[]{:S(2)}, u32[]{:S(2)}) %collective-permute-start.32) | collective-permute-done | bytes 131104 | tf_op jit(solution)/shard_map/ppermute | solution.py:22
  526.8 79.6 %reduce-scatter.2.cloned.1.call-done = bf16[256,256]{1,0:T(8,128)(2,1)} async-done(((bf16[256,2048]{1,0:T(8,128)(2,1)}), bf16[256,256]{1,0:T(8,128)(2,1)}) %reduce-scatter.2.cloned.1.call-update) | async-done | bytes 131088 | tf_op jit(solution)/shard_map/reduce_scatter | solution.py:137
  608.1 34.1 %all-gather.2.cloned.1.call-done = bf16[256,2048]{1,0:T(8,128)(2,1)} async-done(((bf16[256,256]{1,0:T(8,128)(2,1)}), bf16[256,2048]{1,0:T(8,128)(2,1)}) %all-gather.2.cloned.1.call-update) | async-done | bytes 1048592 | tf_op jit(solution)/shard_map/all_gather | solution.py:142
  651.1 13.1 %collective-permute-start.43 = (bf16[256,256]{0,1:T(8,128)(2,1)S(1)}, bf16[256,256]{0,1:T(8,128)(2,1)S(1)}, u32[]{:S(2)}, u32[]{:S(2)}) collective-permute-start(bf16[256,256]{0,1:T(8,128)(2,1)S(1)} %get-tuple-element.40), channel_id=1, source_target_pairs={{0,192},{8,200},{16,208},{24,216},{32,224},{40,232},{48,240},{56,2... | collective-permute-start | bytes 393224 | tf_op jit(solution)/shard_map/ppermute | solution.py:22
  677.7 12.6 %collective-permute-start.48 = (bf16[256,256]{0,1:T(8,128)(2,1)S(1)}, bf16[256,256]{0,1:T(8,128)(2,1)S(1)}, u32[]{:S(2)}, u32[]{:S(2)}) collective-permute-start(bf16[256,256]{0,1:T(8,128)(2,1)S(1)} %get-tuple-element.45), channel_id=1, source_target_pairs={{0,312},{8,320},{16,328},{24,336},{32,344},{40,352},{48,360},{56,3... | collective-permute-start | bytes 393224 | tf_op jit(solution)/shard_map/ppermute | solution.py:22
  692.1 15.2 %collective-permute-start.50 = (bf16[256,256]{0,1:T(8,128)(2,1)S(1)}, bf16[256,256]{0,1:T(8,128)(2,1)S(1)}, u32[]{:S(2)}, u32[]{:S(2)}) collective-permute-start(bf16[256,256]{0,1:T(8,128)(2,1)S(1)} %get-tuple-element.46), channel_id=1, source_target_pairs={{0,328},{8,336},{16,344},{24,352},{32,360},{40,368},{48,376},{56,3... | collective-permute-start | bytes 393224 | tf_op jit(solution)/shard_map/ppermute | solution.py:22
  737.1 21.9 %collective-permute-start.64 = (bf16[256,256]{0,1:T(8,128)(2,1)S(1)}, bf16[256,256]{0,1:T(8,128)(2,1)S(1)}, u32[]{:S(2)}, u32[]{:S(2)}) collective-permute-start(bf16[256,256]{0,1:T(8,128)(2,1)S(1)} %get-tuple-element.27), channel_id=1, source_target_pairs={{0,264},{8,272},{16,280},{24,288},{32,296},{40,304},{48,312},{56,3... | collective-permute-start | bytes 393224 | tf_op jit(solution)/shard_map/ppermute | solution.py:22
  766.2 13.5 %collective-permute-start.67 = (bf16[256,256]{0,1:T(8,128)(2,1)S(1)}, bf16[256,256]{0,1:T(8,128)(2,1)S(1)}, u32[]{:S(2)}, u32[]{:S(2)}) collective-permute-start(bf16[256,256]{0,1:T(8,128)(2,1)S(1)} %get-tuple-element.29), channel_id=1, source_target_pairs={{0,328},{8,336},{16,344},{24,352},{32,360},{40,368},{48,376},{56,3... | collective-permute-start | bytes 393224 | tf_op jit(solution)/shard_map/ppermute | solution.py:22
  797.1 12.2 %collective-permute-start.36 = (bf16[256,256]{0,1:T(8,128)(2,1)S(1)}, bf16[256,256]{0,1:T(8,128)(2,1)S(1)}, u32[]{:S(2)}, u32[]{:S(2)}) collective-permute-start(bf16[256,256]{0,1:T(8,128)(2,1)S(1)} %get-tuple-element.33), channel_id=1, source_target_pairs={{56,0},{64,8},{72,16},{80,24},{88,32},{96,40},{104,48},{112,56},{1... | collective-permute-start | bytes 393224 | tf_op jit(solution)/shard_map/ppermute | solution.py:17
  836.8 15.6 %collective-permute-start.41 = (bf16[256,256]{0,1:T(8,128)(2,1)S(1)}, bf16[256,256]{0,1:T(8,128)(2,1)S(1)}, u32[]{:S(2)}, u32[]{:S(2)}) collective-permute-start(bf16[256,256]{0,1:T(8,128)(2,1)S(1)} %get-tuple-element.38), channel_id=1, source_target_pairs={{0,72},{8,80},{16,88},{24,96},{32,104},{40,112},{48,120},{56,128},... | collective-permute-start | bytes 393224 | tf_op jit(solution)/shard_map/ppermute | solution.py:17
  863.8 30.1 %collective-permute-start.52 = (bf16[256,256]{0,1:T(8,128)(2,1)S(1)}, bf16[256,256]{0,1:T(8,128)(2,1)S(1)}, u32[]{:S(2)}, u32[]{:S(2)}) collective-permute-start(bf16[256,256]{0,1:T(8,128)(2,1)S(1)} %get-tuple-element.15), channel_id=1, source_target_pairs={{64,0},{72,8},{80,16},{88,24},{96,32},{104,40},{112,48},{120,56},{... | collective-permute-start | bytes 393224 | tf_op jit(solution)/shard_map/ppermute | solution.py:17
  899.6 16.9 %collective-permute-start.55 = (bf16[256,256]{0,1:T(8,128)(2,1)}, bf16[256,256]{0,1:T(8,128)(2,1)}, u32[]{:S(2)}, u32[]{:S(2)}) collective-permute-start(bf16[256,256]{0,1:T(8,128)(2,1)} %get-tuple-element.18), channel_id=1, source_target_pairs={{0,8},{8,16},{16,24},{24,32},{32,40},{40,48},{48,56},{56,64},{64,7... | collective-permute-start | bytes 393224 | tf_op jit(solution)/shard_map/ppermute | solution.py:17
  918.5 44.2 %collective-permute-start.57 = (bf16[256,256]{0,1:T(8,128)(2,1)}, bf16[256,256]{0,1:T(8,128)(2,1)}, u32[]{:S(2)}, u32[]{:S(2)}) collective-permute-start(bf16[256,256]{0,1:T(8,128)(2,1)} %get-tuple-element.20), channel_id=1, source_target_pairs={{0,64},{8,72},{16,80},{24,88},{32,96},{40,104},{48,112},{56,120},{... | collective-permute-start | bytes 393224 | tf_op jit(solution)/shard_map/ppermute | solution.py:17
  979.9 21.3 %collective-permute-done.59 = bf16[256,256]{0,1:T(8,128)(2,1)} collective-permute-done((bf16[256,256]{0,1:T(8,128)(2,1)}, bf16[256,256]{0,1:T(8,128)(2,1)}, u32[]{:S(2)}, u32[]{:S(2)}) %collective-permute-start.59) | collective-permute-done | bytes 131104 | tf_op jit(solution)/shard_map/ppermute | solution.py:22
  (279 shorter events, 353.0 us)
Async XLA Ops:
  7.2 599.2 %reduce-scatter.2.cloned.1.call-start = ((), (), s32[]{:S(2)}) async-start(), calls=%async_computation.1 | async-start | bytes 1179648 | tf_op jit(solution)/shard_map/reduce_scatter | solution.py:137
  7.2 270.3 %collective-permute-start.14 = (bf16[256,256]{1,0:T(8,128)(2,1)}, bf16[256,256]{1,0:T(8,128)(2,1)S(1)}, u32[]{:S(2)}, u32[]{:S(2)}) collective-permute-start(bf16[256,256]{1,0:T(8,128)(2,1)} %param.9), channel_id=1, source_target_pairs={{0,200},{8,208},{16,216},{24,224},{32,232},{40,240},{48,248},{56,2... | collective-permute-start | bytes 393224 | tf_op jit(solution)/shard_map/ppermute | solution.py:22
  23.0 252.6 %collective-permute-start.13 = (bf16[256,256]{1,0:T(8,128)(2,1)}, bf16[256,256]{1,0:T(8,128)(2,1)S(1)}, u32[]{:S(2)}, u32[]{:S(2)}) collective-permute-start(bf16[256,256]{1,0:T(8,128)(2,1)} %param.9), channel_id=1, source_target_pairs={{0,248},{8,256},{16,264},{24,272},{32,280},{40,288},{48,296},{56,3... | collective-permute-start | bytes 393224 | tf_op jit(solution)/shard_map/ppermute | solution.py:22
  26.5 229.8 %collective-permute-start.12 = (bf16[256,256]{1,0:T(8,128)(2,1)}, bf16[256,256]{1,0:T(8,128)(2,1)S(1)}, u32[]{:S(2)}, u32[]{:S(2)}) collective-permute-start(bf16[256,256]{1,0:T(8,128)(2,1)} %param.9), channel_id=1, source_target_pairs={{0,256},{8,264},{16,272},{24,280},{32,288},{40,296},{48,304},{56,3... | collective-permute-start | bytes 393224 | tf_op jit(solution)/shard_map/ppermute | solution.py:22
  29.7 216.5 %collective-permute-start.11 = (bf16[256,256]{1,0:T(8,128)(2,1)}, bf16[256,256]{1,0:T(8,128)(2,1)S(1)}, u32[]{:S(2)}, u32[]{:S(2)}) collective-permute-start(bf16[256,256]{1,0:T(8,128)(2,1)} %param.9), channel_id=1, source_target_pairs={{0,264},{8,272},{16,280},{24,288},{32,296},{40,304},{48,312},{56,3... | collective-permute-start | bytes 393224 | tf_op jit(solution)/shard_map/ppermute | solution.py:22
  256.4 250.9 %collective-permute-start.31 = (bf16[256,256]{1,0:T(8,128)(2,1)S(1)}, bf16[256,256]{1,0:T(8,128)(2,1)S(1)}, u32[]{:S(2)}, u32[]{:S(2)}) collective-permute-start(bf16[256,256]{1,0:T(8,128)(2,1)S(1)} %copy-done.43), channel_id=1, source_target_pairs={{0,200},{8,208},{16,216},{24,224},{32,232},{40,240},{48,248},{56,2... | collective-permute-start | bytes 393224 | tf_op jit(solution)/shard_map/ppermute | solution.py:22
  275.6 231.7 %collective-permute-start.30 = (bf16[256,256]{1,0:T(8,128)(2,1)S(1)}, bf16[256,256]{1,0:T(8,128)(2,1)S(1)}, u32[]{:S(2)}, u32[]{:S(2)}) collective-permute-start(bf16[256,256]{1,0:T(8,128)(2,1)S(1)} %copy-done.43), channel_id=1, source_target_pairs={{0,248},{8,256},{16,264},{24,272},{32,280},{40,288},{48,296},{56,3... | collective-permute-start | bytes 393224 | tf_op jit(solution)/shard_map/ppermute | solution.py:22
  277.5 229.7 %collective-permute-start.29 = (bf16[256,256]{1,0:T(8,128)(2,1)S(1)}, bf16[256,256]{1,0:T(8,128)(2,1)S(1)}, u32[]{:S(2)}, u32[]{:S(2)}) collective-permute-start(bf16[256,256]{1,0:T(8,128)(2,1)S(1)} %copy-done.43), channel_id=1, source_target_pairs={{0,256},{8,264},{16,272},{24,280},{32,288},{40,296},{48,304},{56,3... | collective-permute-start | bytes 393224 | tf_op jit(solution)/shard_map/ppermute | solution.py:22
  279.5 215.9 %collective-permute-start.28 = (bf16[256,256]{1,0:T(8,128)(2,1)S(1)}, bf16[256,256]{1,0:T(8,128)(2,1)S(1)}, u32[]{:S(2)}, u32[]{:S(2)}) collective-permute-start(bf16[256,256]{1,0:T(8,128)(2,1)S(1)} %copy-done.43), channel_id=1, source_target_pairs={{0,264},{8,272},{16,280},{24,288},{32,296},{40,304},{48,312},{56,3... | collective-permute-start | bytes 393224 | tf_op jit(solution)/shard_map/ppermute | solution.py:22
  478.3 45.2 %collective-permute-start.33 = (bf16[256,256]{1,0:T(8,128)(2,1)S(1)}, bf16[256,256]{1,0:T(8,128)(2,1)S(1)}, u32[]{:S(2)}, u32[]{:S(2)}) collective-permute-start(bf16[256,256]{1,0:T(8,128)(2,1)S(1)} %copy-done.43), channel_id=1, source_target_pairs={{0,184},{8,192},{16,200},{24,208},{32,216},{40,224},{48,232},{56,2... | collective-permute-start | bytes 393224 | tf_op jit(solution)/shard_map/ppermute | solution.py:22
  526.5 115.6 %all-gather.2.cloned.1.call-start = ((), (), s32[]{:S(2)}) async-start(), calls=%async_computation.2 | async-start | bytes 1179648 | tf_op jit(solution)/shard_map/all_gather | solution.py:142
  672.8 49.5 %collective-permute-start.47 = (bf16[256,256]{0,1:T(8,128)(2,1)S(1)}, bf16[256,256]{0,1:T(8,128)(2,1)S(1)}, u32[]{:S(2)}, u32[]{:S(2)}) collective-permute-start(bf16[256,256]{0,1:T(8,128)(2,1)S(1)} %get-tuple-element.44), channel_id=1, source_target_pairs={{0,264},{8,272},{16,280},{24,288},{32,296},{40,304},{48,312},{56,3... | collective-permute-start | bytes 393224 | tf_op jit(solution)/shard_map/ppermute | solution.py:22
  677.7 48.6 %collective-permute-start.48 = (bf16[256,256]{0,1:T(8,128)(2,1)S(1)}, bf16[256,256]{0,1:T(8,128)(2,1)S(1)}, u32[]{:S(2)}, u32[]{:S(2)}) collective-permute-start(bf16[256,256]{0,1:T(8,128)(2,1)S(1)} %get-tuple-element.45), channel_id=1, source_target_pairs={{0,312},{8,320},{16,328},{24,336},{32,344},{40,352},{48,360},{56,3... | collective-permute-start | bytes 393224 | tf_op jit(solution)/shard_map/ppermute | solution.py:22
  692.1 43.0 %collective-permute-start.50 = (bf16[256,256]{0,1:T(8,128)(2,1)S(1)}, bf16[256,256]{0,1:T(8,128)(2,1)S(1)}, u32[]{:S(2)}, u32[]{:S(2)}) collective-permute-start(bf16[256,256]{0,1:T(8,128)(2,1)S(1)} %get-tuple-element.46), channel_id=1, source_target_pairs={{0,328},{8,336},{16,344},{24,352},{32,360},{40,368},{48,376},{56,3... | collective-permute-start | bytes 393224 | tf_op jit(solution)/shard_map/ppermute | solution.py:22
  710.6 48.4 %collective-permute-start.60 = (bf16[256,256]{0,1:T(8,128)(2,1)S(1)}, bf16[256,256]{0,1:T(8,128)(2,1)S(1)}, u32[]{:S(2)}, u32[]{:S(2)}) collective-permute-start(bf16[256,256]{0,1:T(8,128)(2,1)S(1)} %get-tuple-element.23), channel_id=1, source_target_pairs={{0,192},{8,200},{16,208},{24,216},{32,224},{40,232},{48,240},{56,2... | collective-permute-start | bytes 393224 | tf_op jit(solution)/shard_map/ppermute | solution.py:22
  722.3 43.9 %collective-permute-start.61 = (bf16[256,256]{0,1:T(8,128)(2,1)S(1)}, bf16[256,256]{0,1:T(8,128)(2,1)S(1)}, u32[]{:S(2)}, u32[]{:S(2)}) collective-permute-start(bf16[256,256]{0,1:T(8,128)(2,1)S(1)} %get-tuple-element.24), channel_id=1, source_target_pairs={{0,200},{8,208},{16,216},{24,224},{32,232},{40,240},{48,248},{56,2... | collective-permute-start | bytes 393224 | tf_op jit(solution)/shard_map/ppermute | solution.py:22
  726.2 53.5 %collective-permute-start.62 = (bf16[256,256]{0,1:T(8,128)(2,1)S(1)}, bf16[256,256]{0,1:T(8,128)(2,1)S(1)}, u32[]{:S(2)}, u32[]{:S(2)}) collective-permute-start(bf16[256,256]{0,1:T(8,128)(2,1)S(1)} %get-tuple-element.25), channel_id=1, source_target_pairs={{0,248},{8,256},{16,264},{24,272},{32,280},{40,288},{48,296},{56,3... | collective-permute-start | bytes 393224 | tf_op jit(solution)/shard_map/ppermute | solution.py:22
  735.1 52.6 %collective-permute-start.63 = (bf16[256,256]{0,1:T(8,128)(2,1)S(1)}, bf16[256,256]{0,1:T(8,128)(2,1)S(1)}, u32[]{:S(2)}, u32[]{:S(2)}) collective-permute-start(bf16[256,256]{0,1:T(8,128)(2,1)S(1)} %get-tuple-element.26), channel_id=1, source_target_pairs={{0,256},{8,264},{16,272},{24,280},{32,288},{40,296},{48,304},{56,3... | collective-permute-start | bytes 393224 | tf_op jit(solution)/shard_map/ppermute | solution.py:22
  737.1 52.6 %collective-permute-start.64 = (bf16[256,256]{0,1:T(8,128)(2,1)S(1)}, bf16[256,256]{0,1:T(8,128)(2,1)S(1)}, u32[]{:S(2)}, u32[]{:S(2)}) collective-permute-start(bf16[256,256]{0,1:T(8,128)(2,1)S(1)} %get-tuple-element.27), channel_id=1, source_target_pairs={{0,264},{8,272},{16,280},{24,288},{32,296},{40,304},{48,312},{56,3... | collective-permute-start | bytes 393224 | tf_op jit(solution)/shard_map/ppermute | solution.py:22
  766.2 43.8 %collective-permute-start.67 = (bf16[256,256]{0,1:T(8,128)(2,1)S(1)}, bf16[256,256]{0,1:T(8,128)(2,1)S(1)}, u32[]{:S(2)}, u32[]{:S(2)}) collective-permute-start(bf16[256,256]{0,1:T(8,128)(2,1)S(1)} %get-tuple-element.29), channel_id=1, source_target_pairs={{0,328},{8,336},{16,344},{24,352},{32,360},{40,368},{48,376},{56,3... | collective-permute-start | bytes 393224 | tf_op jit(solution)/shard_map/ppermute | solution.py:22
  789.7 43.7 %collective-permute-start.35 = (bf16[256,256]{0,1:T(8,128)(2,1)S(1)}, bf16[256,256]{0,1:T(8,128)(2,1)S(1)}, u32[]{:S(2)}, u32[]{:S(2)}) collective-permute-start(bf16[256,256]{0,1:T(8,128)(2,1)S(1)} %get-tuple-element.32), channel_id=1, source_target_pairs={{64,0},{72,8},{80,16},{88,24},{96,32},{104,40},{112,48},{120,56},{... | collective-permute-start | bytes 393224 | tf_op jit(solution)/shard_map/ppermute | solution.py:17
  810.0 43.3 %collective-permute-start.37 = (bf16[256,256]{0,1:T(8,128)(2,1)S(1)}, bf16[256,256]{0,1:T(8,128)(2,1)S(1)}, u32[]{:S(2)}, u32[]{:S(2)}) collective-permute-start(bf16[256,256]{0,1:T(8,128)(2,1)S(1)} %get-tuple-element.34), channel_id=1, source_target_pairs={{8,0},{16,8},{24,16},{32,24},{40,32},{48,40},{56,48},{64,56},{72,6... | collective-permute-start | bytes 393224 | tf_op jit(solution)/shard_map/ppermute | solution.py:17
  833.4 60.5 %collective-permute-start.40 = (bf16[256,256]{0,1:T(8,128)(2,1)S(1)}, bf16[256,256]{0,1:T(8,128)(2,1)S(1)}, u32[]{:S(2)}, u32[]{:S(2)}) collective-permute-start(bf16[256,256]{0,1:T(8,128)(2,1)S(1)} %get-tuple-element.37), channel_id=1, source_target_pairs={{0,64},{8,72},{16,80},{24,88},{32,96},{40,104},{48,112},{56,120},{... | collective-permute-start | bytes 393224 | tf_op jit(solution)/shard_map/ppermute | solution.py:17
  836.8 59.1 %collective-permute-start.41 = (bf16[256,256]{0,1:T(8,128)(2,1)S(1)}, bf16[256,256]{0,1:T(8,128)(2,1)S(1)}, u32[]{:S(2)}, u32[]{:S(2)}) collective-permute-start(bf16[256,256]{0,1:T(8,128)(2,1)S(1)} %get-tuple-element.38), channel_id=1, source_target_pairs={{0,72},{8,80},{16,88},{24,96},{32,104},{40,112},{48,120},{56,128},... | collective-permute-start | bytes 393224 | tf_op jit(solution)/shard_map/ppermute | solution.py:17
  853.3 46.3 %collective-permute-start.42 = (bf16[256,256]{0,1:T(8,128)(2,1)S(1)}, bf16[256,256]{0,1:T(8,128)(2,1)S(1)}, u32[]{:S(2)}, u32[]{:S(2)}) collective-permute-start(bf16[256,256]{0,1:T(8,128)(2,1)S(1)} %get-tuple-element.39), channel_id=1, source_target_pairs={{0,184},{8,192},{16,200},{24,208},{32,216},{40,224},{48,232},{56,2... | collective-permute-start | bytes 393224 | tf_op jit(solution)/shard_map/ppermute | solution.py:22
  855.2 61.3 %collective-permute-start.51 = (bf16[256,256]{0,1:T(8,128)(2,1)S(1)}, bf16[256,256]{0,1:T(8,128)(2,1)S(1)}, u32[]{:S(2)}, u32[]{:S(2)}) collective-permute-start(bf16[256,256]{0,1:T(8,128)(2,1)S(1)} %get-tuple-element.14), channel_id=1, source_target_pairs={{72,0},{80,8},{88,16},{96,24},{104,32},{112,40},{120,48},{128,56},... | collective-permute-start | bytes 393224 | tf_op jit(solution)/shard_map/ppermute | solution.py:17
  863.8 54.7 %collective-permute-start.52 = (bf16[256,256]{0,1:T(8,128)(2,1)S(1)}, bf16[256,256]{0,1:T(8,128)(2,1)S(1)}, u32[]{:S(2)}, u32[]{:S(2)}) collective-permute-start(bf16[256,256]{0,1:T(8,128)(2,1)S(1)} %get-tuple-element.15), channel_id=1, source_target_pairs={{64,0},{72,8},{80,16},{88,24},{96,32},{104,40},{112,48},{120,56},{... | collective-permute-start | bytes 393224 | tf_op jit(solution)/shard_map/ppermute | solution.py:17
  893.9 68.7 %collective-permute-start.53 = (bf16[256,256]{0,1:T(8,128)(2,1)S(1)}, bf16[256,256]{0,1:T(8,128)(2,1)S(1)}, u32[]{:S(2)}, u32[]{:S(2)}) collective-permute-start(bf16[256,256]{0,1:T(8,128)(2,1)S(1)} %get-tuple-element.16), channel_id=1, source_target_pairs={{56,0},{64,8},{72,16},{80,24},{88,32},{96,40},{104,48},{112,56},{1... | collective-permute-start | bytes 393224 | tf_op jit(solution)/shard_map/ppermute | solution.py:17
  895.9 68.7 %collective-permute-start.54 = (bf16[256,256]{0,1:T(8,128)(2,1)S(1)}, bf16[256,256]{0,1:T(8,128)(2,1)S(1)}, u32[]{:S(2)}, u32[]{:S(2)}) collective-permute-start(bf16[256,256]{0,1:T(8,128)(2,1)S(1)} %get-tuple-element.17), channel_id=1, source_target_pairs={{8,0},{16,8},{24,16},{32,24},{40,32},{48,40},{56,48},{64,56},{72,6... | collective-permute-start | bytes 393224 | tf_op jit(solution)/shard_map/ppermute | solution.py:17
  899.6 70.4 %collective-permute-start.55 = (bf16[256,256]{0,1:T(8,128)(2,1)}, bf16[256,256]{0,1:T(8,128)(2,1)}, u32[]{:S(2)}, u32[]{:S(2)}) collective-permute-start(bf16[256,256]{0,1:T(8,128)(2,1)} %get-tuple-element.18), channel_id=1, source_target_pairs={{0,8},{8,16},{16,24},{24,32},{32,40},{40,48},{48,56},{56,64},{64,7... | collective-permute-start | bytes 393224 | tf_op jit(solution)/shard_map/ppermute | solution.py:17
  916.5 53.5 %collective-permute-start.56 = (bf16[256,256]{0,1:T(8,128)(2,1)}, bf16[256,256]{0,1:T(8,128)(2,1)}, u32[]{:S(2)}, u32[]{:S(2)}) collective-permute-start(bf16[256,256]{0,1:T(8,128)(2,1)} %get-tuple-element.19), channel_id=1, source_target_pairs={{0,56},{8,64},{16,72},{24,80},{32,88},{40,96},{48,104},{56,112},{6... | collective-permute-start | bytes 393224 | tf_op jit(solution)/shard_map/ppermute | solution.py:17
  918.5 61.5 %collective-permute-start.57 = (bf16[256,256]{0,1:T(8,128)(2,1)}, bf16[256,256]{0,1:T(8,128)(2,1)}, u32[]{:S(2)}, u32[]{:S(2)}) collective-permute-start(bf16[256,256]{0,1:T(8,128)(2,1)} %get-tuple-element.20), channel_id=1, source_target_pairs={{0,64},{8,72},{16,80},{24,88},{32,96},{40,104},{48,112},{56,120},{... | collective-permute-start | bytes 393224 | tf_op jit(solution)/shard_map/ppermute | solution.py:17
  (84 other events, 4554.2 us)
Sparse Core Ops, SparseCore 0:
  526.7 79.6 reduce-scatter.1
  609.1 33.0 all-gather.1
where the time goes:
time: 1010 us
  starting transfers between devices  535 us (53%)
  waiting for transfers between devices  428 us (42%)
  between operations  15.9 us (2%)
  matrix products  13 us (1%)
  other arithmetic  11.8 us (1%)
    ppermute x36, starting transfers between devices, shifted_2(): lax.ppermute(shard, axis, [(i, (i + by) % peers) for i in range(peers)])  268 us
    ppermute x32, starting transfers between devices, shifted(): lax.ppermute(value, axis, [(source, source + steps) for source in range(f...  267 us
    ppermute x32, waiting for transfers between devices, shifted(): lax.ppermute(value, axis, [(source, source + steps) for source in range(f...  195 us
    ppermute x36, waiting for transfers between devices, shifted_2(): lax.ppermute(shard, axis, [(i, (i + by) % peers) for i in range(peers)])  119 us
    reduce_scatter x1, waiting for transfers between devices, body(): lax.psum_scatter(partial_rows.astype(jnp.bfloat16), 'head', scatter_dimen...  79.6 us
    all_gather x1, waiting for transfers between devices, body(): lax.all_gather(residue, 'head', axis=1, tiled=True)  34.1 us
  transfers between devices with their start and end apart: 70, of which 33 were waited for; matrix products, arithmetic and copies ran while one was open for 1% of the time, Pallas kernels for 0%

commit v1 on v0

v1 whole, which is shorter than its diff:
```python
import jax
import jax.numpy as jnp
from jax import lax
from jax.experimental import pallas as pl
from jax.experimental.pallas import tpu as pltpu
from jax.sharding import Mesh, PartitionSpec as P

HD = 128
TW = 8
TILE = 256
SLOTS = 18
MASKED = -1e30
SCORE_SCALE = HD ** (-0.5)
LOG2_E = 1.4426950408889634

TILE_AXES = ("xf", "xr", "zr", "zc")
HEAD_AXES = ("y", "core")


def contract_last(left, right):
    return lax.dot_general(left, right, (((1,), (1,)), ((), ())), preferred_element_type=jnp.float32)


def contract_first(left, right):
    return lax.dot_general(left, right, (((0,), (0,)), ((), ())), preferred_element_type=jnp.float32)


def contract_inner(left, right):
    return lax.dot_general(left, right, (((1,), (0,)), ((), ())), preferred_element_type=jnp.float32)


def slot_refs(refs):
    return [(ref, index) for ref in refs for index in range(ref.shape[0])]


def forward_kernel(q_ref, bias_ref, *refs):
    windows, (weights_ref, attended_ref, inverse_ref, scores_ref) = refs[:6], refs[6:]
    slots = slot_refs(windows)
    for f in range(2):
        cols = slice(f * TILE, (f + 1) * TILE)
        query = q_ref[cols, :]
        highest = jnp.full((8, TILE), -jnp.inf, jnp.float32)
        for s, (ref, index) in enumerate(slots):
            scores = contract_last(ref[index, 0], query) * (SCORE_SCALE * LOG2_E)
            scores = scores + bias_ref[s : s + 1, cols]
            scores_ref[s] = scores
            highest = jnp.maximum(highest, jnp.max(scores.reshape(TILE // 8, 8, TILE), axis=0))
        highest = jnp.max(highest, axis=0, keepdims=True)
        total = jnp.zeros((8, TILE), jnp.float32)
        summed = jnp.zeros((HD, TILE), jnp.float32)
        for s, (ref, index) in enumerate(slots):
            weights = jnp.exp2(scores_ref[s] - highest)
            total = total + jnp.sum(weights.reshape(TILE // 8, 8, TILE), axis=0)
            weights = weights.astype(jnp.bfloat16)
            weights_ref[s, :, cols] = weights
            summed = summed + contract_first(ref[index, 1], weights)
        inverse = 1.0 / jnp.sum(total, axis=0, keepdims=True)
        inverse_ref[:, cols] = jnp.broadcast_to(inverse, (8, TILE))
        attended_ref[cols, :] = (summed * inverse).T.astype(jnp.bfloat16)


def backward_kernel(q_ref, grad_ref, attended_ref, inverse_ref, weights_ref, *refs):
    windows, (grad_q_ref, *parts) = refs[:6], refs[6:]
    slots = slot_refs(windows)
    outs = slot_refs(parts)
    queries = [q_ref[f * TILE : (f + 1) * TILE, :] for f in range(2)]
    grads = [grad_ref[f * TILE : (f + 1) * TILE, :] for f in range(2)]
    deltas = []
    for f in range(2):
        product = grads[f].astype(jnp.float32) * attended_ref[f * TILE : (f + 1) * TILE, :].astype(jnp.float32)
        deltas.append(jnp.sum(product.T, axis=0, keepdims=True))
    grad_q = [jnp.zeros((HD, TILE), jnp.float32) for _ in range(2)]
    for s, ((ref, index), (out, out_index)) in enumerate(zip(slots, outs)):
        key, value = ref[index, 0], ref[index, 1]
        grad_key = jnp.zeros((TILE, HD), jnp.float32)
        grad_value = jnp.zeros((TILE, HD), jnp.float32)
        for f in range(2):
            cols = slice(f * TILE, (f + 1) * TILE)
            dprob = contract_last(value, grads[f])
            probs = weights_ref[s, :, cols].astype(jnp.float32) * inverse_ref[0:1, cols]
            dscore = (probs * (dprob - deltas[f])).astype(jnp.bfloat16)
            grad_key = grad_key + contract_inner(dscore, queries[f])
            grad_value = grad_value + contract_inner(probs.astype(jnp.bfloat16), grads[f])
            grad_q[f] = grad_q[f] + contract_first(key, dscore)
        out[out_index, 0] = (grad_key * SCORE_SCALE).astype(jnp.bfloat16)
        out[out_index, 1] = grad_value.astype(jnp.bfloat16)
    for f in range(2):
        grad_q_ref[f * TILE : (f + 1) * TILE, :] = (grad_q[f] * SCORE_SCALE).T.astype(jnp.bfloat16)


def project_kernel(group_ref, attended_ref, weight_ref, teacher_ref, student_ref, grad_ref, total_ref):
    step = pl.program_id(0)
    group = group_ref[0]
    acc = jnp.zeros((TILE, TILE), jnp.float32)
    for g in range(8):
        rows = jnp.concatenate([attended_ref[0, g], attended_ref[1, g]], axis=1)
        acc = acc + contract_inner(rows, weight_ref[g])
    student = acc.astype(jnp.bfloat16)

    @pl.when(step == group)
    def _():
        student_ref[...] = student

    residue = (student.astype(jnp.float32) - teacher_ref[0].astype(jnp.float32)).astype(jnp.bfloat16)
    update = contract_last(residue, weight_ref[group])

    @pl.when(step == 0)
    def _():
        total_ref[...] = update

    @pl.when(step > 0)
    def _():
        total_ref[...] += update

    @pl.when(step == 7)
    def _():
        grad_ref[...] = total_ref[...].astype(jnp.bfloat16)


def vmem_specs(count):
    return [pl.BlockSpec(memory_space=pltpu.VMEM) for _ in range(count)]


def forward(query, bias, windows):
    return pl.pallas_call(
        forward_kernel,
        out_shape=(
            jax.ShapeDtypeStruct((SLOTS, TILE, 2 * TILE), jnp.bfloat16),
            jax.ShapeDtypeStruct((2 * TILE, HD), jnp.bfloat16),
            jax.ShapeDtypeStruct((8, 2 * TILE), jnp.float32),
        ),
        in_specs=vmem_specs(2 + len(windows)),
        out_specs=tuple(vmem_specs(3)),
        scratch_shapes=[pltpu.VMEM((SLOTS, TILE, TILE), jnp.float32)],
        compiler_params=pltpu.CompilerParams(vmem_limit_bytes=48 * 1024 * 1024),
        cost_estimate=pl.CostEstimate(flops=3_000_000_000, bytes_accessed=8_000_000, transcendentals=2_400_000),
        name="attend",
    )(query, bias, *windows)


def backward(query, grad, attended, inverse, weights, windows):
    out_shape = [jax.ShapeDtypeStruct((2 * TILE, HD), jnp.bfloat16)]
    out_shape += [jax.ShapeDtypeStruct(window.shape, jnp.bfloat16) for window in windows]
    return pl.pallas_call(
        backward_kernel,
        out_shape=tuple(out_shape),
        in_specs=vmem_specs(5 + len(windows)),
        out_specs=tuple(vmem_specs(len(out_shape))),
        compiler_params=pltpu.CompilerParams(vmem_limit_bytes=48 * 1024 * 1024),
        cost_estimate=pl.CostEstimate(flops=6_000_000_000, bytes_accessed=10_000_000, transcendentals=0),
        name="attend_back",
    )(query, grad, attended, inverse, weights, *windows)


def project(group, attended, weight, teacher):
    width = TILE
    return pl.pallas_call(
        project_kernel,
        grid_spec=pltpu.PrefetchScalarGridSpec(
            num_scalar_prefetch=1,
            grid=(8,),
            in_specs=[
                pl.BlockSpec((2, 8, TILE, HD), lambda j, g: (0, 0, 0, 0)),
                pl.BlockSpec((8, TILE, width), lambda j, g: (0, 0, j)),
                pl.BlockSpec((1, TILE, TILE), lambda j, g: (j, 0, 0)),
            ],
            out_specs=[
                pl.BlockSpec((TILE, TILE), lambda j, g: (0, 0)),
                pl.BlockSpec((TILE, TILE), lambda j, g: (0, 0)),
            ],
            scratch_shapes=[pltpu.VMEM((TILE, TILE), jnp.float32)],
        ),
        out_shape=[jax.ShapeDtypeStruct((TILE, TILE), jnp.bfloat16)] * 2,
        compiler_params=pltpu.CompilerParams(vmem_limit_bytes=48 * 1024 * 1024),
        cost_estimate=pl.CostEstimate(flops=2_500_000_000, bytes_accessed=10_000_000, transcendentals=0),
        name="project",
    )(group, attended, weight, teacher)


def column_shift(value, step, lines):
    pairs = [
        (line * TW + col, line * TW + col + step)
        for line in lines
        for col in range(TW)
        if 0 <= col + step < TW
    ]
    return lax.ppermute(value, ("xr", "zr", "zc"), pairs)


ALL_LINES = (0, 1, 2, 3)
MIDDLE_LINES = (1, 2)


def slot_tiles(xr, zr, zc):
    third = 2 - xr
    middle = xr != zr
    tiles = []
    for step in (0, -1, 1):
        col = zc + step
        inside = (col >= 0) & (col < TW)
        for f in range(2):
            for pair_row in range(2):
                tiles.append(jnp.where(inside, f * 32 + (2 * xr + pair_row) * TW + col, -2))
    for step in (0, -1, 1):
        col = zc + step
        inside = (col >= 0) & (col < TW) & middle
        for f in range(2):
            tiles.append(jnp.where(inside, f * 32 + third * TW + col, -2))
    return jnp.stack(tiles)


def body(queries, keys, values, out_weight, teacher, block_lists):
    xf, xr, zr, zc = (lax.axis_index(axis) for axis in TILE_AXES)
    group = lax.axis_index(HEAD_AXES)
    swap = [(0, 1), (1, 0)]

    listed = jnp.any(block_lists[:, 0, :, None] == slot_tiles(xr, zr, zc)[None, None, :], axis=1)
    listed = jnp.pad(listed.astype(jnp.bfloat16), ((0, 0), (0, HD - SLOTS)))
    query_heads = queries.reshape(TILE, 2, HD).transpose(1, 0, 2)
    with_mask = jnp.concatenate(
        [query_heads, jnp.broadcast_to(listed[:, None, :], (2, 16, HD))], axis=1
    )
    mine = lax.dynamic_index_in_dim(with_mask, xf, 0, keepdims=False)
    others = lax.dynamic_index_in_dim(with_mask, 1 - xf, 0, keepdims=False)

    heads = jnp.stack([keys.reshape(TILE, 2, HD), values.reshape(TILE, 2, HD)])
    heads = heads.transpose(2, 0, 1, 3)
    send = jnp.broadcast_to(heads[:, None], (2, 2, 2, TILE, HD)).reshape(4, 2, TILE, HD)
    rows = lax.all_to_all(send, ("xf", "zr"), 0, 0, tiled=True)

    got = lax.ppermute(others, "xf", swap)
    pair = jnp.where(xf == 0, jnp.stack([mine, got]), jnp.stack([got, mine]))
    query = pair[:, :TILE].reshape(2 * TILE, HD)
    allowed = pair[:, TILE, :SLOTS].T
    bias = jnp.where(jnp.repeat(allowed, TILE, axis=1) > 0.5, 0.0, MASKED).astype(jnp.float32)

    packed = jnp.concatenate([out_weight, teacher.reshape(32, 2048)])
    packed = lax.all_gather(packed, HEAD_AXES)

    third_send = jnp.where(zr == 0, rows.reshape(2, 2, 2, TILE, HD)[:, 1], rows.reshape(2, 2, 2, TILE, HD)[:, 0])
    third = lax.ppermute(third_send, ("xr", "zr"), [(0, 2), (3, 1)])
    rows_left = column_shift(rows, 1, ALL_LINES)
    rows_right = column_shift(rows, -1, ALL_LINES)
    third_left = column_shift(third, 1, MIDDLE_LINES)
    third_right = column_shift(third, -1, MIDDLE_LINES)
    windows = (rows, rows_left, rows_right, third, third_left, third_right)

    weights, attended, inverse = forward(query, bias, windows)

    spread = jnp.broadcast_to(attended.reshape(2, 1, TILE, HD), (2, 8, TILE, HD)).reshape(16, TILE, HD)
    gathered = lax.all_to_all(spread, ("xf",) + HEAD_AXES, 0, 0, tiled=True).reshape(2, 8, TILE, HD)
    teacher_all = packed[:, TILE:, :].reshape(8, TILE, TILE)
    student, grad_own = project(group.astype(jnp.int32)[None], gathered, packed, teacher_all)

    grad_heads = grad_own.reshape(TILE, 2, HD).transpose(1, 0, 2)
    grad_mine = lax.dynamic_index_in_dim(grad_heads, xf, 0, keepdims=False)
    grad_got = lax.ppermute(lax.dynamic_index_in_dim(grad_heads, 1 - xf, 0, keepdims=False), "xf", swap)
    grad = jnp.where(
        xf == 0, jnp.concatenate([grad_mine, grad_got]), jnp.concatenate([grad_got, grad_mine])
    )

    grad_query, part, part_left, part_right, far, far_left, far_right = backward(
        query, grad, attended, inverse, weights, windows
    )

    def sum_of(*terms):
        total = terms[0].astype(jnp.float32)
        for term in terms[1:]:
            total = total + term.astype(jnp.float32)
        return total

    far_from_right = column_shift(far_left, -1, MIDDLE_LINES)
    far_from_left = column_shift(far_right, 1, MIDDLE_LINES)
    part_from_right = column_shift(part_left, -1, ALL_LINES)
    part_from_left = column_shift(part_right, 1, ALL_LINES)
    far_sum = sum_of(far, far_from_right, far_from_left).astype(jnp.bfloat16)
    third_back = lax.ppermute(far_sum, ("xr", "zr"), [(2, 0), (1, 3)])
    row_of_third = jnp.arange(2) == 1 - zr
    third_back = jnp.where(row_of_third[None, :, None, None, None], third_back[:, None], 0)
    part_sum = sum_of(part, part_from_right, part_from_left, third_back.reshape(4, 2, TILE, HD))
    back = lax.all_to_all(part_sum.astype(jnp.bfloat16), ("xf", "zr"), 0, 0, tiled=True)
    back = back.reshape(2, 2, 2, TILE, HD).astype(jnp.float32)
    back = (back[:, 0] + back[:, 1]).astype(jnp.bfloat16)
    back = back.transpose(1, 2, 0, 3).reshape(2, TILE, 2 * HD)

    own_q = lax.dynamic_slice_in_dim(grad_query, xf * TILE, TILE)
    got_q = lax.ppermute(lax.dynamic_slice_in_dim(grad_query, (1 - xf) * TILE, TILE), "xf", swap)
    grad_queries = jnp.where(
        xf == 0, jnp.concatenate([own_q, got_q], axis=1), jnp.concatenate([got_q, own_q], axis=1)
    )
    return student, grad_queries, back[0], back[1]


def solution(mesh):
    split = Mesh(mesh.devices.reshape(2, 2, 2, 8, 4, 2), TILE_AXES + HEAD_AXES)
    both = P(TILE_AXES, HEAD_AXES)
    return jax.shard_map(
        body,
        mesh=split,
        in_specs=(both, both, both, P(HEAD_AXES, None), both, P(HEAD_AXES, TILE_AXES, None)),
        out_specs=(both, both, both, both),
        check_vma=False,
    )
```

time: 1010 us -> 218 us (0.22)
  the two profiles are of different devices: /device:TPU:5 before, /device:TPU:63 now
where the time goes in v1:
time: 218 us; the launch traced here: 217 us
  waiting for transfers between devices  93.3 us (43%)
  starting transfers between devices  64.9 us (30%)
  Pallas kernels  26 us (12%)
  between operations  14.5 us (7%)
  local copies, waits for them, and re-layouts  13.3 us (6%)
  other arithmetic  5.22 us (2%)
    all_to_all x1, waiting for transfers between devices, body(): rows = lax.all_to_all(send, ('xf', 'zr'), 0, 0, tiled=True)  32.3 us
    all_to_all x1, waiting for transfers between devices, body(): lax.all_to_all(part_sum.astype(jnp.bfloat16), ('xf', 'zr'), 0, 0, tiled=T...  26.2 us
    ppermute x8, starting transfers between devices, column_shift(): return lax.ppermute(value, ('xr', 'zr', 'zc'), pairs)  21.2 us
    all_to_all x1, starting transfers between devices, body(): rows = lax.all_to_all(send, ('xf', 'zr'), 0, 0, tiled=True)  16.6 us
    ppermute x8, waiting for transfers between devices, column_shift(): return lax.ppermute(value, ('xr', 'zr', 'zc'), pairs)  15 us
    all_to_all x1, waiting for transfers between devices, body(): lax.all_to_all(spread, ('xf',) + HEAD_AXES, 0, 0, tiled=True)  10 us
    pallas_call x1, Pallas kernels, project(): pl.pallas_call(project_kernel, grid_spec=pltpu.PrefetchScalarGridSpec(num...  9.9 us
    pallas_call x1, Pallas kernels, backward(): pl.pallas_call(backward_kernel, out_shape=tuple(out_shape), in_specs=vmem...  9.35 us
  transfers between devices with their start and end apart: 17, of which 11 were waited for; matrix products, arithmetic and copies ran while one was open for 4% of the time, Pallas kernels for 3%

profile of v1, /device:TPU:63, one launch (start us, length us, event | category | flops | bytes accessed | tf_op | source)
XLA Modules:
  0.0 217.2 jit_solution(18118644036800356825)
XLA Ops:
  8.3 2.4 %pad_maximum_fusion = bf16[288,2048]{1,0:T(8,128)(2,1)} fusion(bf16[32,2048]{1,0:T(8,128)(2,1)S(1)} %reshape.83, bf16[256,2048]{1,0:T(8,128)(2,1)} %param.9), kind=kLoop, calls=%fused_computation | loop fusion | flops 2359296 | bytes 2359296 | tf_op jit(solution)/shard_map/concatenate | solution.py:237
  12.0 16.6 %all-to-all-start = ((bf16[4,2,256,128]{3,2,1,0:T(8,128)(2,1)}), bf16[4,2,256,128]{3,2,1,0:T(8,128)(2,1)S(1)}, u32[]{:S(2)}, u32[]{:S(2)}) async-start(bf16[4,2,256,128]{3,2,1,0:T(8,128)(2,1)} %bitcast.27), calls=%async_computation | async-start | bytes 1048576 | tf_op jit(solution)/shard_map/all_to_all | solution.py:229
  29.0 32.3 %all-to-all-done.refs_0_ = bf16[4,2,256,128]{3,2,1,0:T(8,128)(2,1)S(1)} async-done(((bf16[4,2,256,128]{3,2,1,0:T(8,128)(2,1)}), bf16[4,2,256,128]{3,2,1,0:T(8,128)(2,1)S(1)}, u32[]{:S(2)}, u32[]{:S(2)}) %all-to-all-start) | async-done | bytes 524320 | tf_op jit(solution)/shard_map/all_to_all | solution.py:229
  61.4 1.3 collective-permute-start.3
  62.7 1.9 collective-permute-start.1
  64.6 3.4 %collective-permute-start.2 = (bf16[4,2,256,128]{3,2,1,0:T(8,128)(2,1)S(1)}, bf16[4,2,256,128]{3,2,1,0:T(8,128)(2,1)S(1)}, u32[]{:S(2)}, u32[]{:S(2)}) collective-permute-start(bf16[4,2,256,128]{3,2,1,0:T(8,128)(2,1)S(1)} %all-to-all-done.refs_0_), channel_id=1, source_target_pairs={{8,0},{16,8},{24,16},{32,24},{40,32},{48,40},{56,48},{72,64},{80,7... | collective-permute-start | bytes 1572872 | tf_op jit(solution)/shard_map/ppermute | solution.py:187
  68.3 2.2 %collective-permute-start = (bf16[272,128]{1,0:T(8,128)(2,1)S(1)}, bf16[272,128]{1,0:T(8,128)(2,1)S(1)}, u32[]{:S(2)}, u32[]{:S(2)}) collective-permute-start(bf16[272,128]{1,0:T(8,128)(2,1)S(1)} %bitcast.88), channel_id=1, source_target_pairs={{0,256},{256,0},{1,257},{257,1},{2,258},{258,2},{3,259},{259,3},{4... | collective-permute-start | bytes 208904 | tf_op jit(solution)/shard_map/ppermute | solution.py:231
  70.5 1.9 collective-permute-start.4
  72.5 3.4 %collective-permute-start.5 = (bf16[2,2,256,128]{3,2,1,0:T(8,128)(2,1)S(1)}, bf16[2,2,256,128]{3,2,1,0:T(8,128)(2,1)S(1)}, u32[]{:S(2)}, u32[]{:S(2)}) collective-permute-start(bf16[2,2,256,128]{3,2,1,0:T(8,128)(2,1)S(1)} %collective-permute-done.3.refs_3_), channel_id=1, source_target_pairs={{72,64},{80,72},{88,80},{96,88},{104,96},{112,104},{120,112},{136,... | collective-permute-start | bytes 786440 | tf_op jit(solution)/shard_map/ppermute | solution.py:187
  76.5 5.7 %collective-permute-done.4.refs_4_ = bf16[2,2,256,128]{3,2,1,0:T(8,128)(2,1)S(1)} collective-permute-done((bf16[2,2,256,128]{3,2,1,0:T(8,128)(2,1)S(1)}, bf16[2,2,256,128]{3,2,1,0:T(8,128)(2,1)S(1)}, u32[]{:S(2)}, u32[]{:S(2)}) %collective-permute-start.4) | collective-permute-done | bytes 262176 | tf_op jit(solution)/shard_map/ppermute | solution.py:187
  82.2 1.9 collective-permute-done.5.refs_5_
  84.1 6.7 %attend.1 = (bf16[18,256,512]{2,1,0:T(8,128)(2,1)}, bf16[512,128]{1,0:T(8,128)(2,1)S(1)}, f32[8,512]{1,0:T(8,128)S(1)}) custom-call(bf16[512,128]{1,0:T(8,128)(2,1)S(1)} %bitcast.77, f32[18,512]{1,0:T(8,128)S(1)} %bitcast.79, bf16[4,2,256,128]{3,2,1,0:T(8,128)(2,1)S(1)} %all-to-all-done.refs_0_, bf16[4,2,256,128]{3,2,1,0:T(8,128)(2,1)S(1)} %collective-permute-done.1.refs_1_, ...), custom_call_target="tpu_custom_call" | custom-call | flops 3000000000 | bytes 8000000 | tf_op jit(solution)/shard_map/attend/pallas_call | solution.py:125
  92.0 9.1 %all-to-all-start.1 = ((bf16[16,256,128]{2,1,0:T(8,128)(2,1)}), bf16[16,256,128]{2,1,0:T(8,128)(2,1)S(1)}, u32[]{:S(2)}, u32[]{:S(2)}) async-start(bf16[16,256,128]{2,1,0:T(8,128)(2,1)} %bitcast.31), calls=%async_computation.1 | async-start | bytes 2097152 | tf_op jit(solution)/shard_map/all_to_all | solution.py:251
  101.2 2.3 %slice.42 = bf16[8,32,2048]{2,1,0:T(8,128)(2,1)} slice(bf16[8,288,2048]{2,1,0:T(8,128)(2,1)} %bitcast.80), slice={[0:8], [256:288], [0:2048]} | slice | bytes 2097152 | tf_op jit(solution)/shard_map/slice | solution.py:252
  103.5 1.6 reshape.84.teacher_ref
  105.1 10.0 %all-to-all-done.1 = bf16[16,256,128]{2,1,0:T(8,128)(2,1)S(1)} async-done(((bf16[16,256,128]{2,1,0:T(8,128)(2,1)}), bf16[16,256,128]{2,1,0:T(8,128)(2,1)S(1)}, u32[]{:S(2)}, u32[]{:S(2)}) %all-to-all-start.1) | async-done | bytes 1048608 | tf_op jit(solution)/shard_map/all_to_all | solution.py:251
  115.1 9.9 %project.1 = (bf16[256,256]{1,0:T(8,128)(2,1)}, bf16[256,256]{1,0:T(8,128)(2,1)S(1)}) custom-call(s32[1]{0:T(128)} %bitcast.group_ref, bf16[2,8,256,128]{3,2,1,0:T(8,128)(2,1)S(1)} %bitcast.74, bf16[8,288,2048]{2,1,0:T(8,128)(2,1)} %bitcast.81, bf16[8,256,256]{2,1,0:T(8,128)(2,1)S(1)} %reshape.84.teacher_ref), custom_call_target="tpu_custom_call" | custom-call | flops 2500000000 | bytes 10000000 | tf_op jit(solution)/shard_map/project/pallas_call | solution.py:157
  125.4 4.9 %collective-permute-start.6 = (bf16[256,128]{1,0:T(8,128)(2,1)S(1)}, bf16[256,128]{1,0:T(8,128)(2,1)S(1)}, u32[]{:S(2)}, u32[]{:S(2)}) collective-permute-start(bf16[256,128]{1,0:T(8,128)(2,1)S(1)} %bitcast.90), channel_id=1, source_target_pairs={{0,256},{256,0},{1,257},{257,1},{2,258},{258,2},{3,259},{259,3},{4... | collective-permute-start | bytes 196616 | tf_op jit(solution)/shard_map/ppermute | solution.py:257
  130.3 1.9 collective-permute-done.6
  136.2 9.3 %attend_back.1 = (bf16[512,128]{1,0:T(8,128)(2,1)S(1)}, bf16[4,2,256,128]{3,2,1,0:T(8,128)(2,1)S(1)}, bf16[4,2,256,128]{3,2,1,0:T(8,128)(2,1)S(1)}, bf16[4,2,256...) custom-call(bf16[512,128]{1,0:T(8,128)(2,1)S(1)} %bitcast.78, ...), custom_call_target="tpu_custom_call" | custom-call | flops 6000000000 | bytes 10000000 | tf_op jit(solution)/shard_map/attend_back/pallas_call | solution.py:144
  145.5 3.4 %collective-permute-start.10 = (bf16[2,2,256,128]{3,2,1,0:T(8,128)(2,1)S(1)}, bf16[2,2,256,128]{3,2,1,0:T(8,128)(2,1)S(1)}, u32[]{:S(2)}, u32[]{:S(2)}) collective-permute-start(bf16[2,2,256,128]{3,2,1,0:T(8,128)(2,1)S(1)} %get-tuple-element.26), channel_id=1, source_target_pairs={{72,64},{80,72},{88,80},{96,88},{104,96},{112,104},{120,112},{136,... | collective-permute-start | bytes 786440 | tf_op jit(solution)/shard_map/ppermute | solution.py:187
  148.9 1.9 collective-permute-start.11
  150.9 3.4 %collective-permute-start.8 = (bf16[4,2,256,128]{3,2,1,0:T(8,128)(2,1)S(1)}, bf16[4,2,256,128]{3,2,1,0:T(8,128)(2,1)S(1)}, u32[]{:S(2)}, u32[]{:S(2)}) collective-permute-start(bf16[4,2,256,128]{3,2,1,0:T(8,128)(2,1)S(1)} %get-tuple-element.23), channel_id=1, source_target_pairs={{8,0},{16,8},{24,16},{32,24},{40,32},{48,40},{56,48},{72,64},{80,7... | collective-permute-start | bytes 1572872 | tf_op jit(solution)/shard_map/ppermute | solution.py:187
  154.3 1.9 collective-permute-start.9
  157.4 1.3 collective-permute-start.12
  158.9 3.2 %collective-permute-done.12 = bf16[2,2,256,128]{3,2,1,0:T(8,128)(2,1)S(1)} collective-permute-done((bf16[2,2,256,128]{3,2,1,0:T(8,128)(2,1)S(1)}, bf16[2,2,256,128]{3,2,1,0:T(8,128)(2,1)S(1)}, u32[]{:S(2)}, u32[]{:S(2)}) %collective-permute-start.12) | collective-permute-done | bytes 262176 | tf_op jit(solution)/shard_map/ppermute | solution.py:277
  162.0 3.2 %collective-permute-done.8 = bf16[4,2,256,128]{3,2,1,0:T(8,128)(2,1)S(1)} collective-permute-done((bf16[4,2,256,128]{3,2,1,0:T(8,128)(2,1)S(1)}, bf16[4,2,256,128]{3,2,1,0:T(8,128)(2,1)S(1)}, u32[]{:S(2)}, u32[]{:S(2)}) %collective-permute-start.8) | collective-permute-done | bytes 524320 | tf_op jit(solution)/shard_map/ppermute | solution.py:187
  165.2 3.1 %collective-permute-done.9 = bf16[4,2,256,128]{3,2,1,0:T(8,128)(2,1)S(1)} collective-permute-done((bf16[4,2,256,128]{3,2,1,0:T(8,128)(2,1)S(1)}, bf16[4,2,256,128]{3,2,1,0:T(8,128)(2,1)S(1)}, u32[]{:S(2)}, u32[]{:S(2)}) %collective-permute-start.9) | collective-permute-done | bytes 524320 | tf_op jit(solution)/shard_map/ppermute | solution.py:187
  169.4 6.3 %all-to-all-start.2 = ((bf16[4,2,256,128]{3,2,1,0:T(8,128)(2,1)}), bf16[4,2,256,128]{3,2,1,0:T(8,128)(2,1)S(1)}, u32[]{:S(2)}, u32[]{:S(2)}) async-start(bf16[4,2,256,128]{3,2,1,0:T(8,128)(2,1)} %add_convert_fusion), calls=%async_computation.2 | async-start | bytes 1048576 | tf_op jit(solution)/shard_map/all_to_all | solution.py:281
  175.7 2.0 collective-permute-start.7
  177.7 4.5 %collective-permute-done.7 = bf16[256,128]{1,0:T(8,128)(2,1)S(1)} collective-permute-done((bf16[256,128]{1,0:T(8,128)(2,1)S(1)}, bf16[256,128]{1,0:T(8,128)(2,1)S(1)}, u32[]{:S(2)}, u32[]{:S(2)}) %collective-permute-start.7) | collective-permute-done | bytes 65568 | tf_op jit(solution)/shard_map/ppermute | solution.py:287
  182.9 26.2 %all-to-all-done.2 = bf16[4,2,256,128]{3,2,1,0:T(8,128)(2,1)S(1)} async-done(((bf16[4,2,256,128]{3,2,1,0:T(8,128)(2,1)}), bf16[4,2,256,128]{3,2,1,0:T(8,128)(2,1)S(1)}, u32[]{:S(2)}, u32[]{:S(2)}) %all-to-all-start.2) | async-done | bytes 524320 | tf_op jit(solution)/shard_map/all_to_all | solution.py:281
  (75 shorter events, 13.5 us)
Async XLA Ops:
  7.2 3.5 %copy-start.8 = (bf16[256,256]{1,0:T(8,128)(2,1)S(1)}, bf16[256,256]{1,0:T(8,128)(2,1)}, u32[]{:S(2)}) copy-start(bf16[256,256]{1,0:T(8,128)(2,1)} %param.7) | copy-start | bytes 393220
  7.2 3.5 %copy-start.9 = (bf16[256,256]{1,0:T(8,128)(2,1)S(1)}, bf16[256,256]{1,0:T(8,128)(2,1)}, u32[]{:S(2)}) copy-start(bf16[256,256]{1,0:T(8,128)(2,1)} %param.8) | copy-start | bytes 393220
  7.2 94.0 %all-gather.3.cloned.1.call-start = ((), (), s32[]{:S(2)}) async-start(), calls=%async_computation.3 | async-start | bytes 10616832 | tf_op jit(solution)/shard_map/all_gather | solution.py:238
  10.6 18.0 %copy-start.10 = (bf16[256,256]{1,0:T(8,128)(2,1)S(1)}, bf16[256,256]{1,0:T(8,128)(2,1)}, u32[]{:S(2)}) copy-start(bf16[256,256]{1,0:T(8,128)(2,1)} %param.6) | copy-start | bytes 393220
  10.6 18.2 %copy-start.11 = (s32[2,1,27]{2,1,0:T(1,128)S(1)}, s32[2,1,27]{2,1,0:T(1,128)}, u32[]{:S(2)}) copy-start(s32[2,1,27]{2,1,0:T(1,128)} %param.11) | copy-start | bytes 652
  12.0 49.3 %all-to-all-start = ((bf16[4,2,256,128]{3,2,1,0:T(8,128)(2,1)}), bf16[4,2,256,128]{3,2,1,0:T(8,128)(2,1)S(1)}, u32[]{:S(2)}, u32[]{:S(2)}) async-start(bf16[4,2,256,128]{3,2,1,0:T(8,128)(2,1)} %bitcast.27), calls=%async_computation | async-start | bytes 1048576 | tf_op jit(solution)/shard_map/all_to_all | solution.py:229
  61.4 9.1 %collective-permute-start.3 = (bf16[2,2,256,128]{3,2,1,0:T(8,128)(2,1)S(1)}, bf16[2,2,256,128]{3,2,1,0:T(8,128)(2,1)S(1)}, u32[]{:S(2)}, u32[]{:S(2)}) collective-permute-start(bf16[2,2,256,128]{3,2,1,0:T(8,128)(2,1)S(1)} %fusion.3), channel_id=1, source_target_pairs={{0,128},{192,64},{1,129},{193,65},{2,130},{194,66},{3,131},{195,67... | collective-permute-start | bytes 786440 | tf_op jit(solution)/shard_map/ppermute | solution.py:241
  62.7 21.4 %collective-permute-start.1 = (bf16[4,2,256,128]{3,2,1,0:T(8,128)(2,1)S(1)}, bf16[4,2,256,128]{3,2,1,0:T(8,128)(2,1)S(1)}, u32[]{:S(2)}, u32[]{:S(2)}) collective-permute-start(bf16[4,2,256,128]{3,2,1,0:T(8,128)(2,1)S(1)} %all-to-all-done.refs_0_), channel_id=1, source_target_pairs={{0,8},{8,16},{16,24},{24,32},{32,40},{40,48},{48,56},{64,72},{72,8... | collective-permute-start | bytes 1572872 | tf_op jit(solution)/shard_map/ppermute | solution.py:187
  64.6 19.5 %collective-permute-start.2 = (bf16[4,2,256,128]{3,2,1,0:T(8,128)(2,1)S(1)}, bf16[4,2,256,128]{3,2,1,0:T(8,128)(2,1)S(1)}, u32[]{:S(2)}, u32[]{:S(2)}) collective-permute-start(bf16[4,2,256,128]{3,2,1,0:T(8,128)(2,1)S(1)} %all-to-all-done.refs_0_), channel_id=1, source_target_pairs={{8,0},{16,8},{24,16},{32,24},{40,32},{48,40},{56,48},{72,64},{80,7... | collective-permute-start | bytes 1572872 | tf_op jit(solution)/shard_map/ppermute | solution.py:187
  68.3 7.5 %collective-permute-start = (bf16[272,128]{1,0:T(8,128)(2,1)S(1)}, bf16[272,128]{1,0:T(8,128)(2,1)S(1)}, u32[]{:S(2)}, u32[]{:S(2)}) collective-permute-start(bf16[272,128]{1,0:T(8,128)(2,1)S(1)} %bitcast.88), channel_id=1, source_target_pairs={{0,256},{256,0},{1,257},{257,1},{2,258},{258,2},{3,259},{259,3},{4... | collective-permute-start | bytes 208904 | tf_op jit(solution)/shard_map/ppermute | solution.py:231
  70.5 20.3 %copy-start.2 = (bf16[2,2,256,128]{3,2,1,0:T(8,128)(2,1)}, bf16[2,2,256,128]{3,2,1,0:T(8,128)(2,1)S(1)}, u32[]{:S(2)}) copy-start(bf16[2,2,256,128]{3,2,1,0:T(8,128)(2,1)S(1)} %collective-permute-done.3.refs_3_) | copy-start | bytes 786436
  70.5 11.6 %collective-permute-start.4 = (bf16[2,2,256,128]{3,2,1,0:T(8,128)(2,1)S(1)}, bf16[2,2,256,128]{3,2,1,0:T(8,128)(2,1)S(1)}, u32[]{:S(2)}, u32[]{:S(2)}) collective-permute-start(bf16[2,2,256,128]{3,2,1,0:T(8,128)(2,1)S(1)} %collective-permute-done.3.refs_3_), channel_id=1, source_target_pairs={{64,72},{72,80},{80,88},{88,96},{96,104},{104,112},{112,120},{128,... | collective-permute-start | bytes 786440 | tf_op jit(solution)/shard_map/ppermute | solution.py:187
  72.5 11.6 %collective-permute-start.5 = (bf16[2,2,256,128]{3,2,1,0:T(8,128)(2,1)S(1)}, bf16[2,2,256,128]{3,2,1,0:T(8,128)(2,1)S(1)}, u32[]{:S(2)}, u32[]{:S(2)}) collective-permute-start(bf16[2,2,256,128]{3,2,1,0:T(8,128)(2,1)S(1)} %collective-permute-done.3.refs_3_), channel_id=1, source_target_pairs={{72,64},{80,72},{88,80},{96,88},{104,96},{112,104},{120,112},{136,... | collective-permute-start | bytes 786440 | tf_op jit(solution)/shard_map/ppermute | solution.py:187
  82.2 8.7 %copy-start.4 = (bf16[2,2,256,128]{3,2,1,0:T(8,128)(2,1)}, bf16[2,2,256,128]{3,2,1,0:T(8,128)(2,1)S(1)}, u32[]{:S(2)}) copy-start(bf16[2,2,256,128]{3,2,1,0:T(8,128)(2,1)S(1)} %collective-permute-done.4.refs_4_) | copy-start | bytes 786436
  84.1 6.7 %copy-start.6 = (bf16[2,2,256,128]{3,2,1,0:T(8,128)(2,1)}, bf16[2,2,256,128]{3,2,1,0:T(8,128)(2,1)S(1)}, u32[]{:S(2)}) copy-start(bf16[2,2,256,128]{3,2,1,0:T(8,128)(2,1)S(1)} %collective-permute-done.5.refs_5_) | copy-start | bytes 786436
  84.1 6.7 %copy-start = (bf16[4,2,256,128]{3,2,1,0:T(8,128)(2,1)}, bf16[4,2,256,128]{3,2,1,0:T(8,128)(2,1)S(1)}, u32[]{:S(2)}) copy-start(bf16[4,2,256,128]{3,2,1,0:T(8,128)(2,1)S(1)} %collective-permute-done.2.refs_2_) | copy-start | bytes 1572868
  92.0 23.1 %all-to-all-start.1 = ((bf16[16,256,128]{2,1,0:T(8,128)(2,1)}), bf16[16,256,128]{2,1,0:T(8,128)(2,1)S(1)}, u32[]{:S(2)}, u32[]{:S(2)}) async-start(bf16[16,256,128]{2,1,0:T(8,128)(2,1)} %bitcast.31), calls=%async_computation.1 | async-start | bytes 2097152 | tf_op jit(solution)/shard_map/all_to_all | solution.py:251
  125.4 6.9 %collective-permute-start.6 = (bf16[256,128]{1,0:T(8,128)(2,1)S(1)}, bf16[256,128]{1,0:T(8,128)(2,1)S(1)}, u32[]{:S(2)}, u32[]{:S(2)}) collective-permute-start(bf16[256,128]{1,0:T(8,128)(2,1)S(1)} %bitcast.90), channel_id=1, source_target_pairs={{0,256},{256,0},{1,257},{257,1},{2,258},{258,2},{3,259},{259,3},{4... | collective-permute-start | bytes 196616 | tf_op jit(solution)/shard_map/ppermute | solution.py:257
  132.3 1.0 copy-start.1
  133.3 0.9 copy-start.3
  134.3 0.9 copy-start.5
  135.2 0.9 copy-start.7
  145.5 10.6 %collective-permute-start.10 = (bf16[2,2,256,128]{3,2,1,0:T(8,128)(2,1)S(1)}, bf16[2,2,256,128]{3,2,1,0:T(8,128)(2,1)S(1)}, u32[]{:S(2)}, u32[]{:S(2)}) collective-permute-start(bf16[2,2,256,128]{3,2,1,0:T(8,128)(2,1)S(1)} %get-tuple-element.26), channel_id=1, source_target_pairs={{72,64},{80,72},{88,80},{96,88},{104,96},{112,104},{120,112},{136,... | collective-permute-start | bytes 786440 | tf_op jit(solution)/shard_map/ppermute | solution.py:187
  148.9 8.4 %collective-permute-start.11 = (bf16[2,2,256,128]{3,2,1,0:T(8,128)(2,1)S(1)}, bf16[2,2,256,128]{3,2,1,0:T(8,128)(2,1)S(1)}, u32[]{:S(2)}, u32[]{:S(2)}) collective-permute-start(bf16[2,2,256,128]{3,2,1,0:T(8,128)(2,1)S(1)} %get-tuple-element.27), channel_id=1, source_target_pairs={{64,72},{72,80},{80,88},{88,96},{96,104},{104,112},{112,120},{128,... | collective-permute-start | bytes 786440 | tf_op jit(solution)/shard_map/ppermute | solution.py:187
  150.9 14.3 %collective-permute-start.8 = (bf16[4,2,256,128]{3,2,1,0:T(8,128)(2,1)S(1)}, bf16[4,2,256,128]{3,2,1,0:T(8,128)(2,1)S(1)}, u32[]{:S(2)}, u32[]{:S(2)}) collective-permute-start(bf16[4,2,256,128]{3,2,1,0:T(8,128)(2,1)S(1)} %get-tuple-element.23), channel_id=1, source_target_pairs={{8,0},{16,8},{24,16},{32,24},{40,32},{48,40},{56,48},{72,64},{80,7... | collective-permute-start | bytes 1572872 | tf_op jit(solution)/shard_map/ppermute | solution.py:187
  154.3 14.1 %collective-permute-start.9 = (bf16[4,2,256,128]{3,2,1,0:T(8,128)(2,1)S(1)}, bf16[4,2,256,128]{3,2,1,0:T(8,128)(2,1)S(1)}, u32[]{:S(2)}, u32[]{:S(2)}) collective-permute-start(bf16[4,2,256,128]{3,2,1,0:T(8,128)(2,1)S(1)} %get-tuple-element.24), channel_id=1, source_target_pairs={{0,8},{8,16},{16,24},{24,32},{32,40},{40,48},{48,56},{64,72},{72,8... | collective-permute-start | bytes 1572872 | tf_op jit(solution)/shard_map/ppermute | solution.py:187
  157.4 4.6 %collective-permute-start.12 = (bf16[2,2,256,128]{3,2,1,0:T(8,128)(2,1)S(1)}, bf16[2,2,256,128]{3,2,1,0:T(8,128)(2,1)S(1)}, u32[]{:S(2)}, u32[]{:S(2)}) collective-permute-start(bf16[2,2,256,128]{3,2,1,0:T(8,128)(2,1)S(1)} %add_convert_fusion.1), channel_id=1, source_target_pairs={{128,0},{64,192},{129,1},{65,193},{130,2},{66,194},{131,3},{67,195... | collective-permute-start | bytes 786440 | tf_op jit(solution)/shard_map/ppermute | solution.py:277
  169.4 39.7 %all-to-all-start.2 = ((bf16[4,2,256,128]{3,2,1,0:T(8,128)(2,1)}), bf16[4,2,256,128]{3,2,1,0:T(8,128)(2,1)S(1)}, u32[]{:S(2)}, u32[]{:S(2)}) async-start(bf16[4,2,256,128]{3,2,1,0:T(8,128)(2,1)} %add_convert_fusion), calls=%async_computation.2 | async-start | bytes 1048576 | tf_op jit(solution)/shard_map/all_to_all | solution.py:281
  175.7 6.5 %collective-permute-start.7 = (bf16[256,128]{1,0:T(8,128)(2,1)S(1)}, bf16[256,128]{1,0:T(8,128)(2,1)S(1)}, u32[]{:S(2)}, u32[]{:S(2)}) collective-permute-start(bf16[256,128]{1,0:T(8,128)(2,1)S(1)} %get-tuple-element.33), channel_id=1, source_target_pairs={{0,256},{256,0},{1,257},{257,1},{2,258},{258,2},{3,259},{259,3},{4... | collective-permute-start | bytes 196616 | tf_op jit(solution)/shard_map/ppermute | solution.py:287
Sparse Core Ops, SparseCore 0:
  10.8 64.2 all-gather.2

commit v2 on v1

v2 whole, which is shorter than its diff:
```python
import functools

import jax
import jax.numpy as jnp
from jax import lax
from jax.experimental import pallas as pl
from jax.experimental.pallas import tpu as pltpu
from jax.sharding import Mesh, PartitionSpec as P

HD = 128
TW = 8
TILE = 256
SLOTS = 18
MASKED = -1e30
SCORE_SCALE = HD ** (-0.5)
LOG2_E = 1.4426950408889634

TILE_AXES = ("xf", "xr", "zr", "zc")
HEAD_AXES = ("y", "core")


def contract_last(left, right):
    return lax.dot_general(left, right, (((1,), (1,)), ((), ())), preferred_element_type=jnp.float32)


def contract_first(left, right):
    return lax.dot_general(left, right, (((0,), (0,)), ((), ())), preferred_element_type=jnp.float32)


def contract_inner(left, right):
    return lax.dot_general(left, right, (((1,), (0,)), ((), ())), preferred_element_type=jnp.float32)


def slot_refs(refs):
    return [(ref, index) for ref in refs for index in range(ref.shape[0])]


def copy_all(pairs, sems):
    copies = [pltpu.make_async_copy(source, target, sems.at[i]) for i, (source, target) in enumerate(pairs)]
    for copy in copies:
        copy.start()
    return copies


def prepare_kernel(
    place_ref, queries_ref, keys_ref, values_ref, mine_ref, other_ref, q_mine_ref, q_other_ref, in_ref, sems
):
    sources = (keys_ref, values_ref, queries_ref)
    copies = copy_all([(source, in_ref.at[i]) for i, source in enumerate(sources)], sems)
    first = pl.multiple_of(place_ref[0] * HD, HD)
    mine, other = pl.ds(first, HD), pl.ds(pl.multiple_of(HD - first, HD), HD)
    for index in range(2):
        copies[index].wait()
        mine_ref[index] = in_ref[index, :, mine]
        other_ref[index] = in_ref[index, :, other]
    copies[2].wait()
    q_mine_ref[...] = in_ref[2, :, mine]
    q_other_ref[...] = in_ref[2, :, other]


def prepare(place, queries, keys, values):
    out_shape = [shape(2, TILE, HD)] * 2 + [shape(TILE, HD)] * 2
    return pl.pallas_call(
        prepare_kernel,
        out_shape=tuple(out_shape),
        in_specs=place_spec() + [pl.BlockSpec(memory_space=pltpu.HBM)] * 3,
        out_specs=tuple(vmem_specs(len(out_shape))),
        scratch_shapes=[pltpu.VMEM((3, TILE, TILE), jnp.bfloat16), pltpu.SemaphoreType.DMA((3,))],
        compiler_params=pltpu.CompilerParams(vmem_limit_bytes=8 * 1024 * 1024),
        cost_estimate=pl.CostEstimate(flops=1_000_000, bytes_accessed=2_000_000, transcendentals=0),
        name="prepare",
    )(place, queries, keys, values)


def pair_kernel(mine_ref, frame_ref, pair_ref):
    pair_ref[0] = mine_ref[...]
    for part in range(2):
        pair_ref[1, part] = frame_ref[part * TILE : (part + 1) * TILE, :]


def forward_kernel(allowed_ref, q_mine_ref, frame_ref, *refs):
    windows, kept_refs, refs = refs[:9], refs[9:12], refs[12:]
    attended_refs, (inverse_ref, window_ref, scores_ref, weights_ref, sems, in_sems) = refs[:2], refs[2:]
    pairs, start = [], 0
    for window in windows:
        pairs.append((window, window_ref.at[pl.ds(start, window.shape[0])]))
        start += window.shape[0]
    arriving = dict(zip(range(0, SLOTS, 2), copy_all(pairs, in_sems)))
    copies = []

    def bias_of(f, s):
        return jnp.where(allowed_ref[f, s] > 0, 0.0, MASKED)

    for f in range(2):
        cols = slice(f * TILE, (f + 1) * TILE)
        query = q_mine_ref[...] if f == 0 else frame_ref[2 * TILE : 3 * TILE, :]
        highest = jnp.full((8, TILE), -jnp.inf, jnp.float32)
        for s in range(SLOTS):
            if f == 0 and s in arriving:
                arriving[s].wait()
            products = contract_last(window_ref[s, 0], query)
            scores_ref[s] = products
            top = jnp.max(products.reshape(TILE // 8, 8, TILE), axis=0) * (SCORE_SCALE * LOG2_E)
            highest = jnp.maximum(highest, top + bias_of(f, s))
        highest = jnp.max(highest, axis=0, keepdims=True)
        total = jnp.zeros((8, TILE), jnp.float32)
        summed = jnp.zeros((HD, TILE), jnp.float32)
        for s in range(SLOTS):
            weights = jnp.exp2(scores_ref[s] * (SCORE_SCALE * LOG2_E) + (bias_of(f, s) - highest))
            total = total + jnp.sum(weights.reshape(TILE // 8, 8, TILE), axis=0)
            weights = weights.astype(jnp.bfloat16)
            weights_ref[f, s] = weights
            summed = summed + contract_first(window_ref[s, 1], weights)
        inverse = 1.0 / jnp.sum(total, axis=0, keepdims=True)
        inverse_ref[:, cols] = jnp.broadcast_to(inverse, (8, TILE))
        attended_refs[f][...] = (summed * inverse).T.astype(jnp.bfloat16)
        start = 0
        for part, kept_ref in enumerate(kept_refs):
            count = kept_ref.shape[1]
            copy = pltpu.make_async_copy(
                weights_ref.at[f, pl.ds(start, count)], kept_ref.at[f], sems.at[f, part]
            )
            copy.start()
            copies.append(copy)
            start += count
    for copy in copies:
        copy.wait()


def backward_kernel(
    count, last, q_mine_ref, frame_ref, grad_mine_ref, grad_got_ref, own_ref, other_ref, inverse_ref, *refs
):
    before_ref, kept_ref, *refs = refs
    windows, (grad_q_ref, *parts) = refs[:count], refs[count : 2 * count + 1]
    weights_ref, sems, *window_refs = refs[2 * count + 1 :]
    copies = copy_all([(kept_ref, weights_ref), *zip(windows, window_refs)], sems)
    queries = [q_mine_ref[...], frame_ref[2 * TILE : 3 * TILE, :]]
    grads = [grad_mine_ref[...], grad_got_ref[...]]
    deltas = []
    for f in range(2):
        product = grads[f].astype(jnp.float32) * (own_ref, other_ref)[f][...].astype(jnp.float32)
        deltas.append(jnp.sum(product.T, axis=0, keepdims=True))
    grad_q = [before_ref[f] for f in range(2)]
    for copy in copies:
        copy.wait()
    for s, ((ref, index), (out, out_index)) in enumerate(zip(slot_refs(window_refs), slot_refs(parts))):
        key, value = ref[index, 0], ref[index, 1]
        grad_key = jnp.zeros((TILE, HD), jnp.float32)
        grad_value = jnp.zeros((TILE, HD), jnp.float32)
        for f in range(2):
            cols = slice(f * TILE, (f + 1) * TILE)
            dprob = contract_last(value, grads[f])
            probs = weights_ref[f, s].astype(jnp.float32) * inverse_ref[0:1, cols]
            dscore = (probs * (dprob - deltas[f])).astype(jnp.bfloat16)
            grad_key = grad_key + contract_inner(dscore, queries[f])
            grad_value = grad_value + contract_inner(probs.astype(jnp.bfloat16), grads[f])
            grad_q[f] = grad_q[f] + contract_first(key, dscore)
        out[out_index, 0] = (grad_key * SCORE_SCALE).astype(jnp.bfloat16)
        out[out_index, 1] = grad_value.astype(jnp.bfloat16)
    for f in range(2):
        if last:
            grad_q_ref[f] = (grad_q[f] * SCORE_SCALE).T.astype(jnp.bfloat16)
        else:
            grad_q_ref[f] = grad_q[f]


def project_kernel(*refs):
    attended_refs, pack_refs, out_ref = refs[:4], refs[4:8], refs[8]
    for block in range(8):
        cols = slice(block * TILE, (block + 1) * TILE)
        total = jnp.zeros((TILE, TILE), jnp.float32)
        for attended_ref, pack_ref in zip(attended_refs, pack_refs):
            total = total + contract_inner(attended_ref[...], pack_ref[:, cols])
        out_ref[:, cols] = total.astype(jnp.bfloat16)


def residue_kernel(place_ref, mine_ref, other_ref, weight_ref, *refs):
    teacher_refs, (student_ref, mine_grad_ref, other_grad_ref) = refs[:4], refs[4:]
    row, core = place_ref[1], place_ref[2]
    grad = jnp.zeros((TILE, TILE), jnp.float32)
    for side in range(2):
        for back in range(4):
            group = lax.rem(row + 4 - back, 4) * 2 + (core if side == 0 else 1 - core)
            cols = pl.ds(pl.multiple_of(group * TILE, TILE), TILE)
            student = mine_ref[:, cols].astype(jnp.float32) + other_ref[:, cols].astype(jnp.float32)
            student = student.astype(jnp.bfloat16)
            if side == 0 and back == 0:
                student_ref[...] = student
            teacher = teacher_refs[back][:, side * TILE : (side + 1) * TILE]
            residue = (student.astype(jnp.float32) - teacher.astype(jnp.float32)).astype(jnp.bfloat16)
            grad = grad + contract_last(residue, weight_ref[:, cols])
    mine_grad_ref[...] = grad[:, :HD].astype(jnp.bfloat16)
    other_grad_ref[...] = grad[:, HD:].astype(jnp.bfloat16)


def merge_kernel(part_ref, right_ref, left_ref, third_ref, out_ref):
    out_ref[...] = sum_of(part_ref[...], right_ref[...], left_ref[...], third_ref[...]).astype(jnp.bfloat16)


def far_kernel(part_ref, right_ref, left_ref, out_ref):
    out_ref[...] = sum_of(part_ref[...], right_ref[...], left_ref[...]).astype(jnp.bfloat16)


def frame_kernel(part_ref, right_ref, left_ref, row_ref, grad_q_ref, frame_ref):
    total = sum_of(part_ref[1], right_ref[1], left_ref[1], row_ref[1]).astype(jnp.bfloat16)
    frame_ref[0] = total[0]
    frame_ref[1] = total[1]
    frame_ref[2] = grad_q_ref[1]


def join_kernel(place_ref, part_ref, right_ref, left_ref, row_ref, grad_q_ref, frame_ref, *outs):
    first = pl.multiple_of(place_ref[0] * HD, HD)
    mine, other = pl.ds(first, HD), pl.ds(pl.multiple_of(HD - first, HD), HD)
    own = sum_of(part_ref[0], right_ref[0], left_ref[0], row_ref[0]).astype(jnp.bfloat16)
    outs[0][:, mine] = grad_q_ref[0]
    outs[0][:, other] = frame_ref[2]
    for index in range(2):
        outs[1 + index][:, mine] = own[index]
        outs[1 + index][:, other] = frame_ref[index]


def vmem_specs(count):
    return [pl.BlockSpec(memory_space=pltpu.VMEM) for _ in range(count)]


def any_specs(count):
    return [pl.BlockSpec(memory_space=pl.ANY) for _ in range(count)]


def place_spec():
    return [pl.BlockSpec(memory_space=pltpu.SMEM)]


def shape(*dims, dtype=jnp.bfloat16):
    return jax.ShapeDtypeStruct(dims, dtype)


def simple(kernel, name, out_shape, *args, place=None, limit=8):
    head = [] if place is None else [place]
    return pl.pallas_call(
        kernel,
        out_shape=tuple(out_shape),
        in_specs=place_spec() * len(head) + vmem_specs(len(args)),
        out_specs=tuple(vmem_specs(len(out_shape))),
        compiler_params=pltpu.CompilerParams(vmem_limit_bytes=limit * 1024 * 1024),
        cost_estimate=pl.CostEstimate(flops=1_000_000, bytes_accessed=2_000_000, transcendentals=0),
        name=name,
    )(*head, *args)


def forward(allowed, q_mine, frame, windows):
    kept = [shape(2, 6, TILE, TILE) for _ in range(3)]
    return pl.pallas_call(
        forward_kernel,
        out_shape=(*kept, shape(TILE, HD), shape(TILE, HD), shape(8, 2 * TILE, dtype=jnp.float32)),
        in_specs=place_spec() + vmem_specs(2) + any_specs(len(windows)),
        out_specs=tuple(any_specs(3) + vmem_specs(3)),
        scratch_shapes=[
            pltpu.VMEM((SLOTS, 2, TILE, HD), jnp.bfloat16),
            pltpu.VMEM((SLOTS, TILE, TILE), jnp.float32),
            pltpu.VMEM((2, SLOTS, TILE, TILE), jnp.bfloat16),
            pltpu.SemaphoreType.DMA((2, 3)),
            pltpu.SemaphoreType.DMA((9,)),
        ],
        compiler_params=pltpu.CompilerParams(vmem_limit_bytes=18 * 1024 * 1024),
        cost_estimate=pl.CostEstimate(flops=3_000_000_000, bytes_accessed=8_000_000, transcendentals=2_400_000),
        name="attend",
    )(allowed, q_mine, frame, *windows)


def backward(common, before, weights, windows, last=False):
    if last:
        out_shape = [shape(2, TILE, HD)]
    else:
        out_shape = [shape(2, HD, TILE, dtype=jnp.float32)]
    out_shape += [shape(*window.shape) for window in windows]
    blocks = 2 * weights.shape[1]
    return pl.pallas_call(
        functools.partial(backward_kernel, len(windows), last),
        out_shape=tuple(out_shape),
        in_specs=vmem_specs(len(common) + 1) + any_specs(1 + len(windows)),
        out_specs=tuple(vmem_specs(len(out_shape))),
        scratch_shapes=[
            pltpu.VMEM(weights.shape, jnp.bfloat16),
            pltpu.SemaphoreType.DMA((1 + len(windows),)),
            *[pltpu.VMEM(window.shape, jnp.bfloat16) for window in windows],
        ],
        compiler_params=pltpu.CompilerParams(vmem_limit_bytes=10 * 1024 * 1024),
        cost_estimate=pl.CostEstimate(
            flops=blocks * 8 * TILE * TILE * HD, bytes_accessed=blocks * 300_000, transcendentals=0
        ),
        name="attend_back",
    )(*common, before, weights, *windows)


def project(attended, packs):
    return pl.pallas_call(
        project_kernel,
        in_specs=vmem_specs(8),
        out_specs=pl.BlockSpec(memory_space=pltpu.VMEM),
        out_shape=jax.ShapeDtypeStruct((TILE, 8 * TILE), jnp.bfloat16),
        compiler_params=pltpu.CompilerParams(vmem_limit_bytes=10 * 1024 * 1024),
        cost_estimate=pl.CostEstimate(flops=1_100_000_000, bytes_accessed=6_000_000, transcendentals=0),
        name="project",
    )(*attended, *packs)


def residue_grad(place, mine, other, packs):
    out_shape = [shape(TILE, TILE), shape(TILE, HD), shape(TILE, HD)]
    return pl.pallas_call(
        residue_kernel,
        grid=(1,),
        out_shape=tuple(out_shape),
        in_specs=place_spec()
        + vmem_specs(2)
        + [pl.BlockSpec((TILE, 8 * TILE), lambda i: (0, 0))]
        + [pl.BlockSpec((TILE, 2 * TILE), lambda i: (0, 4)) for _ in packs],
        out_specs=tuple(vmem_specs(len(out_shape))),
        compiler_params=pltpu.CompilerParams(vmem_limit_bytes=10 * 1024 * 1024),
        cost_estimate=pl.CostEstimate(flops=300_000_000, bytes_accessed=5_000_000, transcendentals=0),
        name="residue",
    )(place, mine, other, packs[0], *packs)


def column_shift(value, step, lines):
    pairs = [
        (line * TW + col, line * TW + col + step)
        for line in lines
        for col in range(TW)
        if 0 <= col + step < TW
    ]
    return lax.ppermute(value, ("xr", "zr", "zc"), pairs)


ALL_LINES = (0, 1, 2, 3)
MIDDLE_LINES = (1, 2)
SWAP = [(0, 1), (1, 0)]


def slot_tiles(frame, xr, zr, zc):
    tiles = []
    for row, live in ((2 * xr + zr, True), (2 * xr + 1 - zr, True), (2 - xr, xr != zr)):
        for step in (0, -1, 1):
            col = zc + step
            inside = (col >= 0) & (col < TW) & live
            for f in (frame, 1 - frame):
                tiles.append(jnp.where(inside, f * 32 + row * TW + col, -2))
    return jnp.stack(tiles)


def beside(value, lines):
    return column_shift(value, 1, lines), column_shift(value, -1, lines)


def from_rows(value):
    return [lax.ppermute(value, "y", [(i, (i + step) % 4) for i in range(4)]) for step in (1, 2, 3)]


def sum_of(*terms):
    total = terms[0].astype(jnp.float32)
    for term in terms[1:]:
        total = total + term.astype(jnp.float32)
    return total


def body(queries, keys, values, out_weight, teacher, block_lists):
    xf, xr, zr, zc = (lax.axis_index(axis) for axis in TILE_AXES)
    place = jnp.stack([xf, lax.axis_index("y"), lax.axis_index("core")]).astype(jnp.int32)

    kv_mine, kv_other, q_mine, q_other = prepare(place, queries, keys, values)

    def listed(head, frame):
        lists = lax.dynamic_index_in_dim(block_lists[:, 0], head, 0, keepdims=False)
        return jnp.any(lists[:, None] == slot_tiles(frame, xr, zr, zc)[None, :], axis=0)

    mask_row = jnp.pad(listed(1 - xf, 1 - xf).astype(jnp.bfloat16), (0, HD - SLOTS))
    message = jnp.concatenate(
        [kv_other.reshape(2 * TILE, HD), q_other, jnp.broadcast_to(mask_row[None], (16, HD))]
    )
    xf_got = lax.ppermute(message, "xf", SWAP)
    allowed = jnp.stack([listed(xf, xf), xf_got[3 * TILE, :SLOTS] > 0.5]).astype(jnp.int32)

    pair = simple(pair_kernel, "pair", [shape(2, 2, TILE, HD)], kv_mine, xf_got)[0]
    row = lax.ppermute(pair, "zr", SWAP)
    third = lax.ppermute(row, ("xr", "zr"), [(0, 2), (3, 1)])
    own_windows = (pair, *beside(pair, ALL_LINES))
    row_windows = (row, *beside(row, ALL_LINES))
    third_windows = (third, *beside(third, MIDDLE_LINES))

    weight_heads = out_weight.reshape(2, HD, 8 * TILE)
    first_head = jnp.where(xf == 0, weight_heads[0], weight_heads[1])
    second_head = jnp.where(xf == 0, weight_heads[1], weight_heads[0])
    far_teacher = lax.ppermute(teacher, "core", SWAP)
    first_head, _ = lax.optimization_barrier((first_head, xf_got))
    pack = jnp.concatenate([jnp.concatenate([first_head, second_head]), teacher, far_teacher], axis=1)
    ring = [(i, (i + 1) % 4) for i in range(4)]
    up = lax.ppermute(pack, "y", ring)
    down = lax.ppermute(pack, "y", [(i, (i + 3) % 4) for i in range(4)])
    across = lax.ppermute(up, "y", ring)
    packs = [pack, up, across, down]

    *weights, own, other, inverse = forward(
        allowed, q_mine, xf_got, own_windows + row_windows + third_windows
    )

    got = lax.ppermute(other, "xf", SWAP)
    attended = jnp.concatenate([own, got], axis=1)
    partial_mine = project([attended] + from_rows(attended), packs)
    partial_other = lax.ppermute(partial_mine, "core", SWAP)
    student, grad_mine, grad_other = residue_grad(place, partial_mine, partial_other, packs)
    grad_got = lax.ppermute(grad_other, "xf", SWAP)

    own_weights, row_weights, third_weights = weights
    common = (q_mine, xf_got, grad_mine, grad_got, own, other, inverse)
    before = jnp.zeros((2, HD, TILE), jnp.float32)
    before, far, far_left, far_right = backward(common, before, third_weights, third_windows)
    before, part, part_left, part_right = backward(common, before, row_weights, row_windows)
    grad_query, near, near_left, near_right = backward(common, before, own_weights, own_windows, last=True)

    def returned(left, right, lines):
        return column_shift(left, -1, lines), column_shift(right, 1, lines)

    far_sum = simple(
        far_kernel, "far_sum", [shape(2, 2, TILE, HD)], far, *returned(far_left, far_right, MIDDLE_LINES)
    )[0]
    third_back = lax.ppermute(far_sum, ("xr", "zr"), [(2, 0), (1, 3)])
    row_sum = simple(
        merge_kernel,
        "merge",
        [shape(2, 2, TILE, HD)],
        part,
        *returned(part_left, part_right, ALL_LINES),
        third_back,
    )[0]
    row_back = lax.ppermute(row_sum, "zr", SWAP)
    from_right, from_left = returned(near_left, near_right, ALL_LINES)
    sums = (near, from_right, from_left, row_back, grad_query)
    frame_sum = simple(frame_kernel, "frame_sum", [shape(3, TILE, HD)], *sums)[0]
    xf_back = lax.ppermute(frame_sum, "xf", SWAP)
    grad_queries, grad_keys, grad_values = simple(
        join_kernel, "join", [shape(TILE, TILE)] * 3, *sums, xf_back, place=place
    )
    return student, grad_queries, grad_keys, grad_values


def solution(mesh):
    split = Mesh(mesh.devices.reshape(2, 2, 2, 8, 4, 2), TILE_AXES + HEAD_AXES)
    both = P(TILE_AXES, HEAD_AXES)
    return jax.shard_map(
        body,
        mesh=split,
        in_specs=(both, both, both, P(HEAD_AXES, None), both, P(HEAD_AXES, TILE_AXES, None)),
        out_specs=(both, both, both, both),
        check_vma=False,
    )
```

time: 218 us -> 209 us (0.959)
  the two profiles are of different devices: /device:TPU:63 before, /device:TPU:58 now
where the time goes in v2:
time: 209 us; the launch traced here: 208 us
  starting transfers between devices  96.2 us (46%)
  waiting for transfers between devices  75.7 us (36%)
  Pallas kernels  29.6 us (14%)
  local copies, waits for them, and re-layouts  3.64 us (2%)
    ppermute x12, starting transfers between devices, column_shift(): return lax.ppermute(value, ('xr', 'zr', 'zc'), pairs)  37.9 us
    ppermute x12, waiting for transfers between devices, column_shift(): return lax.ppermute(value, ('xr', 'zr', 'zc'), pairs)  21.3 us
    ppermute x1, waiting for transfers between devices, body(): row_back = lax.ppermute(row_sum, 'zr', SWAP)  20.3 us
    ppermute x1, starting transfers between devices, body(): row = lax.ppermute(pair, 'zr', SWAP)  14.8 us
    pallas_call x3, Pallas kernels, backward(): pl.pallas_call(functools.partial(backward_kernel, len(windows), last), ou...  13.3 us
    ppermute x3, starting transfers between devices, from_rows(): lax.ppermute(value, 'y', [(i, (i + step) % 4) for i in range(4)])  9.56 us
    pallas_call x1, Pallas kernels, forward(): pl.pallas_call(forward_kernel, out_shape=(*kept, shape(TILE, HD), shape(T...  8.16 us
    ppermute x1, waiting for transfers between devices, body(): up = lax.ppermute(pack, 'y', ring)  7.89 us
  transfers between devices with their start and end apart: 28, of which 16 were waited for; matrix products, arithmetic and copies ran while one was open for 1% of the time, Pallas kernels for 8%

profile of v2, /device:TPU:58, one launch (start us, length us, event | category | flops | bytes accessed | tf_op | source)
XLA Modules:
  0.0 208.1 jit_solution(1199023036638914853)
XLA Ops:
  5.7 4.0 %collective-permute-start = (bf16[784,128]{1,0:T(8,128)(2,1)S(1)}, bf16[784,128]{1,0:T(8,128)(2,1)S(1)}, u32[]{:S(2)}, u32[]{:S(2)}) collective-permute-start(bf16[784,128]{1,0:T(8,128)(2,1)S(1)} %pad_maximum_fusion.1), channel_id=1, source_target_pairs={{0,256},{256,0},{1,257},{257,1},{2,258},{258,2},{3,259},{259,3},{4... | collective-permute-start | bytes 602120 | tf_op jit(solution)/shard_map/ppermute | solution.py:380
  12.9 2.9 %collective-permute-done.frame_ref = bf16[784,128]{1,0:T(8,128)(2,1)S(1)} collective-permute-done((bf16[784,128]{1,0:T(8,128)(2,1)S(1)}, bf16[784,128]{1,0:T(8,128)(2,1)S(1)}, u32[]{:S(2)}, u32[]{:S(2)}) %collective-permute-start) | collective-permute-done | bytes 200736 | tf_op jit(solution)/shard_map/ppermute | solution.py:380
  18.1 14.8 %collective-permute-start.3 = (bf16[2,2,256,128]{3,2,1,0:T(8,128)(2,1)S(1)}, bf16[2,2,256,128]{3,2,1,0:T(8,128)(2,1)}, u32[]{:S(2)}, u32[]{:S(2)}) collective-permute-start(bf16[2,2,256,128]{3,2,1,0:T(8,128)(2,1)S(1)} %pair.1.refs_0_.refs_2_), channel_id=1, source_target_pairs={{0,64},{64,0},{1,65},{65,1},{2,66},{66,2},{3,67},{67,3},{4,68},{68... | collective-permute-start | bytes 786440 | tf_op jit(solution)/shard_map/ppermute | solution.py:384
  32.9 2.9 %collective-permute-start.1 = (bf16[2,2,256,128]{3,2,1,0:T(8,128)(2,1)S(1)}, bf16[2,2,256,128]{3,2,1,0:T(8,128)(2,1)S(1)}, u32[]{:S(2)}, u32[]{:S(2)}) collective-permute-start(bf16[2,2,256,128]{3,2,1,0:T(8,128)(2,1)S(1)} %pair.1.refs_0_.refs_2_), channel_id=1, source_target_pairs={{0,8},{8,16},{16,24},{24,32},{32,40},{40,48},{48,56},{64,72},{72,8... | collective-permute-start | bytes 786440 | tf_op jit(solution)/shard_map/ppermute | solution.py:332
  35.9 3.7 %collective-permute-start.16 = (bf16[256,2560]{1,0:T(8,128)(2,1)S(1)}, bf16[256,2560]{1,0:T(8,128)(2,1)}, u32[]{:S(2)}, u32[]{:S(2)}) collective-permute-start(bf16[256,2560]{1,0:T(8,128)(2,1)S(1)} %pad_maximum_fusion.refs_4_.weight_ref.refs_0_), channel_id=1, source_target_pairs={{0,6},{2,0},{4,2},{6,4},{1,7},{3,1},{5,3},{7,5},{8,14},{10,8},{12,... | collective-permute-start | bytes 3932168 | tf_op jit(solution)/shard_map/ppermute | solution.py:398
  39.6 7.9 %collective-permute-done.14.refs_5_.refs_1_ = bf16[256,2560]{1,0:T(8,128)(2,1)S(1)} collective-permute-done((bf16[256,2560]{1,0:T(8,128)(2,1)S(1)}, bf16[256,2560]{1,0:T(8,128)(2,1)S(1)}, u32[]{:S(2)}, u32[]{:S(2)}) %collective-permute-start.14) | collective-permute-done | bytes 1310752 | tf_op jit(solution)/shard_map/ppermute | solution.py:397
  47.5 3.4 %collective-permute-start.15 = (bf16[256,2560]{1,0:T(8,128)(2,1)S(1)}, bf16[256,2560]{1,0:T(8,128)(2,1)}, u32[]{:S(2)}, u32[]{:S(2)}) collective-permute-start(bf16[256,2560]{1,0:T(8,128)(2,1)S(1)} %collective-permute-done.14.refs_5_.refs_1_), channel_id=1, source_target_pairs={{0,2},{2,4},{4,6},{6,0},{1,3},{3,5},{5,7},{7,1},{8,10},{10,12},{12... | collective-permute-start | bytes 3932168 | tf_op jit(solution)/shard_map/ppermute | solution.py:399
  56.7 2.8 %collective-permute-done.1.refs_1_.refs_3_ = bf16[2,2,256,128]{3,2,1,0:T(8,128)(2,1)S(1)} collective-permute-done((bf16[2,2,256,128]{3,2,1,0:T(8,128)(2,1)S(1)}, bf16[2,2,256,128]{3,2,1,0:T(8,128)(2,1)S(1)}, u32[]{:S(2)}, u32[]{:S(2)}) %collective-permute-start.1) | collective-permute-done | bytes 262176 | tf_op jit(solution)/shard_map/ppermute | solution.py:332
  59.5 3.4 %collective-permute-start.4 = (bf16[2,2,256,128]{3,2,1,0:T(8,128)(2,1)}, bf16[2,2,256,128]{3,2,1,0:T(8,128)(2,1)}, u32[]{:S(2)}, u32[]{:S(2)}) collective-permute-start(bf16[2,2,256,128]{3,2,1,0:T(8,128)(2,1)} %collective-permute-done.3.refs_3_.refs_2_), channel_id=1, source_target_pairs={{0,8},{8,16},{16,24},{24,32},{32,40},{40,48},{48,56},{64,72},{72,8... | collective-permute-start | bytes 786440 | tf_op jit(solution)/shard_map/ppermute | solution.py:332
  63.2 3.1 %collective-permute-start.5 = (bf16[2,2,256,128]{3,2,1,0:T(8,128)(2,1)}, bf16[2,2,256,128]{3,2,1,0:T(8,128)(2,1)S(1)}, u32[]{:S(2)}, u32[]{:S(2)}) collective-permute-start(bf16[2,2,256,128]{3,2,1,0:T(8,128)(2,1)} %collective-permute-done.3.refs_3_.refs_2_), channel_id=1, source_target_pairs={{8,0},{16,8},{24,16},{32,24},{40,32},{48,40},{56,48},{72,64},{80,7... | collective-permute-start | bytes 786440 | tf_op jit(solution)/shard_map/ppermute | solution.py:332
  69.1 3.1 %collective-permute-start.8 = (bf16[2,2,256,128]{3,2,1,0:T(8,128)(2,1)}, bf16[2,2,256,128]{3,2,1,0:T(8,128)(2,1)S(1)}, u32[]{:S(2)}, u32[]{:S(2)}) collective-permute-start(bf16[2,2,256,128]{3,2,1,0:T(8,128)(2,1)} %collective-permute-done.6.refs_6_.refs_2_), channel_id=1, source_target_pairs={{72,64},{80,72},{88,80},{96,88},{104,96},{112,104},{120,112},{136,... | collective-permute-start | bytes 786440 | tf_op jit(solution)/shard_map/ppermute | solution.py:332
  75.0 4.5 %collective-permute-done.8.refs_8_.refs_4_ = bf16[2,2,256,128]{3,2,1,0:T(8,128)(2,1)S(1)} collective-permute-done((bf16[2,2,256,128]{3,2,1,0:T(8,128)(2,1)}, bf16[2,2,256,128]{3,2,1,0:T(8,128)(2,1)S(1)}, u32[]{:S(2)}, u32[]{:S(2)}) %collective-permute-start.8) | collective-permute-done | bytes 262176 | tf_op jit(solution)/shard_map/ppermute | solution.py:332
  79.5 8.2 %attend.1 = (bf16[2,6,256,256]{3,2,1,0:T(8,128)(2,1)S(1)}, bf16[2,6,256,256]{3,2,1,0:T(8,128)(2,1)S(1)}, bf16[2,6,256,256]{3,2,1,0:T(8,128)(2,1)S(1)}, bf16[256,...) custom-call(s32[2,18]{1,0:T(2,128)S(1)} %add_convert_fusion.allowed_ref, ...), custom_call_target="tpu_custom_call" | custom-call | flops 3000000000 | bytes 8000000 | tf_op jit(solution)/shard_map/attend/pallas_call | solution.py:253
  87.7 4.0 %collective-permute-start.9 = (bf16[256,128]{1,0:T(8,128)(2,1)S(1)}, bf16[256,128]{1,0:T(8,128)(2,1)S(1)}, u32[]{:S(2)}, u32[]{:S(2)}) collective-permute-start(bf16[256,128]{1,0:T(8,128)(2,1)S(1)} %get-tuple-element.38.other_ref), channel_id=1, source_target_pairs={{0,256},{256,0},{1,257},{257,1},{2,258},{258,2},{3,259},{259,3},{4... | collective-permute-start | bytes 196616 | tf_op jit(solution)/shard_map/ppermute | solution.py:406
  91.7 3.6 %collective-permute-done.9 = bf16[256,128]{1,0:T(8,128)(2,1)S(1)} collective-permute-done((bf16[256,128]{1,0:T(8,128)(2,1)S(1)}, bf16[256,128]{1,0:T(8,128)(2,1)S(1)}, u32[]{:S(2)}, u32[]{:S(2)}) %collective-permute-start.9) | collective-permute-done | bytes 65568 | tf_op jit(solution)/shard_map/ppermute | solution.py:406
  95.3 3.4 %collective-permute-start.10 = (bf16[256,256]{1,0:T(8,128)(2,1)S(1)}, bf16[256,256]{1,0:T(8,128)(2,1)S(1)}, u32[]{:S(2)}, u32[]{:S(2)}) collective-permute-start(bf16[256,256]{1,0:T(8,128)(2,1)S(1)} %constant_dynamic-update-slice_fusion.refs_0_), channel_id=1, source_target_pairs={{0,2},{2,4},{4,6},{6,0},{1,3},{3,5},{5,7},{7,1},{8,10},{10,12},{12... | collective-permute-start | bytes 393224 | tf_op jit(solution)/shard_map/ppermute | solution.py:356
  98.8 4.1 %collective-permute-start.11 = (bf16[256,256]{1,0:T(8,128)(2,1)S(1)}, bf16[256,256]{1,0:T(8,128)(2,1)S(1)}, u32[]{:S(2)}, u32[]{:S(2)}) collective-permute-start(bf16[256,256]{1,0:T(8,128)(2,1)S(1)} %constant_dynamic-update-slice_fusion.refs_0_), channel_id=1, source_target_pairs={{0,4},{2,6},{4,0},{6,2},{1,5},{3,7},{5,1},{7,3},{8,12},{10,14},{12... | collective-permute-start | bytes 393224 | tf_op jit(solution)/shard_map/ppermute | solution.py:356
  104.9 3.0 %collective-permute-done.11.refs_2_ = bf16[256,256]{1,0:T(8,128)(2,1)S(1)} collective-permute-done((bf16[256,256]{1,0:T(8,128)(2,1)S(1)}, bf16[256,256]{1,0:T(8,128)(2,1)S(1)}, u32[]{:S(2)}, u32[]{:S(2)}) %collective-permute-start.11) | collective-permute-done | bytes 131104 | tf_op jit(solution)/shard_map/ppermute | solution.py:356
  107.9 3.0 %collective-permute-done.12.refs_3_ = bf16[256,256]{1,0:T(8,128)(2,1)S(1)} collective-permute-done((bf16[256,256]{1,0:T(8,128)(2,1)S(1)}, bf16[256,256]{1,0:T(8,128)(2,1)S(1)}, u32[]{:S(2)}, u32[]{:S(2)}) %collective-permute-start.12) | collective-permute-done | bytes 131104 | tf_op jit(solution)/shard_map/ppermute | solution.py:356
  111.0 3.0 %project.1.mine_ref = bf16[256,2048]{1,0:T(8,128)(2,1)S(1)} custom-call(bf16[256,256]{1,0:T(8,128)(2,1)S(1)} %constant_dynamic-update-slice_fusion.refs_0_, bf16[256,256]{1,0:T(8,128)(2,1)S(1)} %collective-permute-done.10.refs_1_, bf16[256,256]{1,0:T(8,128)(2,1)S(1)} %collective-permute-done.11.refs_2_, ...), custom_call_target="tpu_custom_call" | custom-call | flops 1100000000 | bytes 6000000 | tf_op jit(solution)/shard_map/project/pallas_call | solution.py:297
  120.8 4.2 %collective-permute-start.18 = (bf16[256,128]{1,0:T(8,128)(2,1)S(1)}, bf16[256,128]{1,0:T(8,128)(2,1)S(1)}, u32[]{:S(2)}, u32[]{:S(2)}) collective-permute-start(bf16[256,128]{1,0:T(8,128)(2,1)S(1)} %get-tuple-element.42), channel_id=1, source_target_pairs={{0,256},{256,0},{1,257},{257,1},{2,258},{258,2},{3,259},{259,3},{4... | collective-permute-start | bytes 196616 | tf_op jit(solution)/shard_map/ppermute | solution.py:411
  125.0 3.4 %collective-permute-done.18.grad_got_ref = bf16[256,128]{1,0:T(8,128)(2,1)S(1)} collective-permute-done((bf16[256,128]{1,0:T(8,128)(2,1)S(1)}, bf16[256,128]{1,0:T(8,128)(2,1)S(1)}, u32[]{:S(2)}, u32[]{:S(2)}) %collective-permute-start.18) | collective-permute-done | bytes 65568 | tf_op jit(solution)/shard_map/ppermute | solution.py:411
  128.5 4.4 %attend_back.3 = (f32[2,128,256]{2,1,0:T(8,128)S(1)}, bf16[2,2,256,128]{3,2,1,0:T(8,128)(2,1)S(1)}, bf16[2,2,256,128]{3,2,1,0:T(8,128)(2,1)S(1)}, bf16[2,2,256,128]{3,2,1,0:T(8,128)(2,1)S(1)}) custom-call(bf16[256,128]{1,0:T(8,128)(2,1)S(1)} %get-tuple-element.35.q_mine_ref, bf16[784,128]{1,0:T(8,128)(2,1)S(1)} %collective-permute-done.frame_ref, ...), custom_call_target="tpu_custom_call" | custom-call | flops 805306368 | bytes 3600000 | tf_op jit(solution)/shard_map/attend_back/pallas_call | solution.py:278
  134.8 4.9 %collective-permute-start.24 = (bf16[2,2,256,128]{3,2,1,0:T(8,128)(2,1)S(1)}, bf16[2,2,256,128]{3,2,1,0:T(8,128)(2,1)S(1)}, u32[]{:S(2)}, u32[]{:S(2)}) collective-permute-start(bf16[2,2,256,128]{3,2,1,0:T(8,128)(2,1)S(1)} %get-tuple-element.57), channel_id=1, source_target_pairs={{64,72},{72,80},{80,88},{88,96},{96,104},{104,112},{112,120},{128,... | collective-permute-start | bytes 786440 | tf_op jit(solution)/shard_map/ppermute | solution.py:332
  139.7 4.4 %attend_back.4 = (f32[2,128,256]{2,1,0:T(8,128)S(1)}, bf16[2,2,256,128]{3,2,1,0:T(8,128)(2,1)S(1)}, bf16[2,2,256,128]{3,2,1,0:T(8,128)(2,1)S(1)}, bf16[2,2,256,128]{3,2,1,0:T(8,128)(2,1)S(1)}) custom-call(bf16[256,128]{1,0:T(8,128)(2,1)S(1)} %get-tuple-element.35.q_mine_ref, bf16[784,128]{1,0:T(8,128)(2,1)S(1)} %collective-permute-done.frame_ref, ...), custom_call_target="tpu_custom_call" | custom-call | flops 805306368 | bytes 3600000 | tf_op jit(solution)/shard_map/attend_back/pallas_call | solution.py:278
  146.0 4.8 %collective-permute-start.22 = (bf16[2,2,256,128]{3,2,1,0:T(8,128)(2,1)S(1)}, bf16[2,2,256,128]{3,2,1,0:T(8,128)(2,1)S(1)}, u32[]{:S(2)}, u32[]{:S(2)}) collective-permute-start(bf16[2,2,256,128]{3,2,1,0:T(8,128)(2,1)S(1)} %get-tuple-element.54), channel_id=1, source_target_pairs={{0,8},{8,16},{16,24},{24,32},{32,40},{40,48},{48,56},{64,72},{72,8... | collective-permute-start | bytes 786440 | tf_op jit(solution)/shard_map/ppermute | solution.py:332
  152.3 4.5 %attend_back.5 = (bf16[2,256,128]{2,1,0:T(8,128)(2,1)S(1)}, bf16[2,2,256,128]{3,2,1,0:T(8,128)(2,1)S(1)}, bf16[2,2,256,128]{3,2,1,0:T(8,128)(2,1)S(1)}, bf16[2,2,256,128]{3,2,1,0:T(8,128)(2,1)S(1)}) custom-call(bf16[256,128]{1,0:T(8,128)(2,1)S(1)} %get-tuple-element.35.q_mine_ref, bf16[784,128]{1,0:T(8,128)(2,1)S(1)} %collective-permute-done.frame_ref, ...), custom_call_target="tpu_custom_call" | custom-call | flops 805306368 | bytes 3600000 | tf_op jit(solution)/shard_map/attend_back/pallas_call | solution.py:278
  158.8 5.1 %collective-permute-start.20 = (bf16[2,2,256,128]{3,2,1,0:T(8,128)(2,1)S(1)}, bf16[2,2,256,128]{3,2,1,0:T(8,128)(2,1)S(1)}, u32[]{:S(2)}, u32[]{:S(2)}) collective-permute-start(bf16[2,2,256,128]{3,2,1,0:T(8,128)(2,1)S(1)} %get-tuple-element.51), channel_id=1, source_target_pairs={{0,8},{8,16},{16,24},{24,32},{32,40},{40,48},{48,56},{64,72},{72,8... | collective-permute-start | bytes 786440 | tf_op jit(solution)/shard_map/ppermute | solution.py:332
  167.6 9.8 %collective-permute-done.20.left_ref = bf16[2,2,256,128]{3,2,1,0:T(8,128)(2,1)S(1)} collective-permute-done((bf16[2,2,256,128]{3,2,1,0:T(8,128)(2,1)S(1)}, bf16[2,2,256,128]{3,2,1,0:T(8,128)(2,1)S(1)}, u32[]{:S(2)}, u32[]{:S(2)}) %collective-permute-start.20) | collective-permute-done | bytes 262176 | tf_op jit(solution)/shard_map/ppermute | solution.py:332
  177.3 20.3 %collective-permute-done.26.row_ref = bf16[2,2,256,128]{3,2,1,0:T(8,128)(2,1)S(1)} collective-permute-done((bf16[2,2,256,128]{3,2,1,0:T(8,128)(2,1)S(1)}, bf16[2,2,256,128]{3,2,1,0:T(8,128)(2,1)S(1)}, u32[]{:S(2)}, u32[]{:S(2)}) %collective-permute-start.26) | collective-permute-done | bytes 262176 | tf_op jit(solution)/shard_map/ppermute | solution.py:435
  197.7 4.0 %collective-permute-start.27 = (bf16[3,256,128]{2,1,0:T(8,128)(2,1)S(1)}, bf16[3,256,128]{2,1,0:T(8,128)(2,1)S(1)}, u32[]{:S(2)}, u32[]{:S(2)}) collective-permute-start(bf16[3,256,128]{2,1,0:T(8,128)(2,1)S(1)} %frame_sum.1), channel_id=1, source_target_pairs={{0,256},{256,0},{1,257},{257,1},{2,258},{258,2},{3,259},{259,3},{4... | collective-permute-start | bytes 589832 | tf_op jit(solution)/shard_map/ppermute | solution.py:439
  201.7 5.0 %collective-permute-done.27.frame_ref = bf16[3,256,128]{2,1,0:T(8,128)(2,1)S(1)} collective-permute-done((bf16[3,256,128]{2,1,0:T(8,128)(2,1)S(1)}, bf16[3,256,128]{2,1,0:T(8,128)(2,1)S(1)}, u32[]{:S(2)}, u32[]{:S(2)}) %collective-permute-start.27) | collective-permute-done | bytes 196640 | tf_op jit(solution)/shard_map/ppermute | solution.py:439
  (60 shorter events, 43.1 us)
Async XLA Ops:
  0.6 15.2 %copy-start.3 = (bf16[256,256]{1,0:T(8,128)(2,1)S(1)}, bf16[256,256]{1,0:T(8,128)(2,1)}, u32[]{:S(2)}) copy-start(bf16[256,256]{1,0:T(8,128)(2,1)} %param.10) | copy-start | bytes 393220
  1.8 0.9 copy-start
  2.7 0.9 copy-start.1
  3.6 0.9 copy-start.2
  5.7 10.1 %collective-permute-start = (bf16[784,128]{1,0:T(8,128)(2,1)S(1)}, bf16[784,128]{1,0:T(8,128)(2,1)S(1)}, u32[]{:S(2)}, u32[]{:S(2)}) collective-permute-start(bf16[784,128]{1,0:T(8,128)(2,1)S(1)} %pad_maximum_fusion.1), channel_id=1, source_target_pairs={{0,256},{256,0},{1,257},{257,1},{2,258},{258,2},{3,259},{259,3},{4... | collective-permute-start | bytes 602120 | tf_op jit(solution)/shard_map/ppermute | solution.py:380
  9.7 6.1 %collective-permute-start.13 = (bf16[256,256]{1,0:T(8,128)(2,1)}, bf16[256,256]{1,0:T(8,128)(2,1)S(1)}, u32[]{:S(2)}, u32[]{:S(2)}) collective-permute-start(bf16[256,256]{1,0:T(8,128)(2,1)} %param.10), channel_id=1, source_target_pairs={{0,1},{1,0},{2,3},{3,2},{4,5},{5,4},{6,7},{7,6},{8,9},{9,8},{10,11... | collective-permute-start | bytes 393224 | tf_op jit(solution)/shard_map/ppermute | solution.py:393
  15.9 31.5 %collective-permute-start.14 = (bf16[256,2560]{1,0:T(8,128)(2,1)S(1)}, bf16[256,2560]{1,0:T(8,128)(2,1)S(1)}, u32[]{:S(2)}, u32[]{:S(2)}) collective-permute-start(bf16[256,2560]{1,0:T(8,128)(2,1)S(1)} %pad_maximum_fusion.refs_4_.weight_ref.refs_0_), channel_id=1, source_target_pairs={{0,2},{2,4},{4,6},{6,0},{1,3},{3,5},{5,7},{7,1},{8,10},{10,12},{12... | collective-permute-start | bytes 3932168 | tf_op jit(solution)/shard_map/ppermute | solution.py:397
  18.1 37.4 %collective-permute-start.3 = (bf16[2,2,256,128]{3,2,1,0:T(8,128)(2,1)S(1)}, bf16[2,2,256,128]{3,2,1,0:T(8,128)(2,1)}, u32[]{:S(2)}, u32[]{:S(2)}) collective-permute-start(bf16[2,2,256,128]{3,2,1,0:T(8,128)(2,1)S(1)} %pair.1.refs_0_.refs_2_), channel_id=1, source_target_pairs={{0,64},{64,0},{1,65},{65,1},{2,66},{66,2},{3,67},{67,3},{4,68},{68... | collective-permute-start | bytes 786440 | tf_op jit(solution)/shard_map/ppermute | solution.py:384
  32.9 26.6 %collective-permute-start.1 = (bf16[2,2,256,128]{3,2,1,0:T(8,128)(2,1)S(1)}, bf16[2,2,256,128]{3,2,1,0:T(8,128)(2,1)S(1)}, u32[]{:S(2)}, u32[]{:S(2)}) collective-permute-start(bf16[2,2,256,128]{3,2,1,0:T(8,128)(2,1)S(1)} %pair.1.refs_0_.refs_2_), channel_id=1, source_target_pairs={{0,8},{8,16},{16,24},{24,32},{32,40},{40,48},{48,56},{64,72},{72,8... | collective-permute-start | bytes 786440 | tf_op jit(solution)/shard_map/ppermute | solution.py:332
  35.9 75.1 %collective-permute-start.16 = (bf16[256,2560]{1,0:T(8,128)(2,1)S(1)}, bf16[256,2560]{1,0:T(8,128)(2,1)}, u32[]{:S(2)}, u32[]{:S(2)}) collective-permute-start(bf16[256,2560]{1,0:T(8,128)(2,1)S(1)} %pad_maximum_fusion.refs_4_.weight_ref.refs_0_), channel_id=1, source_target_pairs={{0,6},{2,0},{4,2},{6,4},{1,7},{3,1},{5,3},{7,5},{8,14},{10,8},{12,... | collective-permute-start | bytes 3932168 | tf_op jit(solution)/shard_map/ppermute | solution.py:398
  47.5 63.5 %collective-permute-start.15 = (bf16[256,2560]{1,0:T(8,128)(2,1)S(1)}, bf16[256,2560]{1,0:T(8,128)(2,1)}, u32[]{:S(2)}, u32[]{:S(2)}) collective-permute-start(bf16[256,2560]{1,0:T(8,128)(2,1)S(1)} %collective-permute-done.14.refs_5_.refs_1_), channel_id=1, source_target_pairs={{0,2},{2,4},{4,6},{6,0},{1,3},{3,5},{5,7},{7,1},{8,10},{10,12},{12... | collective-permute-start | bytes 3932168 | tf_op jit(solution)/shard_map/ppermute | solution.py:399
  50.9 12.3 %collective-permute-start.2 = (bf16[2,2,256,128]{3,2,1,0:T(8,128)(2,1)S(1)}, bf16[2,2,256,128]{3,2,1,0:T(8,128)(2,1)}, u32[]{:S(2)}, u32[]{:S(2)}) collective-permute-start(bf16[2,2,256,128]{3,2,1,0:T(8,128)(2,1)S(1)} %pair.1.refs_0_.refs_2_), channel_id=1, source_target_pairs={{8,0},{16,8},{24,16},{32,24},{40,32},{48,40},{56,48},{72,64},{80,7... | collective-permute-start | bytes 786440 | tf_op jit(solution)/shard_map/ppermute | solution.py:332
  55.5 10.9 %collective-permute-start.6 = (bf16[2,2,256,128]{3,2,1,0:T(8,128)(2,1)}, bf16[2,2,256,128]{3,2,1,0:T(8,128)(2,1)}, u32[]{:S(2)}, u32[]{:S(2)}) collective-permute-start(bf16[2,2,256,128]{3,2,1,0:T(8,128)(2,1)} %collective-permute-done.3.refs_3_.refs_2_), channel_id=1, source_target_pairs={{0,128},{192,64},{1,129},{193,65},{2,130},{194,66},{3,131},{195,67... | collective-permute-start | bytes 786440 | tf_op jit(solution)/shard_map/ppermute | solution.py:385
  59.5 9.6 %collective-permute-start.4 = (bf16[2,2,256,128]{3,2,1,0:T(8,128)(2,1)}, bf16[2,2,256,128]{3,2,1,0:T(8,128)(2,1)}, u32[]{:S(2)}, u32[]{:S(2)}) collective-permute-start(bf16[2,2,256,128]{3,2,1,0:T(8,128)(2,1)} %collective-permute-done.3.refs_3_.refs_2_), channel_id=1, source_target_pairs={{0,8},{8,16},{16,24},{24,32},{32,40},{40,48},{48,56},{64,72},{72,8... | collective-permute-start | bytes 786440 | tf_op jit(solution)/shard_map/ppermute | solution.py:332
  63.2 9.8 %collective-permute-start.5 = (bf16[2,2,256,128]{3,2,1,0:T(8,128)(2,1)}, bf16[2,2,256,128]{3,2,1,0:T(8,128)(2,1)S(1)}, u32[]{:S(2)}, u32[]{:S(2)}) collective-permute-start(bf16[2,2,256,128]{3,2,1,0:T(8,128)(2,1)} %collective-permute-done.3.refs_3_.refs_2_), channel_id=1, source_target_pairs={{8,0},{16,8},{24,16},{32,24},{40,32},{48,40},{56,48},{72,64},{80,7... | collective-permute-start | bytes 786440 | tf_op jit(solution)/shard_map/ppermute | solution.py:332
  66.4 8.6 %collective-permute-start.7 = (bf16[2,2,256,128]{3,2,1,0:T(8,128)(2,1)}, bf16[2,2,256,128]{3,2,1,0:T(8,128)(2,1)S(1)}, u32[]{:S(2)}, u32[]{:S(2)}) collective-permute-start(bf16[2,2,256,128]{3,2,1,0:T(8,128)(2,1)} %collective-permute-done.6.refs_6_.refs_2_), channel_id=1, source_target_pairs={{64,72},{72,80},{80,88},{88,96},{96,104},{104,112},{112,120},{128,... | collective-permute-start | bytes 786440 | tf_op jit(solution)/shard_map/ppermute | solution.py:332
  69.1 10.4 %collective-permute-start.8 = (bf16[2,2,256,128]{3,2,1,0:T(8,128)(2,1)}, bf16[2,2,256,128]{3,2,1,0:T(8,128)(2,1)S(1)}, u32[]{:S(2)}, u32[]{:S(2)}) collective-permute-start(bf16[2,2,256,128]{3,2,1,0:T(8,128)(2,1)} %collective-permute-done.6.refs_6_.refs_2_), channel_id=1, source_target_pairs={{72,64},{80,72},{88,80},{96,88},{104,96},{112,104},{120,112},{136,... | collective-permute-start | bytes 786440 | tf_op jit(solution)/shard_map/ppermute | solution.py:332
  87.7 7.7 %collective-permute-start.9 = (bf16[256,128]{1,0:T(8,128)(2,1)S(1)}, bf16[256,128]{1,0:T(8,128)(2,1)S(1)}, u32[]{:S(2)}, u32[]{:S(2)}) collective-permute-start(bf16[256,128]{1,0:T(8,128)(2,1)S(1)} %get-tuple-element.38.other_ref), channel_id=1, source_target_pairs={{0,256},{256,0},{1,257},{257,1},{2,258},{258,2},{3,259},{259,3},{4... | collective-permute-start | bytes 196616 | tf_op jit(solution)/shard_map/ppermute | solution.py:406
  95.3 9.6 %collective-permute-start.10 = (bf16[256,256]{1,0:T(8,128)(2,1)S(1)}, bf16[256,256]{1,0:T(8,128)(2,1)S(1)}, u32[]{:S(2)}, u32[]{:S(2)}) collective-permute-start(bf16[256,256]{1,0:T(8,128)(2,1)S(1)} %constant_dynamic-update-slice_fusion.refs_0_), channel_id=1, source_target_pairs={{0,2},{2,4},{4,6},{6,0},{1,3},{3,5},{5,7},{7,1},{8,10},{10,12},{12... | collective-permute-start | bytes 393224 | tf_op jit(solution)/shard_map/ppermute | solution.py:356
  98.8 9.1 %collective-permute-start.11 = (bf16[256,256]{1,0:T(8,128)(2,1)S(1)}, bf16[256,256]{1,0:T(8,128)(2,1)S(1)}, u32[]{:S(2)}, u32[]{:S(2)}) collective-permute-start(bf16[256,256]{1,0:T(8,128)(2,1)S(1)} %constant_dynamic-update-slice_fusion.refs_0_), channel_id=1, source_target_pairs={{0,4},{2,6},{4,0},{6,2},{1,5},{3,7},{5,1},{7,3},{8,12},{10,14},{12... | collective-permute-start | bytes 393224 | tf_op jit(solution)/shard_map/ppermute | solution.py:356
  102.9 8.1 %collective-permute-start.12 = (bf16[256,256]{1,0:T(8,128)(2,1)S(1)}, bf16[256,256]{1,0:T(8,128)(2,1)S(1)}, u32[]{:S(2)}, u32[]{:S(2)}) collective-permute-start(bf16[256,256]{1,0:T(8,128)(2,1)S(1)} %constant_dynamic-update-slice_fusion.refs_0_), channel_id=1, source_target_pairs={{0,6},{2,0},{4,2},{6,4},{1,7},{3,1},{5,3},{7,5},{8,14},{10,8},{12,... | collective-permute-start | bytes 393224 | tf_op jit(solution)/shard_map/ppermute | solution.py:356
  113.9 4.6 %collective-permute-start.17 = (bf16[256,2048]{1,0:T(8,128)(2,1)S(1)}, bf16[256,2048]{1,0:T(8,128)(2,1)S(1)}, u32[]{:S(2)}, u32[]{:S(2)}) collective-permute-start(bf16[256,2048]{1,0:T(8,128)(2,1)S(1)} %project.1.mine_ref), channel_id=1, source_target_pairs={{0,1},{1,0},{2,3},{3,2},{4,5},{5,4},{6,7},{7,6},{8,9},{9,8},{10,11... | collective-permute-start | bytes 3145736 | tf_op jit(solution)/shard_map/ppermute | solution.py:409
  120.8 7.7 %collective-permute-start.18 = (bf16[256,128]{1,0:T(8,128)(2,1)S(1)}, bf16[256,128]{1,0:T(8,128)(2,1)S(1)}, u32[]{:S(2)}, u32[]{:S(2)}) collective-permute-start(bf16[256,128]{1,0:T(8,128)(2,1)S(1)} %get-tuple-element.42), channel_id=1, source_target_pairs={{0,256},{256,0},{1,257},{257,1},{2,258},{258,2},{3,259},{259,3},{4... | collective-permute-start | bytes 196616 | tf_op jit(solution)/shard_map/ppermute | solution.py:411
  132.9 18.0 %collective-permute-start.23 = (bf16[2,2,256,128]{3,2,1,0:T(8,128)(2,1)S(1)}, bf16[2,2,256,128]{3,2,1,0:T(8,128)(2,1)S(1)}, u32[]{:S(2)}, u32[]{:S(2)}) collective-permute-start(bf16[2,2,256,128]{3,2,1,0:T(8,128)(2,1)S(1)} %get-tuple-element.56), channel_id=1, source_target_pairs={{72,64},{80,72},{88,80},{96,88},{104,96},{112,104},{120,112},{136,... | collective-permute-start | bytes 786440 | tf_op jit(solution)/shard_map/ppermute | solution.py:332
  134.8 16.1 %collective-permute-start.24 = (bf16[2,2,256,128]{3,2,1,0:T(8,128)(2,1)S(1)}, bf16[2,2,256,128]{3,2,1,0:T(8,128)(2,1)S(1)}, u32[]{:S(2)}, u32[]{:S(2)}) collective-permute-start(bf16[2,2,256,128]{3,2,1,0:T(8,128)(2,1)S(1)} %get-tuple-element.57), channel_id=1, source_target_pairs={{64,72},{72,80},{80,88},{88,96},{96,104},{104,112},{112,120},{128,... | collective-permute-start | bytes 786440 | tf_op jit(solution)/shard_map/ppermute | solution.py:332
  144.1 19.8 %collective-permute-start.21 = (bf16[2,2,256,128]{3,2,1,0:T(8,128)(2,1)S(1)}, bf16[2,2,256,128]{3,2,1,0:T(8,128)(2,1)S(1)}, u32[]{:S(2)}, u32[]{:S(2)}) collective-permute-start(bf16[2,2,256,128]{3,2,1,0:T(8,128)(2,1)S(1)} %get-tuple-element.53), channel_id=1, source_target_pairs={{8,0},{16,8},{24,16},{32,24},{40,32},{48,40},{56,48},{72,64},{80,7... | collective-permute-start | bytes 786440 | tf_op jit(solution)/shard_map/ppermute | solution.py:332
  146.0 17.9 %collective-permute-start.22 = (bf16[2,2,256,128]{3,2,1,0:T(8,128)(2,1)S(1)}, bf16[2,2,256,128]{3,2,1,0:T(8,128)(2,1)S(1)}, u32[]{:S(2)}, u32[]{:S(2)}) collective-permute-start(bf16[2,2,256,128]{3,2,1,0:T(8,128)(2,1)S(1)} %get-tuple-element.54), channel_id=1, source_target_pairs={{0,8},{8,16},{16,24},{24,32},{32,40},{40,48},{48,56},{64,72},{72,8... | collective-permute-start | bytes 786440 | tf_op jit(solution)/shard_map/ppermute | solution.py:332
  151.0 12.9 %collective-permute-start.25 = (bf16[2,2,256,128]{3,2,1,0:T(8,128)(2,1)S(1)}, bf16[2,2,256,128]{3,2,1,0:T(8,128)(2,1)S(1)}, u32[]{:S(2)}, u32[]{:S(2)}) collective-permute-start(bf16[2,2,256,128]{3,2,1,0:T(8,128)(2,1)S(1)} %far_sum.1), channel_id=1, source_target_pairs={{128,0},{64,192},{129,1},{65,193},{130,2},{66,194},{131,3},{67,195... | collective-permute-start | bytes 786440 | tf_op jit(solution)/shard_map/ppermute | solution.py:426
  156.9 10.7 %collective-permute-start.19 = (bf16[2,2,256,128]{3,2,1,0:T(8,128)(2,1)S(1)}, bf16[2,2,256,128]{3,2,1,0:T(8,128)(2,1)S(1)}, u32[]{:S(2)}, u32[]{:S(2)}) collective-permute-start(bf16[2,2,256,128]{3,2,1,0:T(8,128)(2,1)S(1)} %get-tuple-element.50), channel_id=1, source_target_pairs={{8,0},{16,8},{24,16},{32,24},{40,32},{48,40},{56,48},{72,64},{80,7... | collective-permute-start | bytes 786440 | tf_op jit(solution)/shard_map/ppermute | solution.py:332
  158.8 18.6 %collective-permute-start.20 = (bf16[2,2,256,128]{3,2,1,0:T(8,128)(2,1)S(1)}, bf16[2,2,256,128]{3,2,1,0:T(8,128)(2,1)S(1)}, u32[]{:S(2)}, u32[]{:S(2)}) collective-permute-start(bf16[2,2,256,128]{3,2,1,0:T(8,128)(2,1)S(1)} %get-tuple-element.51), channel_id=1, source_target_pairs={{0,8},{8,16},{16,24},{24,32},{32,40},{40,48},{48,56},{64,72},{72,8... | collective-permute-start | bytes 786440 | tf_op jit(solution)/shard_map/ppermute | solution.py:332
  164.1 33.5 %collective-permute-start.26 = (bf16[2,2,256,128]{3,2,1,0:T(8,128)(2,1)S(1)}, bf16[2,2,256,128]{3,2,1,0:T(8,128)(2,1)S(1)}, u32[]{:S(2)}, u32[]{:S(2)}) collective-permute-start(bf16[2,2,256,128]{3,2,1,0:T(8,128)(2,1)S(1)} %merge.1), channel_id=1, source_target_pairs={{0,64},{64,0},{1,65},{65,1},{2,66},{66,2},{3,67},{67,3},{4,68},{68... | collective-permute-start | bytes 786440 | tf_op jit(solution)/shard_map/ppermute | solution.py:435
  197.7 9.1 %collective-permute-start.27 = (bf16[3,256,128]{2,1,0:T(8,128)(2,1)S(1)}, bf16[3,256,128]{2,1,0:T(8,128)(2,1)S(1)}, u32[]{:S(2)}, u32[]{:S(2)}) collective-permute-start(bf16[3,256,128]{2,1,0:T(8,128)(2,1)S(1)} %frame_sum.1), channel_id=1, source_target_pairs={{0,256},{256,0},{1,257},{257,1},{2,258},{258,2},{3,259},{259,3},{4... | collective-permute-start | bytes 589832 | tf_op jit(solution)/shard_map/ppermute | solution.py:439

commit v3 on v2

--- a/solution.py
+++ b/solution.py
@@ -91,26 +91,32 @@
     def bias_of(f, s):
         return jnp.where(allowed_ref[f, s] > 0, 0.0, MASKED)
 
+    factor = SCORE_SCALE * LOG2_E
+    queries = [q_mine_ref[...], frame_ref[2 * TILE : 3 * TILE, :]]
+    highest = [jnp.full((8, TILE), -jnp.inf, jnp.float32) for _ in range(2)]
+    for first in range(0, SLOTS, 6):
+        for s in range(first, first + 6):
+            if s in arriving:
+                arriving[s].wait()
+        keys = window_ref[first : first + 6, 0].reshape(6 * TILE, HD)
+        for f in range(2):
+            scores_ref[f, first : first + 6] = contract_last(keys, queries[f]).reshape(6, TILE, TILE)
+            for s in range(first, first + 6):
+                top = jnp.max(scores_ref[f, s].reshape(TILE // 8, 8, TILE), axis=0) * factor
+                highest[f] = jnp.maximum(highest[f], top + bias_of(f, s))
     for f in range(2):
         cols = slice(f * TILE, (f + 1) * TILE)
-        query = q_mine_ref[...] if f == 0 else frame_ref[2 * TILE : 3 * TILE, :]
-        highest = jnp.full((8, TILE), -jnp.inf, jnp.float32)
-        for s in range(SLOTS):
-            if f == 0 and s in arriving:
-                arriving[s].wait()
-            products = contract_last(window_ref[s, 0], query)
-            scores_ref[s] = products
-            top = jnp.max(products.reshape(TILE // 8, 8, TILE), axis=0) * (SCORE_SCALE * LOG2_E)
-            highest = jnp.maximum(highest, top + bias_of(f, s))
-        highest = jnp.max(highest, axis=0, keepdims=True)
+        limit = jnp.max(highest[f], axis=0, keepdims=True)
         total = jnp.zeros((8, TILE), jnp.float32)
         summed = jnp.zeros((HD, TILE), jnp.float32)
-        for s in range(SLOTS):
-            weights = jnp.exp2(scores_ref[s] * (SCORE_SCALE * LOG2_E) + (bias_of(f, s) - highest))
-            total = total + jnp.sum(weights.reshape(TILE // 8, 8, TILE), axis=0)
-            weights = weights.astype(jnp.bfloat16)
-            weights_ref[f, s] = weights
-            summed = summed + contract_first(window_ref[s, 1], weights)
+        for first in range(0, SLOTS, 6):
+            for s in range(first, first + 6):
+                weights = jnp.exp2(scores_ref[f, s] * factor + (bias_of(f, s) - limit))
+                weights_ref[f, s] = weights.astype(jnp.bfloat16)
+            value = window_ref[first : first + 6, 1].reshape(6 * TILE, HD)
+            block = weights_ref[f, first : first + 6].reshape(6 * TILE, TILE)
+            summed = summed + contract_first(value, block)
+            total = total + contract_first(jnp.full((6 * TILE, 8), 0.125, jnp.bfloat16), block)
         inverse = 1.0 / jnp.sum(total, axis=0, keepdims=True)
         inverse_ref[:, cols] = jnp.broadcast_to(inverse, (8, TILE))
         attended_refs[f][...] = (summed * inverse).T.astype(jnp.bfloat16)
@@ -140,23 +146,26 @@
     for f in range(2):
         product = grads[f].astype(jnp.float32) * (own_ref, other_ref)[f][...].astype(jnp.float32)
         deltas.append(jnp.sum(product.T, axis=0, keepdims=True))
-    grad_q = [before_ref[f] for f in range(2)]
     for copy in copies:
         copy.wait()
-    for s, ((ref, index), (out, out_index)) in enumerate(zip(slot_refs(window_refs), slot_refs(parts))):
-        key, value = ref[index, 0], ref[index, 1]
-        grad_key = jnp.zeros((TILE, HD), jnp.float32)
-        grad_value = jnp.zeros((TILE, HD), jnp.float32)
-        for f in range(2):
-            cols = slice(f * TILE, (f + 1) * TILE)
-            dprob = contract_last(value, grads[f])
-            probs = weights_ref[f, s].astype(jnp.float32) * inverse_ref[0:1, cols]
-            dscore = (probs * (dprob - deltas[f])).astype(jnp.bfloat16)
-            grad_key = grad_key + contract_inner(dscore, queries[f])
-            grad_value = grad_value + contract_inner(probs.astype(jnp.bfloat16), grads[f])
-            grad_q[f] = grad_q[f] + contract_first(key, dscore)
-        out[out_index, 0] = (grad_key * SCORE_SCALE).astype(jnp.bfloat16)
-        out[out_index, 1] = grad_value.astype(jnp.bfloat16)
+    slots = slot_refs(window_refs)
+    outs = slot_refs(parts)
+    span = len(slots) * TILE
+    keys = jnp.concatenate([ref[index, 0] for ref, index in slots])
+    values = jnp.concatenate([ref[index, 1] for ref, index in slots])
+    grad_q, grad_keys, grad_values = [], 0.0, 0.0
+    for f in range(2):
+        cols = slice(f * TILE, (f + 1) * TILE)
+        dprob = contract_last(values, grads[f])
+        probs = weights_ref[f].reshape(span, TILE).astype(jnp.float32) * inverse_ref[0:1, cols]
+        dscore = (probs * (dprob - deltas[f])).astype(jnp.bfloat16)
+        grad_keys = grad_keys + contract_inner(dscore, queries[f])
+        grad_values = grad_values + contract_inner(probs.astype(jnp.bfloat16), grads[f])
+        grad_q.append(before_ref[f] + contract_first(keys, dscore))
+    for s, (out, index) in enumerate(outs):
+        rows = slice(s * TILE, (s + 1) * TILE)
+        out[index, 0] = (grad_keys[rows] * SCORE_SCALE).astype(jnp.bfloat16)
+        out[index, 1] = grad_values[rows].astype(jnp.bfloat16)
     for f in range(2):
         if last:
             grad_q_ref[f] = (grad_q[f] * SCORE_SCALE).T.astype(jnp.bfloat16)
@@ -257,7 +266,7 @@
         out_specs=tuple(any_specs(3) + vmem_specs(3)),
         scratch_shapes=[
             pltpu.VMEM((SLOTS, 2, TILE, HD), jnp.bfloat16),
-            pltpu.VMEM((SLOTS, TILE, TILE), jnp.float32),
+            pltpu.VMEM((2, SLOTS, TILE, TILE), jnp.float32),
             pltpu.VMEM((2, SLOTS, TILE, TILE), jnp.bfloat16),
             pltpu.SemaphoreType.DMA((2, 3)),
             pltpu.SemaphoreType.DMA((9,)),

time: 209 us -> 202 us (0.967)
  the two profiles are of different devices: /device:TPU:58 before, /device:TPU:38 now
where the time goes in v3:
time: 202 us; the launch traced here: 201 us
  starting transfers between devices  96.1 us (48%)
  waiting for transfers between devices  75.1 us (37%)
  Pallas kernels  23.2 us (11%)
  local copies, waits for them, and re-layouts  3.64 us (2%)
    ppermute x12, starting transfers between devices, column_shift(): return lax.ppermute(value, ('xr', 'zr', 'zc'), pairs)  38.1 us
    ppermute x1, waiting for transfers between devices, body(): row_back = lax.ppermute(row_sum, 'zr', SWAP)  19.7 us
    ppermute x12, waiting for transfers between devices, column_shift(): return lax.ppermute(value, ('xr', 'zr', 'zc'), pairs)  19.3 us
    ppermute x1, starting transfers between devices, body(): row = lax.ppermute(pair, 'zr', SWAP)  14.8 us
    ppermute x3, starting transfers between devices, from_rows(): lax.ppermute(value, 'y', [(i, (i + step) % 4) for i in range(4)])  11.1 us
    pallas_call x3, Pallas kernels, backward(): pl.pallas_call(functools.partial(backward_kernel, len(windows), last), ou...  9.34 us
    ppermute x1, waiting for transfers between devices, body(): up = lax.ppermute(pack, 'y', ring)  7.96 us
    ppermute x1, waiting for transfers between devices, body(): xf_back = lax.ppermute(frame_sum, 'xf', SWAP)  6.73 us
  transfers between devices with their start and end apart: 28, of which 15 were waited for; matrix products, arithmetic and copies ran while one was open for 1% of the time, Pallas kernels for 6%

profile of v3, /device:TPU:38, one launch (start us, length us, event | category | flops | bytes accessed | tf_op | source)
XLA Modules:
  0.0 201.1 jit_solution(9082126941793120085)
XLA Ops:
  5.7 3.3 %collective-permute-start = (bf16[784,128]{1,0:T(8,128)(2,1)S(1)}, bf16[784,128]{1,0:T(8,128)(2,1)S(1)}, u32[]{:S(2)}, u32[]{:S(2)}) collective-permute-start(bf16[784,128]{1,0:T(8,128)(2,1)S(1)} %pad_maximum_fusion.1), channel_id=1, source_target_pairs={{0,256},{256,0},{1,257},{257,1},{2,258},{258,2},{3,259},{259,3},{4... | collective-permute-start | bytes 602120 | tf_op jit(solution)/shard_map/ppermute | solution.py:389
  12.2 3.6 %collective-permute-done.frame_ref = bf16[784,128]{1,0:T(8,128)(2,1)S(1)} collective-permute-done((bf16[784,128]{1,0:T(8,128)(2,1)S(1)}, bf16[784,128]{1,0:T(8,128)(2,1)S(1)}, u32[]{:S(2)}, u32[]{:S(2)}) %collective-permute-start) | collective-permute-done | bytes 200736 | tf_op jit(solution)/shard_map/ppermute | solution.py:389
  15.9 3.5 %collective-permute-start.14 = (bf16[256,2560]{1,0:T(8,128)(2,1)S(1)}, bf16[256,2560]{1,0:T(8,128)(2,1)S(1)}, u32[]{:S(2)}, u32[]{:S(2)}) collective-permute-start(bf16[256,2560]{1,0:T(8,128)(2,1)S(1)} %pad_maximum_fusion.refs_4_.weight_ref.refs_0_), channel_id=1, source_target_pairs={{0,2},{2,4},{4,6},{6,0},{1,3},{3,5},{5,7},{7,1},{8,10},{10,12},{12... | collective-permute-start | bytes 3932168 | tf_op jit(solution)/shard_map/ppermute | solution.py:406
  19.4 14.8 %collective-permute-start.3 = (bf16[2,2,256,128]{3,2,1,0:T(8,128)(2,1)S(1)}, bf16[2,2,256,128]{3,2,1,0:T(8,128)(2,1)}, u32[]{:S(2)}, u32[]{:S(2)}) collective-permute-start(bf16[2,2,256,128]{3,2,1,0:T(8,128)(2,1)S(1)} %pair.1.refs_0_.refs_2_), channel_id=1, source_target_pairs={{0,64},{64,0},{1,65},{65,1},{2,66},{66,2},{3,67},{67,3},{4,68},{68... | collective-permute-start | bytes 786440 | tf_op jit(solution)/shard_map/ppermute | solution.py:393
  34.3 2.9 %collective-permute-start.1 = (bf16[2,2,256,128]{3,2,1,0:T(8,128)(2,1)S(1)}, bf16[2,2,256,128]{3,2,1,0:T(8,128)(2,1)S(1)}, u32[]{:S(2)}, u32[]{:S(2)}) collective-permute-start(bf16[2,2,256,128]{3,2,1,0:T(8,128)(2,1)S(1)} %pair.1.refs_0_.refs_2_), channel_id=1, source_target_pairs={{0,8},{8,16},{16,24},{24,32},{32,40},{40,48},{48,56},{64,72},{72,8... | collective-permute-start | bytes 786440 | tf_op jit(solution)/shard_map/ppermute | solution.py:341
  37.2 3.6 %collective-permute-start.16 = (bf16[256,2560]{1,0:T(8,128)(2,1)S(1)}, bf16[256,2560]{1,0:T(8,128)(2,1)}, u32[]{:S(2)}, u32[]{:S(2)}) collective-permute-start(bf16[256,2560]{1,0:T(8,128)(2,1)S(1)} %pad_maximum_fusion.refs_4_.weight_ref.refs_0_), channel_id=1, source_target_pairs={{0,6},{2,0},{4,2},{6,4},{1,7},{3,1},{5,3},{7,5},{8,14},{10,8},{12,... | collective-permute-start | bytes 3932168 | tf_op jit(solution)/shard_map/ppermute | solution.py:407
  40.8 8.0 %collective-permute-done.14.refs_5_.refs_1_ = bf16[256,2560]{1,0:T(8,128)(2,1)S(1)} collective-permute-done((bf16[256,2560]{1,0:T(8,128)(2,1)S(1)}, bf16[256,2560]{1,0:T(8,128)(2,1)S(1)}, u32[]{:S(2)}, u32[]{:S(2)}) %collective-permute-start.14) | collective-permute-done | bytes 1310752 | tf_op jit(solution)/shard_map/ppermute | solution.py:406
  53.0 3.8 %collective-permute-done.3.refs_3_.refs_2_ = bf16[2,2,256,128]{3,2,1,0:T(8,128)(2,1)} collective-permute-done((bf16[2,2,256,128]{3,2,1,0:T(8,128)(2,1)S(1)}, bf16[2,2,256,128]{3,2,1,0:T(8,128)(2,1)}, u32[]{:S(2)}, u32[]{:S(2)}) %collective-permute-start.3) | collective-permute-done | bytes 262176 | tf_op jit(solution)/shard_map/ppermute | solution.py:393
  58.0 2.8 %collective-permute-done.1.refs_1_.refs_3_ = bf16[2,2,256,128]{3,2,1,0:T(8,128)(2,1)S(1)} collective-permute-done((bf16[2,2,256,128]{3,2,1,0:T(8,128)(2,1)S(1)}, bf16[2,2,256,128]{3,2,1,0:T(8,128)(2,1)S(1)}, u32[]{:S(2)}, u32[]{:S(2)}) %collective-permute-start.1) | collective-permute-done | bytes 262176 | tf_op jit(solution)/shard_map/ppermute | solution.py:341
  60.8 3.4 %collective-permute-start.4 = (bf16[2,2,256,128]{3,2,1,0:T(8,128)(2,1)}, bf16[2,2,256,128]{3,2,1,0:T(8,128)(2,1)}, u32[]{:S(2)}, u32[]{:S(2)}) collective-permute-start(bf16[2,2,256,128]{3,2,1,0:T(8,128)(2,1)} %collective-permute-done.3.refs_3_.refs_2_), channel_id=1, source_target_pairs={{0,8},{8,16},{16,24},{24,32},{32,40},{40,48},{48,56},{64,72},{72,8... | collective-permute-start | bytes 786440 | tf_op jit(solution)/shard_map/ppermute | solution.py:341
  64.5 3.1 %collective-permute-start.5 = (bf16[2,2,256,128]{3,2,1,0:T(8,128)(2,1)}, bf16[2,2,256,128]{3,2,1,0:T(8,128)(2,1)S(1)}, u32[]{:S(2)}, u32[]{:S(2)}) collective-permute-start(bf16[2,2,256,128]{3,2,1,0:T(8,128)(2,1)} %collective-permute-done.3.refs_3_.refs_2_), channel_id=1, source_target_pairs={{8,0},{16,8},{24,16},{32,24},{40,32},{48,40},{56,48},{72,64},{80,7... | collective-permute-start | bytes 786440 | tf_op jit(solution)/shard_map/ppermute | solution.py:341
  70.4 3.1 %collective-permute-start.8 = (bf16[2,2,256,128]{3,2,1,0:T(8,128)(2,1)}, bf16[2,2,256,128]{3,2,1,0:T(8,128)(2,1)S(1)}, u32[]{:S(2)}, u32[]{:S(2)}) collective-permute-start(bf16[2,2,256,128]{3,2,1,0:T(8,128)(2,1)} %collective-permute-done.6.refs_6_.refs_2_), channel_id=1, source_target_pairs={{72,64},{80,72},{88,80},{96,88},{104,96},{112,104},{120,112},{136,... | collective-permute-start | bytes 786440 | tf_op jit(solution)/shard_map/ppermute | solution.py:341
  76.2 4.6 %collective-permute-done.8.refs_8_.refs_4_ = bf16[2,2,256,128]{3,2,1,0:T(8,128)(2,1)S(1)} collective-permute-done((bf16[2,2,256,128]{3,2,1,0:T(8,128)(2,1)}, bf16[2,2,256,128]{3,2,1,0:T(8,128)(2,1)S(1)}, u32[]{:S(2)}, u32[]{:S(2)}) %collective-permute-start.8) | collective-permute-done | bytes 262176 | tf_op jit(solution)/shard_map/ppermute | solution.py:341
  80.8 5.8 %attend.1 = (bf16[2,6,256,256]{3,2,1,0:T(8,128)(2,1)S(1)}, bf16[2,6,256,256]{3,2,1,0:T(8,128)(2,1)S(1)}, bf16[2,6,256,256]{3,2,1,0:T(8,128)(2,1)S(1)}, bf16[256,...) custom-call(s32[2,18]{1,0:T(2,128)S(1)} %add_convert_fusion.allowed_ref, ...), custom_call_target="tpu_custom_call" | custom-call | flops 3000000000 | bytes 8000000 | tf_op jit(solution)/shard_map/attend/pallas_call | solution.py:262
  86.6 3.3 %collective-permute-start.9 = (bf16[256,128]{1,0:T(8,128)(2,1)S(1)}, bf16[256,128]{1,0:T(8,128)(2,1)S(1)}, u32[]{:S(2)}, u32[]{:S(2)}) collective-permute-start(bf16[256,128]{1,0:T(8,128)(2,1)S(1)} %get-tuple-element.38.other_ref), channel_id=1, source_target_pairs={{0,256},{256,0},{1,257},{257,1},{2,258},{258,2},{3,259},{259,3},{4... | collective-permute-start | bytes 196616 | tf_op jit(solution)/shard_map/ppermute | solution.py:415
  89.9 4.3 %collective-permute-done.9 = bf16[256,128]{1,0:T(8,128)(2,1)S(1)} collective-permute-done((bf16[256,128]{1,0:T(8,128)(2,1)S(1)}, bf16[256,128]{1,0:T(8,128)(2,1)S(1)}, u32[]{:S(2)}, u32[]{:S(2)}) %collective-permute-start.9) | collective-permute-done | bytes 65568 | tf_op jit(solution)/shard_map/ppermute | solution.py:415
  94.2 3.4 %collective-permute-start.10 = (bf16[256,256]{1,0:T(8,128)(2,1)S(1)}, bf16[256,256]{1,0:T(8,128)(2,1)S(1)}, u32[]{:S(2)}, u32[]{:S(2)}) collective-permute-start(bf16[256,256]{1,0:T(8,128)(2,1)S(1)} %constant_dynamic-update-slice_fusion.refs_0_), channel_id=1, source_target_pairs={{0,2},{2,4},{4,6},{6,0},{1,3},{3,5},{5,7},{7,1},{8,10},{10,12},{12... | collective-permute-start | bytes 393224 | tf_op jit(solution)/shard_map/ppermute | solution.py:365
  97.6 3.6 %collective-permute-start.11 = (bf16[256,256]{1,0:T(8,128)(2,1)S(1)}, bf16[256,256]{1,0:T(8,128)(2,1)S(1)}, u32[]{:S(2)}, u32[]{:S(2)}) collective-permute-start(bf16[256,256]{1,0:T(8,128)(2,1)S(1)} %constant_dynamic-update-slice_fusion.refs_0_), channel_id=1, source_target_pairs={{0,4},{2,6},{4,0},{6,2},{1,5},{3,7},{5,1},{7,3},{8,12},{10,14},{12... | collective-permute-start | bytes 393224 | tf_op jit(solution)/shard_map/ppermute | solution.py:365
  101.3 4.1 %collective-permute-start.12 = (bf16[256,256]{1,0:T(8,128)(2,1)S(1)}, bf16[256,256]{1,0:T(8,128)(2,1)S(1)}, u32[]{:S(2)}, u32[]{:S(2)}) collective-permute-start(bf16[256,256]{1,0:T(8,128)(2,1)S(1)} %constant_dynamic-update-slice_fusion.refs_0_), channel_id=1, source_target_pairs={{0,6},{2,0},{4,2},{6,4},{1,7},{3,1},{5,3},{7,5},{8,14},{10,8},{12,... | collective-permute-start | bytes 393224 | tf_op jit(solution)/shard_map/ppermute | solution.py:365
  108.1 3.0 %project.1.mine_ref = bf16[256,2048]{1,0:T(8,128)(2,1)S(1)} custom-call(bf16[256,256]{1,0:T(8,128)(2,1)S(1)} %constant_dynamic-update-slice_fusion.refs_0_, bf16[256,256]{1,0:T(8,128)(2,1)S(1)} %collective-permute-done.10.refs_1_, bf16[256,256]{1,0:T(8,128)(2,1)S(1)} %collective-permute-done.11.refs_2_, ...), custom_call_target="tpu_custom_call" | custom-call | flops 1100000000 | bytes 6000000 | tf_op jit(solution)/shard_map/project/pallas_call | solution.py:306
  118.0 3.3 %collective-permute-start.18 = (bf16[256,128]{1,0:T(8,128)(2,1)S(1)}, bf16[256,128]{1,0:T(8,128)(2,1)S(1)}, u32[]{:S(2)}, u32[]{:S(2)}) collective-permute-start(bf16[256,128]{1,0:T(8,128)(2,1)S(1)} %get-tuple-element.42), channel_id=1, source_target_pairs={{0,256},{256,0},{1,257},{257,1},{2,258},{258,2},{3,259},{259,3},{4... | collective-permute-start | bytes 196616 | tf_op jit(solution)/shard_map/ppermute | solution.py:420
  121.3 4.4 %collective-permute-done.18.grad_got_ref = bf16[256,128]{1,0:T(8,128)(2,1)S(1)} collective-permute-done((bf16[256,128]{1,0:T(8,128)(2,1)S(1)}, bf16[256,128]{1,0:T(8,128)(2,1)S(1)}, u32[]{:S(2)}, u32[]{:S(2)}) %collective-permute-start.18) | collective-permute-done | bytes 65568 | tf_op jit(solution)/shard_map/ppermute | solution.py:420
  125.7 3.1 %attend_back.3 = (f32[2,128,256]{2,1,0:T(8,128)S(1)}, bf16[2,2,256,128]{3,2,1,0:T(8,128)(2,1)S(1)}, bf16[2,2,256,128]{3,2,1,0:T(8,128)(2,1)S(1)}, bf16[2,2,256,128]{3,2,1,0:T(8,128)(2,1)S(1)}) custom-call(bf16[256,128]{1,0:T(8,128)(2,1)S(1)} %get-tuple-element.35.q_mine_ref, bf16[784,128]{1,0:T(8,128)(2,1)S(1)} %collective-permute-done.frame_ref, ...), custom_call_target="tpu_custom_call" | custom-call | flops 805306368 | bytes 3600000 | tf_op jit(solution)/shard_map/attend_back/pallas_call | solution.py:287
  130.7 4.8 %collective-permute-start.24 = (bf16[2,2,256,128]{3,2,1,0:T(8,128)(2,1)S(1)}, bf16[2,2,256,128]{3,2,1,0:T(8,128)(2,1)S(1)}, u32[]{:S(2)}, u32[]{:S(2)}) collective-permute-start(bf16[2,2,256,128]{3,2,1,0:T(8,128)(2,1)S(1)} %get-tuple-element.57), channel_id=1, source_target_pairs={{64,72},{72,80},{80,88},{88,96},{96,104},{104,112},{112,120},{128,... | collective-permute-start | bytes 786440 | tf_op jit(solution)/shard_map/ppermute | solution.py:341
  135.5 3.1 %attend_back.4 = (f32[2,128,256]{2,1,0:T(8,128)S(1)}, bf16[2,2,256,128]{3,2,1,0:T(8,128)(2,1)S(1)}, bf16[2,2,256,128]{3,2,1,0:T(8,128)(2,1)S(1)}, bf16[2,2,256,128]{3,2,1,0:T(8,128)(2,1)S(1)}) custom-call(bf16[256,128]{1,0:T(8,128)(2,1)S(1)} %get-tuple-element.35.q_mine_ref, bf16[784,128]{1,0:T(8,128)(2,1)S(1)} %collective-permute-done.frame_ref, ...), custom_call_target="tpu_custom_call" | custom-call | flops 805306368 | bytes 3600000 | tf_op jit(solution)/shard_map/attend_back/pallas_call | solution.py:287
  140.6 5.0 %collective-permute-start.22 = (bf16[2,2,256,128]{3,2,1,0:T(8,128)(2,1)S(1)}, bf16[2,2,256,128]{3,2,1,0:T(8,128)(2,1)S(1)}, u32[]{:S(2)}, u32[]{:S(2)}) collective-permute-start(bf16[2,2,256,128]{3,2,1,0:T(8,128)(2,1)S(1)} %get-tuple-element.54), channel_id=1, source_target_pairs={{0,8},{8,16},{16,24},{24,32},{32,40},{40,48},{48,56},{64,72},{72,8... | collective-permute-start | bytes 786440 | tf_op jit(solution)/shard_map/ppermute | solution.py:341
  147.1 3.2 %attend_back.5 = (bf16[2,256,128]{2,1,0:T(8,128)(2,1)S(1)}, bf16[2,2,256,128]{3,2,1,0:T(8,128)(2,1)S(1)}, bf16[2,2,256,128]{3,2,1,0:T(8,128)(2,1)S(1)}, bf16[2,2,256,128]{3,2,1,0:T(8,128)(2,1)S(1)}) custom-call(bf16[256,128]{1,0:T(8,128)(2,1)S(1)} %get-tuple-element.35.q_mine_ref, bf16[784,128]{1,0:T(8,128)(2,1)S(1)} %collective-permute-done.frame_ref, ...), custom_call_target="tpu_custom_call" | custom-call | flops 805306368 | bytes 3600000 | tf_op jit(solution)/shard_map/attend_back/pallas_call | solution.py:287
  152.2 5.1 %collective-permute-start.20 = (bf16[2,2,256,128]{3,2,1,0:T(8,128)(2,1)S(1)}, bf16[2,2,256,128]{3,2,1,0:T(8,128)(2,1)S(1)}, u32[]{:S(2)}, u32[]{:S(2)}) collective-permute-start(bf16[2,2,256,128]{3,2,1,0:T(8,128)(2,1)S(1)} %get-tuple-element.51), channel_id=1, source_target_pairs={{0,8},{8,16},{16,24},{24,32},{32,40},{40,48},{48,56},{64,72},{72,8... | collective-permute-start | bytes 786440 | tf_op jit(solution)/shard_map/ppermute | solution.py:341
  157.5 4.1 %collective-permute-start.26 = (bf16[2,2,256,128]{3,2,1,0:T(8,128)(2,1)S(1)}, bf16[2,2,256,128]{3,2,1,0:T(8,128)(2,1)S(1)}, u32[]{:S(2)}, u32[]{:S(2)}) collective-permute-start(bf16[2,2,256,128]{3,2,1,0:T(8,128)(2,1)S(1)} %merge.1), channel_id=1, source_target_pairs={{0,64},{64,0},{1,65},{65,1},{2,66},{66,2},{3,67},{67,3},{4,68},{68... | collective-permute-start | bytes 786440 | tf_op jit(solution)/shard_map/ppermute | solution.py:444
  161.7 9.3 %collective-permute-done.20.left_ref = bf16[2,2,256,128]{3,2,1,0:T(8,128)(2,1)S(1)} collective-permute-done((bf16[2,2,256,128]{3,2,1,0:T(8,128)(2,1)S(1)}, bf16[2,2,256,128]{3,2,1,0:T(8,128)(2,1)S(1)}, u32[]{:S(2)}, u32[]{:S(2)}) %collective-permute-start.20) | collective-permute-done | bytes 262176 | tf_op jit(solution)/shard_map/ppermute | solution.py:341
  171.0 19.7 %collective-permute-done.26.row_ref = bf16[2,2,256,128]{3,2,1,0:T(8,128)(2,1)S(1)} collective-permute-done((bf16[2,2,256,128]{3,2,1,0:T(8,128)(2,1)S(1)}, bf16[2,2,256,128]{3,2,1,0:T(8,128)(2,1)S(1)}, u32[]{:S(2)}, u32[]{:S(2)}) %collective-permute-start.26) | collective-permute-done | bytes 262176 | tf_op jit(solution)/shard_map/ppermute | solution.py:444
  193.1 6.7 %collective-permute-done.27.frame_ref = bf16[3,256,128]{2,1,0:T(8,128)(2,1)S(1)} collective-permute-done((bf16[3,256,128]{2,1,0:T(8,128)(2,1)S(1)}, bf16[3,256,128]{2,1,0:T(8,128)(2,1)S(1)}, u32[]{:S(2)}, u32[]{:S(2)}) %collective-permute-start.27) | collective-permute-done | bytes 196640 | tf_op jit(solution)/shard_map/ppermute | solution.py:448
  (60 shorter events, 40.1 us)
Async XLA Ops:
  0.6 15.2 %copy-start.3 = (bf16[256,256]{1,0:T(8,128)(2,1)S(1)}, bf16[256,256]{1,0:T(8,128)(2,1)}, u32[]{:S(2)}) copy-start(bf16[256,256]{1,0:T(8,128)(2,1)} %param.10) | copy-start | bytes 393220
  1.8 0.9 copy-start
  2.7 0.9 copy-start.1
  3.6 0.9 copy-start.2
  5.7 10.1 %collective-permute-start = (bf16[784,128]{1,0:T(8,128)(2,1)S(1)}, bf16[784,128]{1,0:T(8,128)(2,1)S(1)}, u32[]{:S(2)}, u32[]{:S(2)}) collective-permute-start(bf16[784,128]{1,0:T(8,128)(2,1)S(1)} %pad_maximum_fusion.1), channel_id=1, source_target_pairs={{0,256},{256,0},{1,257},{257,1},{2,258},{258,2},{3,259},{259,3},{4... | collective-permute-start | bytes 602120 | tf_op jit(solution)/shard_map/ppermute | solution.py:389
  9.0 6.8 %collective-permute-start.13 = (bf16[256,256]{1,0:T(8,128)(2,1)}, bf16[256,256]{1,0:T(8,128)(2,1)S(1)}, u32[]{:S(2)}, u32[]{:S(2)}) collective-permute-start(bf16[256,256]{1,0:T(8,128)(2,1)} %param.10), channel_id=1, source_target_pairs={{0,1},{1,0},{2,3},{3,2},{4,5},{5,4},{6,7},{7,6},{8,9},{9,8},{10,11... | collective-permute-start | bytes 393224 | tf_op jit(solution)/shard_map/ppermute | solution.py:402
  15.9 32.8 %collective-permute-start.14 = (bf16[256,2560]{1,0:T(8,128)(2,1)S(1)}, bf16[256,2560]{1,0:T(8,128)(2,1)S(1)}, u32[]{:S(2)}, u32[]{:S(2)}) collective-permute-start(bf16[256,2560]{1,0:T(8,128)(2,1)S(1)} %pad_maximum_fusion.refs_4_.weight_ref.refs_0_), channel_id=1, source_target_pairs={{0,2},{2,4},{4,6},{6,0},{1,3},{3,5},{5,7},{7,1},{8,10},{10,12},{12... | collective-permute-start | bytes 3932168 | tf_op jit(solution)/shard_map/ppermute | solution.py:406
  19.4 37.3 %collective-permute-start.3 = (bf16[2,2,256,128]{3,2,1,0:T(8,128)(2,1)S(1)}, bf16[2,2,256,128]{3,2,1,0:T(8,128)(2,1)}, u32[]{:S(2)}, u32[]{:S(2)}) collective-permute-start(bf16[2,2,256,128]{3,2,1,0:T(8,128)(2,1)S(1)} %pair.1.refs_0_.refs_2_), channel_id=1, source_target_pairs={{0,64},{64,0},{1,65},{65,1},{2,66},{66,2},{3,67},{67,3},{4,68},{68... | collective-permute-start | bytes 786440 | tf_op jit(solution)/shard_map/ppermute | solution.py:393
  34.3 26.5 %collective-permute-start.1 = (bf16[2,2,256,128]{3,2,1,0:T(8,128)(2,1)S(1)}, bf16[2,2,256,128]{3,2,1,0:T(8,128)(2,1)S(1)}, u32[]{:S(2)}, u32[]{:S(2)}) collective-permute-start(bf16[2,2,256,128]{3,2,1,0:T(8,128)(2,1)S(1)} %pair.1.refs_0_.refs_2_), channel_id=1, source_target_pairs={{0,8},{8,16},{16,24},{24,32},{32,40},{40,48},{48,56},{64,72},{72,8... | collective-permute-start | bytes 786440 | tf_op jit(solution)/shard_map/ppermute | solution.py:341
  37.2 70.9 %collective-permute-start.16 = (bf16[256,2560]{1,0:T(8,128)(2,1)S(1)}, bf16[256,2560]{1,0:T(8,128)(2,1)}, u32[]{:S(2)}, u32[]{:S(2)}) collective-permute-start(bf16[256,2560]{1,0:T(8,128)(2,1)S(1)} %pad_maximum_fusion.refs_4_.weight_ref.refs_0_), channel_id=1, source_target_pairs={{0,6},{2,0},{4,2},{6,4},{1,7},{3,1},{5,3},{7,5},{8,14},{10,8},{12,... | collective-permute-start | bytes 3932168 | tf_op jit(solution)/shard_map/ppermute | solution.py:407
  48.7 59.4 %collective-permute-start.15 = (bf16[256,2560]{1,0:T(8,128)(2,1)S(1)}, bf16[256,2560]{1,0:T(8,128)(2,1)}, u32[]{:S(2)}, u32[]{:S(2)}) collective-permute-start(bf16[256,2560]{1,0:T(8,128)(2,1)S(1)} %collective-permute-done.14.refs_5_.refs_1_), channel_id=1, source_target_pairs={{0,2},{2,4},{4,6},{6,0},{1,3},{3,5},{5,7},{7,1},{8,10},{10,12},{12... | collective-permute-start | bytes 3932168 | tf_op jit(solution)/shard_map/ppermute | solution.py:408
  50.9 13.6 %collective-permute-start.2 = (bf16[2,2,256,128]{3,2,1,0:T(8,128)(2,1)S(1)}, bf16[2,2,256,128]{3,2,1,0:T(8,128)(2,1)}, u32[]{:S(2)}, u32[]{:S(2)}) collective-permute-start(bf16[2,2,256,128]{3,2,1,0:T(8,128)(2,1)S(1)} %pair.1.refs_0_.refs_2_), channel_id=1, source_target_pairs={{8,0},{16,8},{24,16},{32,24},{40,32},{48,40},{56,48},{72,64},{80,7... | collective-permute-start | bytes 786440 | tf_op jit(solution)/shard_map/ppermute | solution.py:341
  56.7 10.9 %collective-permute-start.6 = (bf16[2,2,256,128]{3,2,1,0:T(8,128)(2,1)}, bf16[2,2,256,128]{3,2,1,0:T(8,128)(2,1)}, u32[]{:S(2)}, u32[]{:S(2)}) collective-permute-start(bf16[2,2,256,128]{3,2,1,0:T(8,128)(2,1)} %collective-permute-done.3.refs_3_.refs_2_), channel_id=1, source_target_pairs={{0,128},{192,64},{1,129},{193,65},{2,130},{194,66},{3,131},{195,67... | collective-permute-start | bytes 786440 | tf_op jit(solution)/shard_map/ppermute | solution.py:394
  60.8 9.6 %collective-permute-start.4 = (bf16[2,2,256,128]{3,2,1,0:T(8,128)(2,1)}, bf16[2,2,256,128]{3,2,1,0:T(8,128)(2,1)}, u32[]{:S(2)}, u32[]{:S(2)}) collective-permute-start(bf16[2,2,256,128]{3,2,1,0:T(8,128)(2,1)} %collective-permute-done.3.refs_3_.refs_2_), channel_id=1, source_target_pairs={{0,8},{8,16},{16,24},{24,32},{32,40},{40,48},{48,56},{64,72},{72,8... | collective-permute-start | bytes 786440 | tf_op jit(solution)/shard_map/ppermute | solution.py:341
  64.5 9.8 %collective-permute-start.5 = (bf16[2,2,256,128]{3,2,1,0:T(8,128)(2,1)}, bf16[2,2,256,128]{3,2,1,0:T(8,128)(2,1)S(1)}, u32[]{:S(2)}, u32[]{:S(2)}) collective-permute-start(bf16[2,2,256,128]{3,2,1,0:T(8,128)(2,1)} %collective-permute-done.3.refs_3_.refs_2_), channel_id=1, source_target_pairs={{8,0},{16,8},{24,16},{32,24},{40,32},{48,40},{56,48},{72,64},{80,7... | collective-permute-start | bytes 786440 | tf_op jit(solution)/shard_map/ppermute | solution.py:341
  67.6 8.6 %collective-permute-start.7 = (bf16[2,2,256,128]{3,2,1,0:T(8,128)(2,1)}, bf16[2,2,256,128]{3,2,1,0:T(8,128)(2,1)S(1)}, u32[]{:S(2)}, u32[]{:S(2)}) collective-permute-start(bf16[2,2,256,128]{3,2,1,0:T(8,128)(2,1)} %collective-permute-done.6.refs_6_.refs_2_), channel_id=1, source_target_pairs={{64,72},{72,80},{80,88},{88,96},{96,104},{104,112},{112,120},{128,... | collective-permute-start | bytes 786440 | tf_op jit(solution)/shard_map/ppermute | solution.py:341
  70.4 10.4 %collective-permute-start.8 = (bf16[2,2,256,128]{3,2,1,0:T(8,128)(2,1)}, bf16[2,2,256,128]{3,2,1,0:T(8,128)(2,1)S(1)}, u32[]{:S(2)}, u32[]{:S(2)}) collective-permute-start(bf16[2,2,256,128]{3,2,1,0:T(8,128)(2,1)} %collective-permute-done.6.refs_6_.refs_2_), channel_id=1, source_target_pairs={{72,64},{80,72},{88,80},{96,88},{104,96},{112,104},{120,112},{136,... | collective-permute-start | bytes 786440 | tf_op jit(solution)/shard_map/ppermute | solution.py:341
  86.6 7.7 %collective-permute-start.9 = (bf16[256,128]{1,0:T(8,128)(2,1)S(1)}, bf16[256,128]{1,0:T(8,128)(2,1)S(1)}, u32[]{:S(2)}, u32[]{:S(2)}) collective-permute-start(bf16[256,128]{1,0:T(8,128)(2,1)S(1)} %get-tuple-element.38.other_ref), channel_id=1, source_target_pairs={{0,256},{256,0},{1,257},{257,1},{2,258},{258,2},{3,259},{259,3},{4... | collective-permute-start | bytes 196616 | tf_op jit(solution)/shard_map/ppermute | solution.py:415
  94.2 11.2 %collective-permute-start.10 = (bf16[256,256]{1,0:T(8,128)(2,1)S(1)}, bf16[256,256]{1,0:T(8,128)(2,1)S(1)}, u32[]{:S(2)}, u32[]{:S(2)}) collective-permute-start(bf16[256,256]{1,0:T(8,128)(2,1)S(1)} %constant_dynamic-update-slice_fusion.refs_0_), channel_id=1, source_target_pairs={{0,2},{2,4},{4,6},{6,0},{1,3},{3,5},{5,7},{7,1},{8,10},{10,12},{12... | collective-permute-start | bytes 393224 | tf_op jit(solution)/shard_map/ppermute | solution.py:365
  97.6 8.4 %collective-permute-start.11 = (bf16[256,256]{1,0:T(8,128)(2,1)S(1)}, bf16[256,256]{1,0:T(8,128)(2,1)S(1)}, u32[]{:S(2)}, u32[]{:S(2)}) collective-permute-start(bf16[256,256]{1,0:T(8,128)(2,1)S(1)} %constant_dynamic-update-slice_fusion.refs_0_), channel_id=1, source_target_pairs={{0,4},{2,6},{4,0},{6,2},{1,5},{3,7},{5,1},{7,3},{8,12},{10,14},{12... | collective-permute-start | bytes 393224 | tf_op jit(solution)/shard_map/ppermute | solution.py:365
  101.3 6.9 %collective-permute-start.12 = (bf16[256,256]{1,0:T(8,128)(2,1)S(1)}, bf16[256,256]{1,0:T(8,128)(2,1)S(1)}, u32[]{:S(2)}, u32[]{:S(2)}) collective-permute-start(bf16[256,256]{1,0:T(8,128)(2,1)S(1)} %constant_dynamic-update-slice_fusion.refs_0_), channel_id=1, source_target_pairs={{0,6},{2,0},{4,2},{6,4},{1,7},{3,1},{5,3},{7,5},{8,14},{10,8},{12,... | collective-permute-start | bytes 393224 | tf_op jit(solution)/shard_map/ppermute | solution.py:365
  111.1 4.6 %collective-permute-start.17 = (bf16[256,2048]{1,0:T(8,128)(2,1)S(1)}, bf16[256,2048]{1,0:T(8,128)(2,1)S(1)}, u32[]{:S(2)}, u32[]{:S(2)}) collective-permute-start(bf16[256,2048]{1,0:T(8,128)(2,1)S(1)} %project.1.mine_ref), channel_id=1, source_target_pairs={{0,1},{1,0},{2,3},{3,2},{4,5},{5,4},{6,7},{7,6},{8,9},{9,8},{10,11... | collective-permute-start | bytes 3145736 | tf_op jit(solution)/shard_map/ppermute | solution.py:418
  118.0 7.7 %collective-permute-start.18 = (bf16[256,128]{1,0:T(8,128)(2,1)S(1)}, bf16[256,128]{1,0:T(8,128)(2,1)S(1)}, u32[]{:S(2)}, u32[]{:S(2)}) collective-permute-start(bf16[256,128]{1,0:T(8,128)(2,1)S(1)} %get-tuple-element.42), channel_id=1, source_target_pairs={{0,256},{256,0},{1,257},{257,1},{2,258},{258,2},{3,259},{259,3},{4... | collective-permute-start | bytes 196616 | tf_op jit(solution)/shard_map/ppermute | solution.py:420
  128.8 16.9 %collective-permute-start.23 = (bf16[2,2,256,128]{3,2,1,0:T(8,128)(2,1)S(1)}, bf16[2,2,256,128]{3,2,1,0:T(8,128)(2,1)S(1)}, u32[]{:S(2)}, u32[]{:S(2)}) collective-permute-start(bf16[2,2,256,128]{3,2,1,0:T(8,128)(2,1)S(1)} %get-tuple-element.56), channel_id=1, source_target_pairs={{72,64},{80,72},{88,80},{96,88},{104,96},{112,104},{120,112},{136,... | collective-permute-start | bytes 786440 | tf_op jit(solution)/shard_map/ppermute | solution.py:341
  130.7 15.0 %collective-permute-start.24 = (bf16[2,2,256,128]{3,2,1,0:T(8,128)(2,1)S(1)}, bf16[2,2,256,128]{3,2,1,0:T(8,128)(2,1)S(1)}, u32[]{:S(2)}, u32[]{:S(2)}) collective-permute-start(bf16[2,2,256,128]{3,2,1,0:T(8,128)(2,1)S(1)} %get-tuple-element.57), channel_id=1, source_target_pairs={{64,72},{72,80},{80,88},{88,96},{96,104},{104,112},{112,120},{128,... | collective-permute-start | bytes 786440 | tf_op jit(solution)/shard_map/ppermute | solution.py:341
  138.7 18.6 %collective-permute-start.21 = (bf16[2,2,256,128]{3,2,1,0:T(8,128)(2,1)S(1)}, bf16[2,2,256,128]{3,2,1,0:T(8,128)(2,1)S(1)}, u32[]{:S(2)}, u32[]{:S(2)}) collective-permute-start(bf16[2,2,256,128]{3,2,1,0:T(8,128)(2,1)S(1)} %get-tuple-element.53), channel_id=1, source_target_pairs={{8,0},{16,8},{24,16},{32,24},{40,32},{48,40},{56,48},{72,64},{80,7... | collective-permute-start | bytes 786440 | tf_op jit(solution)/shard_map/ppermute | solution.py:341
  140.6 16.7 %collective-permute-start.22 = (bf16[2,2,256,128]{3,2,1,0:T(8,128)(2,1)S(1)}, bf16[2,2,256,128]{3,2,1,0:T(8,128)(2,1)S(1)}, u32[]{:S(2)}, u32[]{:S(2)}) collective-permute-start(bf16[2,2,256,128]{3,2,1,0:T(8,128)(2,1)S(1)} %get-tuple-element.54), channel_id=1, source_target_pairs={{0,8},{8,16},{16,24},{24,32},{32,40},{40,48},{48,56},{64,72},{72,8... | collective-permute-start | bytes 786440 | tf_op jit(solution)/shard_map/ppermute | solution.py:341
  145.8 11.6 %collective-permute-start.25 = (bf16[2,2,256,128]{3,2,1,0:T(8,128)(2,1)S(1)}, bf16[2,2,256,128]{3,2,1,0:T(8,128)(2,1)S(1)}, u32[]{:S(2)}, u32[]{:S(2)}) collective-permute-start(bf16[2,2,256,128]{3,2,1,0:T(8,128)(2,1)S(1)} %far_sum.1), channel_id=1, source_target_pairs={{128,0},{64,192},{129,1},{65,193},{130,2},{66,194},{131,3},{67,195... | collective-permute-start | bytes 786440 | tf_op jit(solution)/shard_map/ppermute | solution.py:435
  150.3 11.4 %collective-permute-start.19 = (bf16[2,2,256,128]{3,2,1,0:T(8,128)(2,1)S(1)}, bf16[2,2,256,128]{3,2,1,0:T(8,128)(2,1)S(1)}, u32[]{:S(2)}, u32[]{:S(2)}) collective-permute-start(bf16[2,2,256,128]{3,2,1,0:T(8,128)(2,1)S(1)} %get-tuple-element.50), channel_id=1, source_target_pairs={{8,0},{16,8},{24,16},{32,24},{40,32},{48,40},{56,48},{72,64},{80,7... | collective-permute-start | bytes 786440 | tf_op jit(solution)/shard_map/ppermute | solution.py:341
  152.2 18.8 %collective-permute-start.20 = (bf16[2,2,256,128]{3,2,1,0:T(8,128)(2,1)S(1)}, bf16[2,2,256,128]{3,2,1,0:T(8,128)(2,1)S(1)}, u32[]{:S(2)}, u32[]{:S(2)}) collective-permute-start(bf16[2,2,256,128]{3,2,1,0:T(8,128)(2,1)S(1)} %get-tuple-element.51), channel_id=1, source_target_pairs={{0,8},{8,16},{16,24},{24,32},{32,40},{40,48},{48,56},{64,72},{72,8... | collective-permute-start | bytes 786440 | tf_op jit(solution)/shard_map/ppermute | solution.py:341
  157.5 33.2 %collective-permute-start.26 = (bf16[2,2,256,128]{3,2,1,0:T(8,128)(2,1)S(1)}, bf16[2,2,256,128]{3,2,1,0:T(8,128)(2,1)S(1)}, u32[]{:S(2)}, u32[]{:S(2)}) collective-permute-start(bf16[2,2,256,128]{3,2,1,0:T(8,128)(2,1)S(1)} %merge.1), channel_id=1, source_target_pairs={{0,64},{64,0},{1,65},{65,1},{2,66},{66,2},{3,67},{67,3},{4,68},{68... | collective-permute-start | bytes 786440 | tf_op jit(solution)/shard_map/ppermute | solution.py:444
  190.7 9.1 %collective-permute-start.27 = (bf16[3,256,128]{2,1,0:T(8,128)(2,1)S(1)}, bf16[3,256,128]{2,1,0:T(8,128)(2,1)S(1)}, u32[]{:S(2)}, u32[]{:S(2)}) collective-permute-start(bf16[3,256,128]{2,1,0:T(8,128)(2,1)S(1)} %frame_sum.1), channel_id=1, source_target_pairs={{0,256},{256,0},{1,257},{257,1},{2,258},{258,2},{3,259},{259,3},{4... | collective-permute-start | bytes 589832 | tf_op jit(solution)/shard_map/ppermute | solution.py:448

commit v4 on v3

--- a/solution.py
+++ b/solution.py
@@ -78,26 +78,31 @@
         pair_ref[1, part] = frame_ref[part * TILE : (part + 1) * TILE, :]
 
 
-def forward_kernel(allowed_ref, q_mine_ref, frame_ref, *refs):
-    windows, kept_refs, refs = refs[:9], refs[9:12], refs[12:]
-    attended_refs, (inverse_ref, window_ref, scores_ref, weights_ref, sems, in_sems) = refs[:2], refs[2:]
-    pairs, start = [], 0
-    for window in windows:
-        pairs.append((window, window_ref.at[pl.ds(start, window.shape[0])]))
-        start += window.shape[0]
-    arriving = dict(zip(range(0, SLOTS, 2), copy_all(pairs, in_sems)))
+def forward_kernel(count, last, allowed_ref, q_mine_ref, frame_ref, *refs):
+    groups = range(3 - count, 3) if last else range(count)
+    windows, refs = refs[: 3 * count], refs[3 * count :]
+    if last:
+        (top_before_ref, total_before_ref, summed_before_ref), refs = refs[:3], refs[3:]
+    kept_refs, refs = refs[:count], refs[count:]
+    if last:
+        (*attended_refs, spread_ref, inverse_before_ref, inverse_ref), refs = refs[:5], refs[5:]
+    else:
+        (top_ref, total_ref, summed_ref), refs = refs[:3], refs[3:]
+    window_ref, scores_ref, weights_ref, sems, in_sems = refs
+    pairs = [(window, window_ref.at[pl.ds(2 * i, 2)]) for i, window in enumerate(windows)]
+    arriving = copy_all(pairs, in_sems)
     copies = []
 
     def bias_of(f, s):
-        return jnp.where(allowed_ref[f, s] > 0, 0.0, MASKED)
+        return jnp.where(allowed_ref[f, 6 * groups[0] + s] > 0, 0.0, MASKED)
 
     factor = SCORE_SCALE * LOG2_E
     queries = [q_mine_ref[...], frame_ref[2 * TILE : 3 * TILE, :]]
-    highest = [jnp.full((8, TILE), -jnp.inf, jnp.float32) for _ in range(2)]
-    for first in range(0, SLOTS, 6):
-        for s in range(first, first + 6):
-            if s in arriving:
-                arriving[s].wait()
+    highest = [jnp.full((8, TILE), 0.1 * MASKED, jnp.float32) for _ in range(2)]
+    for group in range(count):
+        for copy in arriving[3 * group : 3 * group + 3]:
+            copy.wait()
+        first = 6 * group
         keys = window_ref[first : first + 6, 0].reshape(6 * TILE, HD)
         for f in range(2):
             scores_ref[f, first : first + 6] = contract_last(keys, queries[f]).reshape(6, TILE, TILE)
@@ -109,7 +114,8 @@
         limit = jnp.max(highest[f], axis=0, keepdims=True)
         total = jnp.zeros((8, TILE), jnp.float32)
         summed = jnp.zeros((HD, TILE), jnp.float32)
-        for first in range(0, SLOTS, 6):
+        for group in range(count):
+            first = 6 * group
             for s in range(first, first + 6):
                 weights = jnp.exp2(scores_ref[f, s] * factor + (bias_of(f, s) - limit))
                 weights_ref[f, s] = weights.astype(jnp.bfloat16)
@@ -117,18 +123,27 @@
             block = weights_ref[f, first : first + 6].reshape(6 * TILE, TILE)
             summed = summed + contract_first(value, block)
             total = total + contract_first(jnp.full((6 * TILE, 8), 0.125, jnp.bfloat16), block)
-        inverse = 1.0 / jnp.sum(total, axis=0, keepdims=True)
-        inverse_ref[:, cols] = jnp.broadcast_to(inverse, (8, TILE))
-        attended_refs[f][...] = (summed * inverse).T.astype(jnp.bfloat16)
-        start = 0
-        for part, kept_ref in enumerate(kept_refs):
-            count = kept_ref.shape[1]
-            copy = pltpu.make_async_copy(
-                weights_ref.at[f, pl.ds(start, count)], kept_ref.at[f], sems.at[f, part]
-            )
+            copy = pltpu.make_async_copy(weights_ref.at[f, pl.ds(first, 6)], kept_refs[group].at[f], sems.at[f, group])
             copy.start()
             copies.append(copy)
-            start += count
+        total = jnp.sum(total, axis=0, keepdims=True)
+        if not last:
+            top_ref[:, cols] = jnp.broadcast_to(limit, (8, TILE))
+            total_ref[:, cols] = jnp.broadcast_to(total, (8, TILE))
+            summed_ref[f] = summed
+            continue
+        limit_before = top_before_ref[0:1, cols]
+        joint = jnp.maximum(limit, limit_before)
+        share, share_before = jnp.exp2(limit - joint), jnp.exp2(limit_before - joint)
+        inverse = 1.0 / (total * share + total_before_ref[0:1, cols] * share_before)
+        inverse_ref[:, cols] = jnp.broadcast_to(inverse * share, (8, TILE))
+        inverse_before_ref[:, cols] = jnp.broadcast_to(inverse * share_before, (8, TILE))
+        attended = (summed * (inverse * share) + summed_before_ref[f] * (inverse * share_before)).T
+        attended = attended.astype(jnp.bfloat16)
+        attended_refs[f][...] = attended
+        frame = allowed_ref[0, SLOTS]
+        for peer in range(4):
+            spread_ref[frame if f == 0 else 1 - frame, peer] = attended
     for copy in copies:
         copy.wait()
 
@@ -173,13 +188,18 @@
             grad_q_ref[f] = grad_q[f]
 
 
-def project_kernel(*refs):
-    attended_refs, pack_refs, out_ref = refs[:4], refs[4:8], refs[8]
+def project_kernel(place_ref, attended_ref, *refs):
+    pack_refs, (out_ref,) = refs[:4], refs[4:]
+    frame, row = place_ref[0], place_ref[1]
+    pieces = []
+    for back in range(4):
+        source = lax.rem(row + 4 - back, 4)
+        pieces.append(jnp.concatenate([attended_ref[frame, source], attended_ref[1 - frame, source]], axis=1))
     for block in range(8):
         cols = slice(block * TILE, (block + 1) * TILE)
         total = jnp.zeros((TILE, TILE), jnp.float32)
-        for attended_ref, pack_ref in zip(attended_refs, pack_refs):
-            total = total + contract_inner(attended_ref[...], pack_ref[:, cols])
+        for rows, pack_ref in zip(pieces, pack_refs):
+            total = total + contract_inner(rows, pack_ref[:, cols])
         out_ref[:, cols] = total.astype(jnp.bfloat16)
 
 
@@ -206,6 +226,10 @@
     out_ref[...] = sum_of(part_ref[...], right_ref[...], left_ref[...], third_ref[...]).astype(jnp.bfloat16)
 
 
+def widen_kernel(part_ref, out_ref):
+    out_ref[...] = part_ref[...].astype(jnp.float32)
+
+
 def far_kernel(part_ref, right_ref, left_ref, out_ref):
     out_ref[...] = sum_of(part_ref[...], right_ref[...], left_ref[...]).astype(jnp.bfloat16)
 
@@ -244,7 +268,7 @@
     return jax.ShapeDtypeStruct(dims, dtype)
 
 
-def simple(kernel, name, out_shape, *args, place=None, limit=8):
+def simple(kernel, name, out_shape, *args, place=None, limit=8, flops=1_000_000):
     head = [] if place is None else [place]
     return pl.pallas_call(
         kernel,
@@ -252,29 +276,36 @@
         in_specs=place_spec() * len(head) + vmem_specs(len(args)),
         out_specs=tuple(vmem_specs(len(out_shape))),
         compiler_params=pltpu.CompilerParams(vmem_limit_bytes=limit * 1024 * 1024),
-        cost_estimate=pl.CostEstimate(flops=1_000_000, bytes_accessed=2_000_000, transcendentals=0),
+        cost_estimate=pl.CostEstimate(flops=flops, bytes_accessed=2_000_000, transcendentals=0),
         name=name,
     )(*head, *args)
 
 
-def forward(allowed, q_mine, frame, windows):
-    kept = [shape(2, 6, TILE, TILE) for _ in range(3)]
-    return pl.pallas_call(
-        forward_kernel,
-        out_shape=(*kept, shape(TILE, HD), shape(TILE, HD), shape(8, 2 * TILE, dtype=jnp.float32)),
-        in_specs=place_spec() + vmem_specs(2) + any_specs(len(windows)),
-        out_specs=tuple(any_specs(3) + vmem_specs(3)),
+def forward(allowed, q_mine, frame, windows, before=()):
+    count, last = len(windows) // 3, bool(before)
+    rows = shape(8, 2 * TILE, dtype=jnp.float32)
+    if last:
+        out_shape = [shape(TILE, HD), shape(TILE, HD), shape(2, 4, TILE, HD), rows, rows]
+    else:
+        out_shape = [rows, rows, shape(2, HD, TILE, dtype=jnp.float32)]
+    return pl.pallas_call(
+        functools.partial(forward_kernel, count, last),
+        out_shape=tuple([shape(2, 6, TILE, TILE)] * count + out_shape),
+        in_specs=place_spec() + vmem_specs(2) + any_specs(len(windows)) + vmem_specs(len(before)),
+        out_specs=tuple(any_specs(count) + vmem_specs(len(out_shape))),
         scratch_shapes=[
-            pltpu.VMEM((SLOTS, 2, TILE, HD), jnp.bfloat16),
-            pltpu.VMEM((2, SLOTS, TILE, TILE), jnp.float32),
-            pltpu.VMEM((2, SLOTS, TILE, TILE), jnp.bfloat16),
-            pltpu.SemaphoreType.DMA((2, 3)),
-            pltpu.SemaphoreType.DMA((9,)),
+            pltpu.VMEM((6 * count, 2, TILE, HD), jnp.bfloat16),
+            pltpu.VMEM((2, 6 * count, TILE, TILE), jnp.float32),
+            pltpu.VMEM((2, 6 * count, TILE, TILE), jnp.bfloat16),
+            pltpu.SemaphoreType.DMA((2, count)),
+            pltpu.SemaphoreType.DMA((3 * count,)),
         ],
         compiler_params=pltpu.CompilerParams(vmem_limit_bytes=18 * 1024 * 1024),
-        cost_estimate=pl.CostEstimate(flops=3_000_000_000, bytes_accessed=8_000_000, transcendentals=2_400_000),
+        cost_estimate=pl.CostEstimate(
+            flops=count * 1_000_000_000, bytes_accessed=count * 2_700_000, transcendentals=count * 800_000
+        ),
         name="attend",
-    )(allowed, q_mine, frame, *windows)
+    )(allowed, q_mine, frame, *windows, *before)
 
 
 def backward(common, before, weights, windows, last=False):
@@ -302,16 +333,16 @@
     )(*common, before, weights, *windows)
 
 
-def project(attended, packs):
+def project(place, attended, packs):
     return pl.pallas_call(
         project_kernel,
-        in_specs=vmem_specs(8),
+        in_specs=place_spec() + vmem_specs(5),
         out_specs=pl.BlockSpec(memory_space=pltpu.VMEM),
         out_shape=jax.ShapeDtypeStruct((TILE, 8 * TILE), jnp.bfloat16),
         compiler_params=pltpu.CompilerParams(vmem_limit_bytes=10 * 1024 * 1024),
         cost_estimate=pl.CostEstimate(flops=1_100_000_000, bytes_accessed=6_000_000, transcendentals=0),
         name="project",
-    )(*attended, *packs)
+    )(place, attended, *packs)
 
 
 def residue_grad(place, mine, other, packs):
@@ -388,6 +419,7 @@
     )
     xf_got = lax.ppermute(message, "xf", SWAP)
     allowed = jnp.stack([listed(xf, xf), xf_got[3 * TILE, :SLOTS] > 0.5]).astype(jnp.int32)
+    allowed = jnp.concatenate([allowed, jnp.broadcast_to(xf.astype(jnp.int32), (2, 1))], axis=1)
 
     pair = simple(pair_kernel, "pair", [shape(2, 2, TILE, HD)], kv_mine, xf_got)[0]
     row = lax.ppermute(pair, "zr", SWAP)
@@ -408,24 +440,22 @@
     across = lax.ppermute(up, "y", ring)
     packs = [pack, up, across, down]
 
-    *weights, own, other, inverse = forward(
-        allowed, q_mine, xf_got, own_windows + row_windows + third_windows
+    own_weights, row_weights, *sums_before = forward(allowed, q_mine, xf_got, own_windows + row_windows)
+    third_weights, own, other, spread, inverse, inverse_third = forward(
+        allowed, q_mine, xf_got, third_windows, sums_before
     )
 
-    got = lax.ppermute(other, "xf", SWAP)
-    attended = jnp.concatenate([own, got], axis=1)
-    partial_mine = project([attended] + from_rows(attended), packs)
+    gathered = lax.all_to_all(spread.reshape(8, TILE, HD), ("xf", "y"), 0, 0, tiled=True)
+    partial_mine = project(place, gathered.reshape(2, 4, TILE, HD), packs)
     partial_other = lax.ppermute(partial_mine, "core", SWAP)
     student, grad_mine, grad_other = residue_grad(place, partial_mine, partial_other, packs)
     grad_got = lax.ppermute(grad_other, "xf", SWAP)
 
-    own_weights, row_weights, third_weights = weights
     common = (q_mine, xf_got, grad_mine, grad_got, own, other, inverse)
+    common_third = common[:-1] + (inverse_third,)
     before = jnp.zeros((2, HD, TILE), jnp.float32)
-    before, far, far_left, far_right = backward(common, before, third_weights, third_windows)
+    before, far, far_left, far_right = backward(common_third, before, third_weights, third_windows)
     before, part, part_left, part_right = backward(common, before, row_weights, row_windows)
-    grad_query, near, near_left, near_right = backward(common, before, own_weights, own_windows, last=True)
-
     def returned(left, right, lines):
         return column_shift(left, -1, lines), column_shift(right, 1, lines)
 
@@ -442,6 +472,9 @@
         third_back,
     )[0]
     row_back = lax.ppermute(row_sum, "zr", SWAP)
+    row_back = simple(widen_kernel, "widen", [shape(2, 2, TILE, HD, dtype=jnp.float32)], row_back, flops=30_000_000_000)[0]
+    before, _ = lax.optimization_barrier((before, row_sum))
+    grad_query, near, near_left, near_right = backward(common, before, own_weights, own_windows, last=True)
     from_right, from_left = returned(near_left, near_right, ALL_LINES)
     sums = (near, from_right, from_left, row_back, grad_query)
     frame_sum = simple(frame_kernel, "frame_sum", [shape(3, TILE, HD)], *sums)[0]

time: 202 us -> 193 us (0.955)
  the two profiles are of different devices: /device:TPU:38 before, /device:TPU:2 now
where the time goes in v4:
time: 193 us; the launch traced here: 192 us
  starting transfers between devices  82.5 us (43%)
  waiting for transfers between devices  63 us (33%)
  Pallas kernels  24 us (12%)
  blocking collectives  15.7 us (8%)
  local copies, waits for them, and re-layouts  3.62 us (2%)
    ppermute x12, starting transfers between devices, column_shift(): return lax.ppermute(value, ('xr', 'zr', 'zc'), pairs)  32.4 us
    ppermute x12, waiting for transfers between devices, column_shift(): return lax.ppermute(value, ('xr', 'zr', 'zc'), pairs)  19.4 us
    ppermute x1, starting transfers between devices, body(): row = lax.ppermute(pair, 'zr', SWAP)  15.7 us
    all_to_all x1, blocking collectives, body(): lax.all_to_all(spread.reshape(8, TILE, HD), ('xf', 'y'), 0, 0, tiled=True)  15.7 us
    ppermute x1, starting transfers between devices, body(): row_back = lax.ppermute(row_sum, 'zr', SWAP)  10.2 us
    pallas_call x3, Pallas kernels, backward(): pl.pallas_call(functools.partial(backward_kernel, len(windows), last), ou...  8.53 us
    ppermute x1, waiting for transfers between devices, body(): xf_back = lax.ppermute(frame_sum, 'xf', SWAP)  8.27 us
    pallas_call x2, Pallas kernels, forward(): pl.pallas_call(functools.partial(forward_kernel, count, last), out_shape=...  7.26 us
  transfers between devices with their start and end apart: 24, of which 14 were waited for; matrix products, arithmetic and copies ran while one was open for 1% of the time, Pallas kernels for 7%

profile of v4, /device:TPU:2, one launch (start us, length us, event | category | flops | bytes accessed | tf_op | source)
XLA Modules:
  0.0 191.7 jit_solution(14030200349723480357)
XLA Ops:
  5.7 4.0 %collective-permute-start = (bf16[784,128]{1,0:T(8,128)(2,1)S(1)}, bf16[784,128]{1,0:T(8,128)(2,1)S(1)}, u32[]{:S(2)}, u32[]{:S(2)}) collective-permute-start(bf16[784,128]{1,0:T(8,128)(2,1)S(1)} %pad_maximum_fusion.1), channel_id=1, source_target_pairs={{0,256},{256,0},{1,257},{257,1},{2,258},{258,2},{3,259},{259,3},{4... | collective-permute-start | bytes 602120 | tf_op jit(solution)/shard_map/ppermute | solution.py:420
  12.9 2.9 %collective-permute-done.frame_ref = bf16[784,128]{1,0:T(8,128)(2,1)S(1)} collective-permute-done((bf16[784,128]{1,0:T(8,128)(2,1)S(1)}, bf16[784,128]{1,0:T(8,128)(2,1)S(1)}, u32[]{:S(2)}, u32[]{:S(2)}) %collective-permute-start) | collective-permute-done | bytes 200736 | tf_op jit(solution)/shard_map/ppermute | solution.py:420
  15.9 3.5 %collective-permute-start.10 = (bf16[256,2560]{1,0:T(8,128)(2,1)S(1)}, bf16[256,2560]{1,0:T(8,128)(2,1)S(1)}, u32[]{:S(2)}, u32[]{:S(2)}) collective-permute-start(bf16[256,2560]{1,0:T(8,128)(2,1)S(1)} %pad_maximum_fusion.refs_0_.weight_ref), channel_id=1, source_target_pairs={{0,2},{2,4},{4,6},{6,0},{1,3},{3,5},{5,7},{7,1},{8,10},{10,12},{12... | collective-permute-start | bytes 3932168 | tf_op jit(solution)/shard_map/ppermute | solution.py:438
  19.4 15.7 %collective-permute-start.1 = (bf16[2,2,256,128]{3,2,1,0:T(8,128)(2,1)S(1)}, bf16[2,2,256,128]{3,2,1,0:T(8,128)(2,1)}, u32[]{:S(2)}, u32[]{:S(2)}) collective-permute-start(bf16[2,2,256,128]{3,2,1,0:T(8,128)(2,1)S(1)} %pair.1.refs_0_.refs_2_), channel_id=1, source_target_pairs={{0,64},{64,0},{1,65},{65,1},{2,66},{66,2},{3,67},{67,3},{4,68},{68... | collective-permute-start | bytes 786440 | tf_op jit(solution)/shard_map/ppermute | solution.py:425
  35.2 2.9 %collective-permute-start.5 = (bf16[2,2,256,128]{3,2,1,0:T(8,128)(2,1)S(1)}, bf16[2,2,256,128]{3,2,1,0:T(8,128)(2,1)S(1)}, u32[]{:S(2)}, u32[]{:S(2)}) collective-permute-start(bf16[2,2,256,128]{3,2,1,0:T(8,128)(2,1)S(1)} %pair.1.refs_0_.refs_2_), channel_id=1, source_target_pairs={{0,8},{8,16},{16,24},{24,32},{32,40},{40,48},{48,56},{64,72},{72,8... | collective-permute-start | bytes 786440 | tf_op jit(solution)/shard_map/ppermute | solution.py:372
  39.4 3.6 %collective-permute-start.12 = (bf16[256,2560]{1,0:T(8,128)(2,1)S(1)}, bf16[256,2560]{1,0:T(8,128)(2,1)}, u32[]{:S(2)}, u32[]{:S(2)}) collective-permute-start(bf16[256,2560]{1,0:T(8,128)(2,1)S(1)} %pad_maximum_fusion.refs_0_.weight_ref), channel_id=1, source_target_pairs={{0,6},{2,0},{4,2},{6,4},{1,7},{3,1},{5,3},{7,5},{8,14},{10,8},{12,... | collective-permute-start | bytes 3932168 | tf_op jit(solution)/shard_map/ppermute | solution.py:439
  43.0 5.7 %collective-permute-done.10.refs_1_ = bf16[256,2560]{1,0:T(8,128)(2,1)S(1)} collective-permute-done((bf16[256,2560]{1,0:T(8,128)(2,1)S(1)}, bf16[256,2560]{1,0:T(8,128)(2,1)S(1)}, u32[]{:S(2)}, u32[]{:S(2)}) %collective-permute-start.10) | collective-permute-done | bytes 1310752 | tf_op jit(solution)/shard_map/ppermute | solution.py:438
  48.7 2.2 %collective-permute-start.11 = (bf16[256,2560]{1,0:T(8,128)(2,1)S(1)}, bf16[256,2560]{1,0:T(8,128)(2,1)}, u32[]{:S(2)}, u32[]{:S(2)}) collective-permute-start(bf16[256,2560]{1,0:T(8,128)(2,1)S(1)} %collective-permute-done.10.refs_1_), channel_id=1, source_target_pairs={{0,2},{2,4},{4,6},{6,0},{1,3},{3,5},{5,7},{7,1},{8,10},{10,12},{12... | collective-permute-start | bytes 3932168 | tf_op jit(solution)/shard_map/ppermute | solution.py:440
  51.0 5.9 %collective-permute-done.1.refs_3_.refs_2_ = bf16[2,2,256,128]{3,2,1,0:T(8,128)(2,1)} collective-permute-done((bf16[2,2,256,128]{3,2,1,0:T(8,128)(2,1)S(1)}, bf16[2,2,256,128]{3,2,1,0:T(8,128)(2,1)}, u32[]{:S(2)}, u32[]{:S(2)}) %collective-permute-start.1) | collective-permute-done | bytes 262176 | tf_op jit(solution)/shard_map/ppermute | solution.py:425
  56.9 3.2 %collective-permute-start.7 = (bf16[2,2,256,128]{3,2,1,0:T(8,128)(2,1)}, bf16[2,2,256,128]{3,2,1,0:T(8,128)(2,1)S(1)}, u32[]{:S(2)}, u32[]{:S(2)}) collective-permute-start(bf16[2,2,256,128]{3,2,1,0:T(8,128)(2,1)} %collective-permute-done.1.refs_3_.refs_2_), channel_id=1, source_target_pairs={{0,8},{8,16},{16,24},{24,32},{32,40},{40,48},{48,56},{64,72},{72,8... | collective-permute-start | bytes 786440 | tf_op jit(solution)/shard_map/ppermute | solution.py:372
  60.1 2.4 %collective-permute-done.5.refs_1_.refs_3_ = bf16[2,2,256,128]{3,2,1,0:T(8,128)(2,1)S(1)} collective-permute-done((bf16[2,2,256,128]{3,2,1,0:T(8,128)(2,1)S(1)}, bf16[2,2,256,128]{3,2,1,0:T(8,128)(2,1)S(1)}, u32[]{:S(2)}, u32[]{:S(2)}) %collective-permute-start.5) | collective-permute-done | bytes 262176 | tf_op jit(solution)/shard_map/ppermute | solution.py:372
  65.3 5.7 %collective-permute-done.2.refs_0_.refs_2_ = bf16[2,2,256,128]{3,2,1,0:T(8,128)(2,1)S(1)} collective-permute-done((bf16[2,2,256,128]{3,2,1,0:T(8,128)(2,1)}, bf16[2,2,256,128]{3,2,1,0:T(8,128)(2,1)S(1)}, u32[]{:S(2)}, u32[]{:S(2)}) %collective-permute-start.2) | collective-permute-done | bytes 262176 | tf_op jit(solution)/shard_map/ppermute | solution.py:426
  71.0 4.4 %collective-permute-start.3 = (bf16[2,2,256,128]{3,2,1,0:T(8,128)(2,1)S(1)}, bf16[2,2,256,128]{3,2,1,0:T(8,128)(2,1)S(1)}, u32[]{:S(2)}, u32[]{:S(2)}) collective-permute-start(bf16[2,2,256,128]{3,2,1,0:T(8,128)(2,1)S(1)} %collective-permute-done.2.refs_0_.refs_2_), channel_id=1, source_target_pairs={{64,72},{72,80},{80,88},{88,96},{96,104},{104,112},{112,120},{128,... | collective-permute-start | bytes 786440 | tf_op jit(solution)/shard_map/ppermute | solution.py:372
  76.8 4.7 %attend.2 = (bf16[2,6,256,256]{3,2,1,0:T(8,128)(2,1)S(1)}, bf16[2,6,256,256]{3,2,1,0:T(8,128)(2,1)S(1)}, f32[8,512]{1,0:T(8,128)S(1)}, f32[8,512]{1,0:T(8,128)S(1)}, f32[2,128,256]{2,1,0:T(8,128)S(1)}) custom-call(s32[2,19]{1,0:T(2,128)S(1)} %concatenate.13.allowed_ref, bf16[256,128]{1,0:T(8,128)(2,1)S(1)} %get-tuple-element.41.q_mine_ref, ...), custom_call_target="tpu_custom_call" | custom-call | flops 2000000000 | bytes 5400000 | tf_op jit(solution)/shard_map/attend/pallas_call | solution.py:291
  81.5 2.2 %collective-permute-done.4.refs_2_.refs_4_ = bf16[2,2,256,128]{3,2,1,0:T(8,128)(2,1)S(1)} collective-permute-done((bf16[2,2,256,128]{3,2,1,0:T(8,128)(2,1)S(1)}, bf16[2,2,256,128]{3,2,1,0:T(8,128)(2,1)S(1)}, u32[]{:S(2)}, u32[]{:S(2)}) %collective-permute-start.4) | collective-permute-done | bytes 262176 | tf_op jit(solution)/shard_map/ppermute | solution.py:372
  83.7 2.5 %attend.3 = (bf16[2,6,256,256]{3,2,1,0:T(8,128)(2,1)S(1)}, bf16[256,128]{1,0:T(8,128)(2,1)S(1)}, bf16[256,128]{1,0:T(8,128)(2,1)S(1)}, bf16[2,4,256,128]{3,2,1,0...) custom-call(s32[2,19]{1,0:T(2,128)S(1)} %concatenate.13.allowed_ref, ...), custom_call_target="tpu_custom_call" | custom-call | flops 1000000000 | bytes 2700000 | tf_op jit(solution)/shard_map/attend/pallas_call | solution.py:291
  86.2 15.7 %all_to_all.5 = bf16[8,256,128]{2,1,0:T(8,128)(2,1)S(1)} all-to-all(bf16[8,256,128]{2,1,0:T(8,128)(2,1)S(1)} %bitcast.30), channel_id=1, replica_groups=mesh['xf'=2,'xr'=2,'zr'=2,'zc'=8,'y'=4,'core'=2] {'xf','y'}, dimensions={0} | all-to-all | bytes 1048576 | tf_op jit(solution)/shard_map/all_to_all | solution.py:448
  101.9 3.0 %project.1.mine_ref = bf16[256,2048]{1,0:T(8,128)(2,1)S(1)} custom-call(s32[3]{0:T(128)S(1)} %pad_add_fusion.place_ref, bf16[2,4,256,128]{3,2,1,0:T(8,128)(2,1)S(1)} %bitcast.29, bf16[256,2560]{1,0:T(8,128)(2,1)S(1)} %pad_maximum_fusion.refs_0_.weight_ref, bf16[256,2560]{1,0:T(8,128)(2,1)S(1)} %collective-permute-done.10.refs_1_, ...), custom_call_target="tpu_custom_call" | custom-call | flops 1100000000 | bytes 6000000 | tf_op jit(solution)/shard_map/project/pallas_call | solution.py:337
  106.8 2.6 %collective-permute-done.13.other_ref = bf16[256,2048]{1,0:T(8,128)(2,1)S(1)} collective-permute-done((bf16[256,2048]{1,0:T(8,128)(2,1)S(1)}, bf16[256,2048]{1,0:T(8,128)(2,1)S(1)}, u32[]{:S(2)}, u32[]{:S(2)}) %collective-permute-start.13) | collective-permute-done | bytes 1048608 | tf_op jit(solution)/shard_map/ppermute | solution.py:450
  109.5 2.4 %residue.1 = (bf16[256,256]{1,0:T(8,128)(2,1)}, bf16[256,128]{1,0:T(8,128)(2,1)S(1)}, bf16[256,128]{1,0:T(8,128)(2,1)S(1)}) custom-call(s32[3]{0:T(128)S(1)} %pad_add_fusion.place_ref, bf16[256,2048]{1,0:T(8,128)(2,1)S(1)} %project.1.mine_ref, bf16[256,2048]{1,0:T(8,128)(2,1)S(1)} %collective-permute-done.13.other_ref, ...), custom_call_target="tpu_custom_call" | custom-call | flops 300000000 | bytes 5000000 | tf_op jit(solution)/shard_map/residue/pallas_call | solution.py:350
  111.8 2.5 %collective-permute-start.14 = (bf16[256,128]{1,0:T(8,128)(2,1)S(1)}, bf16[256,128]{1,0:T(8,128)(2,1)S(1)}, u32[]{:S(2)}, u32[]{:S(2)}) collective-permute-start(bf16[256,128]{1,0:T(8,128)(2,1)S(1)} %get-tuple-element.50), channel_id=1, source_target_pairs={{0,256},{256,0},{1,257},{257,1},{2,258},{258,2},{3,259},{259,3},{4... | collective-permute-start | bytes 196616 | tf_op jit(solution)/shard_map/ppermute | solution.py:452
  114.4 5.1 %collective-permute-done.14.grad_got_ref = bf16[256,128]{1,0:T(8,128)(2,1)S(1)} collective-permute-done((bf16[256,128]{1,0:T(8,128)(2,1)S(1)}, bf16[256,128]{1,0:T(8,128)(2,1)S(1)}, u32[]{:S(2)}, u32[]{:S(2)}) %collective-permute-start.14) | collective-permute-done | bytes 65568 | tf_op jit(solution)/shard_map/ppermute | solution.py:452
  119.5 2.3 %attend_back.3 = (f32[2,128,256]{2,1,0:T(8,128)S(1)}, bf16[2,2,256,128]{3,2,1,0:T(8,128)(2,1)S(1)}, bf16[2,2,256,128]{3,2,1,0:T(8,128)(2,1)S(1)}, bf16[2,2,256,128]{3,2,1,0:T(8,128)(2,1)S(1)}) custom-call(bf16[256,128]{1,0:T(8,128)(2,1)S(1)} %get-tuple-element.41.q_mine_ref, bf16[784,128]{1,0:T(8,128)(2,1)S(1)} %collective-permute-done.frame_ref, ...), custom_call_target="tpu_custom_call" | custom-call | flops 805306368 | bytes 3600000 | tf_op jit(solution)/shard_map/attend_back/pallas_call | solution.py:318
  123.1 4.7 %collective-permute-start.18 = (bf16[2,2,256,128]{3,2,1,0:T(8,128)(2,1)S(1)}, bf16[2,2,256,128]{3,2,1,0:T(8,128)(2,1)S(1)}, u32[]{:S(2)}, u32[]{:S(2)}) collective-permute-start(bf16[2,2,256,128]{3,2,1,0:T(8,128)(2,1)S(1)} %get-tuple-element.64), channel_id=1, source_target_pairs={{64,72},{72,80},{80,88},{88,96},{96,104},{104,112},{112,120},{128,... | collective-permute-start | bytes 786440 | tf_op jit(solution)/shard_map/ppermute | solution.py:372
  127.9 3.1 %attend_back.4 = (f32[2,128,256]{2,1,0:T(8,128)S(1)}, bf16[2,2,256,128]{3,2,1,0:T(8,128)(2,1)S(1)}, bf16[2,2,256,128]{3,2,1,0:T(8,128)(2,1)S(1)}, bf16[2,2,256,128]{3,2,1,0:T(8,128)(2,1)S(1)}) custom-call(bf16[256,128]{1,0:T(8,128)(2,1)S(1)} %get-tuple-element.41.q_mine_ref, bf16[784,128]{1,0:T(8,128)(2,1)S(1)} %collective-permute-done.frame_ref, ...), custom_call_target="tpu_custom_call" | custom-call | flops 805306368 | bytes 3600000 | tf_op jit(solution)/shard_map/attend_back/pallas_call | solution.py:318
  132.3 4.8 %collective-permute-start.16 = (bf16[2,2,256,128]{3,2,1,0:T(8,128)(2,1)S(1)}, bf16[2,2,256,128]{3,2,1,0:T(8,128)(2,1)S(1)}, u32[]{:S(2)}, u32[]{:S(2)}) collective-permute-start(bf16[2,2,256,128]{3,2,1,0:T(8,128)(2,1)S(1)} %get-tuple-element.61), channel_id=1, source_target_pairs={{0,8},{8,16},{16,24},{24,32},{32,40},{40,48},{48,56},{64,72},{72,8... | collective-permute-start | bytes 786440 | tf_op jit(solution)/shard_map/ppermute | solution.py:372
  143.0 10.2 %collective-permute-start.22 = (bf16[2,2,256,128]{3,2,1,0:T(8,128)(2,1)S(1)}, bf16[2,2,256,128]{3,2,1,0:T(8,128)(2,1)S(1)}, u32[]{:S(2)}, u32[]{:S(2)}) collective-permute-start(bf16[2,2,256,128]{3,2,1,0:T(8,128)(2,1)S(1)} %merge.1), channel_id=1, source_target_pairs={{0,64},{64,0},{1,65},{65,1},{2,66},{66,2},{3,67},{67,3},{4,68},{68... | collective-permute-start | bytes 786440 | tf_op jit(solution)/shard_map/ppermute | solution.py:474
  153.3 3.2 %attend_back.5 = (bf16[2,256,128]{2,1,0:T(8,128)(2,1)S(1)}, bf16[2,2,256,128]{3,2,1,0:T(8,128)(2,1)S(1)}, bf16[2,2,256,128]{3,2,1,0:T(8,128)(2,1)S(1)}, bf16[2,2,256,128]{3,2,1,0:T(8,128)(2,1)S(1)}) custom-call(bf16[256,128]{1,0:T(8,128)(2,1)S(1)} %get-tuple-element.41.q_mine_ref, bf16[784,128]{1,0:T(8,128)(2,1)S(1)} %collective-permute-done.frame_ref, ...), custom_call_target="tpu_custom_call" | custom-call | flops 805306368 | bytes 3600000 | tf_op jit(solution)/shard_map/attend_back/pallas_call | solution.py:318
  157.8 4.6 %collective-permute-start.21 = (bf16[2,2,256,128]{3,2,1,0:T(8,128)(2,1)S(1)}, bf16[2,2,256,128]{3,2,1,0:T(8,128)(2,1)S(1)}, u32[]{:S(2)}, u32[]{:S(2)}) collective-permute-start(bf16[2,2,256,128]{3,2,1,0:T(8,128)(2,1)S(1)} %get-tuple-element.69), channel_id=1, source_target_pairs={{0,8},{8,16},{16,24},{24,32},{32,40},{40,48},{48,56},{64,72},{72,8... | collective-permute-start | bytes 786440 | tf_op jit(solution)/shard_map/ppermute | solution.py:372
  162.3 5.9 %collective-permute-done.22.part_ref = bf16[2,2,256,128]{3,2,1,0:T(8,128)(2,1)S(1)} collective-permute-done((bf16[2,2,256,128]{3,2,1,0:T(8,128)(2,1)S(1)}, bf16[2,2,256,128]{3,2,1,0:T(8,128)(2,1)S(1)}, u32[]{:S(2)}, u32[]{:S(2)}) %collective-permute-start.22) | collective-permute-done | bytes 262176 | tf_op jit(solution)/shard_map/ppermute | solution.py:474
  168.3 11.8 %collective-permute-done.20.right_ref = bf16[2,2,256,128]{3,2,1,0:T(8,128)(2,1)S(1)} collective-permute-done((bf16[2,2,256,128]{3,2,1,0:T(8,128)(2,1)S(1)}, bf16[2,2,256,128]{3,2,1,0:T(8,128)(2,1)S(1)}, u32[]{:S(2)}, u32[]{:S(2)}) %collective-permute-start.20) | collective-permute-done | bytes 262176 | tf_op jit(solution)/shard_map/ppermute | solution.py:372
  182.1 8.3 %collective-permute-done.23.frame_ref = bf16[3,256,128]{2,1,0:T(8,128)(2,1)S(1)} collective-permute-done((bf16[3,256,128]{2,1,0:T(8,128)(2,1)S(1)}, bf16[3,256,128]{2,1,0:T(8,128)(2,1)S(1)}, u32[]{:S(2)}, u32[]{:S(2)}) %collective-permute-start.23) | collective-permute-done | bytes 196640 | tf_op jit(solution)/shard_map/ppermute | solution.py:481
  (54 shorter events, 28.9 us)
Async XLA Ops:
  0.6 15.2 %copy-start.3 = (bf16[256,256]{1,0:T(8,128)(2,1)S(1)}, bf16[256,256]{1,0:T(8,128)(2,1)}, u32[]{:S(2)}) copy-start(bf16[256,256]{1,0:T(8,128)(2,1)} %param.10) | copy-start | bytes 393220
  1.8 0.9 copy-start
  2.7 0.9 copy-start.1
  3.6 0.9 copy-start.2
  5.7 10.1 %collective-permute-start = (bf16[784,128]{1,0:T(8,128)(2,1)S(1)}, bf16[784,128]{1,0:T(8,128)(2,1)S(1)}, u32[]{:S(2)}, u32[]{:S(2)}) collective-permute-start(bf16[784,128]{1,0:T(8,128)(2,1)S(1)} %pad_maximum_fusion.1), channel_id=1, source_target_pairs={{0,256},{256,0},{1,257},{257,1},{2,258},{258,2},{3,259},{259,3},{4... | collective-permute-start | bytes 602120 | tf_op jit(solution)/shard_map/ppermute | solution.py:420
  9.7 6.1 %collective-permute-start.9 = (bf16[256,256]{1,0:T(8,128)(2,1)}, bf16[256,256]{1,0:T(8,128)(2,1)S(1)}, u32[]{:S(2)}, u32[]{:S(2)}) collective-permute-start(bf16[256,256]{1,0:T(8,128)(2,1)} %param.10), channel_id=1, source_target_pairs={{0,1},{1,0},{2,3},{3,2},{4,5},{5,4},{6,7},{7,6},{8,9},{9,8},{10,11... | collective-permute-start | bytes 393224 | tf_op jit(solution)/shard_map/ppermute | solution.py:434
  15.9 32.8 %collective-permute-start.10 = (bf16[256,2560]{1,0:T(8,128)(2,1)S(1)}, bf16[256,2560]{1,0:T(8,128)(2,1)S(1)}, u32[]{:S(2)}, u32[]{:S(2)}) collective-permute-start(bf16[256,2560]{1,0:T(8,128)(2,1)S(1)} %pad_maximum_fusion.refs_0_.weight_ref), channel_id=1, source_target_pairs={{0,2},{2,4},{4,6},{6,0},{1,3},{3,5},{5,7},{7,1},{8,10},{10,12},{12... | collective-permute-start | bytes 3932168 | tf_op jit(solution)/shard_map/ppermute | solution.py:438
  19.4 37.5 %collective-permute-start.1 = (bf16[2,2,256,128]{3,2,1,0:T(8,128)(2,1)S(1)}, bf16[2,2,256,128]{3,2,1,0:T(8,128)(2,1)}, u32[]{:S(2)}, u32[]{:S(2)}) collective-permute-start(bf16[2,2,256,128]{3,2,1,0:T(8,128)(2,1)S(1)} %pair.1.refs_0_.refs_2_), channel_id=1, source_target_pairs={{0,64},{64,0},{1,65},{65,1},{2,66},{66,2},{3,67},{67,3},{4,68},{68... | collective-permute-start | bytes 786440 | tf_op jit(solution)/shard_map/ppermute | solution.py:425
  35.2 27.4 %collective-permute-start.5 = (bf16[2,2,256,128]{3,2,1,0:T(8,128)(2,1)S(1)}, bf16[2,2,256,128]{3,2,1,0:T(8,128)(2,1)S(1)}, u32[]{:S(2)}, u32[]{:S(2)}) collective-permute-start(bf16[2,2,256,128]{3,2,1,0:T(8,128)(2,1)S(1)} %pair.1.refs_0_.refs_2_), channel_id=1, source_target_pairs={{0,8},{8,16},{16,24},{24,32},{32,40},{40,48},{48,56},{64,72},{72,8... | collective-permute-start | bytes 786440 | tf_op jit(solution)/shard_map/ppermute | solution.py:372
  38.1 25.9 %collective-permute-start.6 = (bf16[2,2,256,128]{3,2,1,0:T(8,128)(2,1)S(1)}, bf16[2,2,256,128]{3,2,1,0:T(8,128)(2,1)}, u32[]{:S(2)}, u32[]{:S(2)}) collective-permute-start(bf16[2,2,256,128]{3,2,1,0:T(8,128)(2,1)S(1)} %pair.1.refs_0_.refs_2_), channel_id=1, source_target_pairs={{8,0},{16,8},{24,16},{32,24},{40,32},{48,40},{56,48},{72,64},{80,7... | collective-permute-start | bytes 786440 | tf_op jit(solution)/shard_map/ppermute | solution.py:372
  39.4 62.5 %collective-permute-start.12 = (bf16[256,2560]{1,0:T(8,128)(2,1)S(1)}, bf16[256,2560]{1,0:T(8,128)(2,1)}, u32[]{:S(2)}, u32[]{:S(2)}) collective-permute-start(bf16[256,2560]{1,0:T(8,128)(2,1)S(1)} %pad_maximum_fusion.refs_0_.weight_ref), channel_id=1, source_target_pairs={{0,6},{2,0},{4,2},{6,4},{1,7},{3,1},{5,3},{7,5},{8,14},{10,8},{12,... | collective-permute-start | bytes 3932168 | tf_op jit(solution)/shard_map/ppermute | solution.py:439
  48.7 53.2 %collective-permute-start.11 = (bf16[256,2560]{1,0:T(8,128)(2,1)S(1)}, bf16[256,2560]{1,0:T(8,128)(2,1)}, u32[]{:S(2)}, u32[]{:S(2)}) collective-permute-start(bf16[256,2560]{1,0:T(8,128)(2,1)S(1)} %collective-permute-done.10.refs_1_), channel_id=1, source_target_pairs={{0,2},{2,4},{4,6},{6,0},{1,3},{3,5},{5,7},{7,1},{8,10},{10,12},{12... | collective-permute-start | bytes 3932168 | tf_op jit(solution)/shard_map/ppermute | solution.py:440
  56.9 18.5 %collective-permute-start.7 = (bf16[2,2,256,128]{3,2,1,0:T(8,128)(2,1)}, bf16[2,2,256,128]{3,2,1,0:T(8,128)(2,1)S(1)}, u32[]{:S(2)}, u32[]{:S(2)}) collective-permute-start(bf16[2,2,256,128]{3,2,1,0:T(8,128)(2,1)} %collective-permute-done.1.refs_3_.refs_2_), channel_id=1, source_target_pairs={{0,8},{8,16},{16,24},{24,32},{32,40},{40,48},{48,56},{64,72},{72,8... | collective-permute-start | bytes 786440 | tf_op jit(solution)/shard_map/ppermute | solution.py:372
  62.6 8.5 %collective-permute-start.2 = (bf16[2,2,256,128]{3,2,1,0:T(8,128)(2,1)}, bf16[2,2,256,128]{3,2,1,0:T(8,128)(2,1)S(1)}, u32[]{:S(2)}, u32[]{:S(2)}) collective-permute-start(bf16[2,2,256,128]{3,2,1,0:T(8,128)(2,1)} %collective-permute-done.1.refs_3_.refs_2_), channel_id=1, source_target_pairs={{0,128},{192,64},{1,129},{193,65},{2,130},{194,66},{3,131},{195,67... | collective-permute-start | bytes 786440 | tf_op jit(solution)/shard_map/ppermute | solution.py:426
  64.0 12.7 %collective-permute-start.8 = (bf16[2,2,256,128]{3,2,1,0:T(8,128)(2,1)}, bf16[2,2,256,128]{3,2,1,0:T(8,128)(2,1)S(1)}, u32[]{:S(2)}, u32[]{:S(2)}) collective-permute-start(bf16[2,2,256,128]{3,2,1,0:T(8,128)(2,1)} %collective-permute-done.1.refs_3_.refs_2_), channel_id=1, source_target_pairs={{8,0},{16,8},{24,16},{32,24},{40,32},{48,40},{56,48},{72,64},{80,7... | collective-permute-start | bytes 786440 | tf_op jit(solution)/shard_map/ppermute | solution.py:372
  71.0 10.5 %collective-permute-start.3 = (bf16[2,2,256,128]{3,2,1,0:T(8,128)(2,1)S(1)}, bf16[2,2,256,128]{3,2,1,0:T(8,128)(2,1)S(1)}, u32[]{:S(2)}, u32[]{:S(2)}) collective-permute-start(bf16[2,2,256,128]{3,2,1,0:T(8,128)(2,1)S(1)} %collective-permute-done.2.refs_0_.refs_2_), channel_id=1, source_target_pairs={{64,72},{72,80},{80,88},{88,96},{96,104},{104,112},{112,120},{128,... | collective-permute-start | bytes 786440 | tf_op jit(solution)/shard_map/ppermute | solution.py:372
  75.4 8.3 %collective-permute-start.4 = (bf16[2,2,256,128]{3,2,1,0:T(8,128)(2,1)S(1)}, bf16[2,2,256,128]{3,2,1,0:T(8,128)(2,1)S(1)}, u32[]{:S(2)}, u32[]{:S(2)}) collective-permute-start(bf16[2,2,256,128]{3,2,1,0:T(8,128)(2,1)S(1)} %collective-permute-done.2.refs_0_.refs_2_), channel_id=1, source_target_pairs={{72,64},{80,72},{88,80},{96,88},{104,96},{112,104},{120,112},{136,... | collective-permute-start | bytes 786440 | tf_op jit(solution)/shard_map/ppermute | solution.py:372
  104.9 4.6 %collective-permute-start.13 = (bf16[256,2048]{1,0:T(8,128)(2,1)S(1)}, bf16[256,2048]{1,0:T(8,128)(2,1)S(1)}, u32[]{:S(2)}, u32[]{:S(2)}) collective-permute-start(bf16[256,2048]{1,0:T(8,128)(2,1)S(1)} %project.1.mine_ref), channel_id=1, source_target_pairs={{0,1},{1,0},{2,3},{3,2},{4,5},{5,4},{6,7},{7,6},{8,9},{9,8},{10,11... | collective-permute-start | bytes 3145736 | tf_op jit(solution)/shard_map/ppermute | solution.py:450
  111.8 7.7 %collective-permute-start.14 = (bf16[256,128]{1,0:T(8,128)(2,1)S(1)}, bf16[256,128]{1,0:T(8,128)(2,1)S(1)}, u32[]{:S(2)}, u32[]{:S(2)}) collective-permute-start(bf16[256,128]{1,0:T(8,128)(2,1)S(1)} %get-tuple-element.50), channel_id=1, source_target_pairs={{0,256},{256,0},{1,257},{257,1},{2,258},{258,2},{3,259},{259,3},{4... | collective-permute-start | bytes 196616 | tf_op jit(solution)/shard_map/ppermute | solution.py:452
  121.8 15.2 %collective-permute-start.17 = (bf16[2,2,256,128]{3,2,1,0:T(8,128)(2,1)S(1)}, bf16[2,2,256,128]{3,2,1,0:T(8,128)(2,1)S(1)}, u32[]{:S(2)}, u32[]{:S(2)}) collective-permute-start(bf16[2,2,256,128]{3,2,1,0:T(8,128)(2,1)S(1)} %get-tuple-element.63), channel_id=1, source_target_pairs={{72,64},{80,72},{88,80},{96,88},{104,96},{112,104},{120,112},{136,... | collective-permute-start | bytes 786440 | tf_op jit(solution)/shard_map/ppermute | solution.py:372
  123.1 13.9 %collective-permute-start.18 = (bf16[2,2,256,128]{3,2,1,0:T(8,128)(2,1)S(1)}, bf16[2,2,256,128]{3,2,1,0:T(8,128)(2,1)S(1)}, u32[]{:S(2)}, u32[]{:S(2)}) collective-permute-start(bf16[2,2,256,128]{3,2,1,0:T(8,128)(2,1)S(1)} %get-tuple-element.64), channel_id=1, source_target_pairs={{64,72},{72,80},{80,88},{88,96},{96,104},{104,112},{112,120},{128,... | collective-permute-start | bytes 786440 | tf_op jit(solution)/shard_map/ppermute | solution.py:372
  131.0 9.3 %collective-permute-start.15 = (bf16[2,2,256,128]{3,2,1,0:T(8,128)(2,1)S(1)}, bf16[2,2,256,128]{3,2,1,0:T(8,128)(2,1)S(1)}, u32[]{:S(2)}, u32[]{:S(2)}) collective-permute-start(bf16[2,2,256,128]{3,2,1,0:T(8,128)(2,1)S(1)} %get-tuple-element.60), channel_id=1, source_target_pairs={{8,0},{16,8},{24,16},{32,24},{40,32},{48,40},{56,48},{72,64},{80,7... | collective-permute-start | bytes 786440 | tf_op jit(solution)/shard_map/ppermute | solution.py:372
  132.3 9.2 %collective-permute-start.16 = (bf16[2,2,256,128]{3,2,1,0:T(8,128)(2,1)S(1)}, bf16[2,2,256,128]{3,2,1,0:T(8,128)(2,1)S(1)}, u32[]{:S(2)}, u32[]{:S(2)}) collective-permute-start(bf16[2,2,256,128]{3,2,1,0:T(8,128)(2,1)S(1)} %get-tuple-element.61), channel_id=1, source_target_pairs={{0,8},{8,16},{16,24},{24,32},{32,40},{40,48},{48,56},{64,72},{72,8... | collective-permute-start | bytes 786440 | tf_op jit(solution)/shard_map/ppermute | solution.py:372
  137.2 5.7 %collective-permute-start.19 = (bf16[2,2,256,128]{3,2,1,0:T(8,128)(2,1)S(1)}, bf16[2,2,256,128]{3,2,1,0:T(8,128)(2,1)S(1)}, u32[]{:S(2)}, u32[]{:S(2)}) collective-permute-start(bf16[2,2,256,128]{3,2,1,0:T(8,128)(2,1)S(1)} %far_sum.1), channel_id=1, source_target_pairs={{128,0},{64,192},{129,1},{65,193},{130,2},{66,194},{131,3},{67,195... | collective-permute-start | bytes 786440 | tf_op jit(solution)/shard_map/ppermute | solution.py:465
  143.0 25.2 %collective-permute-start.22 = (bf16[2,2,256,128]{3,2,1,0:T(8,128)(2,1)S(1)}, bf16[2,2,256,128]{3,2,1,0:T(8,128)(2,1)S(1)}, u32[]{:S(2)}, u32[]{:S(2)}) collective-permute-start(bf16[2,2,256,128]{3,2,1,0:T(8,128)(2,1)S(1)} %merge.1), channel_id=1, source_target_pairs={{0,64},{64,0},{1,65},{65,1},{2,66},{66,2},{3,67},{67,3},{4,68},{68... | collective-permute-start | bytes 786440 | tf_op jit(solution)/shard_map/ppermute | solution.py:474
  156.5 23.6 %collective-permute-start.20 = (bf16[2,2,256,128]{3,2,1,0:T(8,128)(2,1)S(1)}, bf16[2,2,256,128]{3,2,1,0:T(8,128)(2,1)S(1)}, u32[]{:S(2)}, u32[]{:S(2)}) collective-permute-start(bf16[2,2,256,128]{3,2,1,0:T(8,128)(2,1)S(1)} %get-tuple-element.68), channel_id=1, source_target_pairs={{8,0},{16,8},{24,16},{32,24},{40,32},{48,40},{56,48},{72,64},{80,7... | collective-permute-start | bytes 786440 | tf_op jit(solution)/shard_map/ppermute | solution.py:372
  157.8 22.3 %collective-permute-start.21 = (bf16[2,2,256,128]{3,2,1,0:T(8,128)(2,1)S(1)}, bf16[2,2,256,128]{3,2,1,0:T(8,128)(2,1)S(1)}, u32[]{:S(2)}, u32[]{:S(2)}) collective-permute-start(bf16[2,2,256,128]{3,2,1,0:T(8,128)(2,1)S(1)} %get-tuple-element.69), channel_id=1, source_target_pairs={{0,8},{8,16},{16,24},{24,32},{32,40},{40,48},{48,56},{64,72},{72,8... | collective-permute-start | bytes 786440 | tf_op jit(solution)/shard_map/ppermute | solution.py:372
  180.2 10.2 %collective-permute-start.23 = (bf16[3,256,128]{2,1,0:T(8,128)(2,1)S(1)}, bf16[3,256,128]{2,1,0:T(8,128)(2,1)S(1)}, u32[]{:S(2)}, u32[]{:S(2)}) collective-permute-start(bf16[3,256,128]{2,1,0:T(8,128)(2,1)S(1)} %frame_sum.1), channel_id=1, source_target_pairs={{0,256},{256,0},{1,257},{257,1},{2,258},{258,2},{3,259},{259,3},{4... | collective-permute-start | bytes 589832 | tf_op jit(solution)/shard_map/ppermute | solution.py:481

commit v5 on v4

--- a/solution.py
+++ b/solution.py
@@ -362,13 +362,12 @@
     )(place, mine, other, packs[0], *packs)
 
 
-def column_shift(value, step, lines):
-    pairs = [
-        (line * TW + col, line * TW + col + step)
-        for line in lines
-        for col in range(TW)
-        if 0 <= col + step < TW
-    ]
+def column_swap(value, turn, lines):
+    pairs = []
+    for line in lines:
+        for col in range(turn, TW - 1, 2):
+            here = line * TW + col
+            pairs += [(here, here + 1), (here + 1, here)]
     return lax.ppermute(value, ("xr", "zr", "zc"), pairs)
 
 
@@ -378,18 +377,18 @@
 
 
 def slot_tiles(frame, xr, zr, zc):
+    toward = 1 - 2 * (zc % 2)
     tiles = []
     for row, live in ((2 * xr + zr, True), (2 * xr + 1 - zr, True), (2 - xr, xr != zr)):
-        for step in (0, -1, 1):
-            col = zc + step
+        for col in (zc, zc + toward, zc - toward):
             inside = (col >= 0) & (col < TW) & live
             for f in (frame, 1 - frame):
                 tiles.append(jnp.where(inside, f * 32 + row * TW + col, -2))
     return jnp.stack(tiles)
 
 
-def beside(value, lines):
-    return column_shift(value, 1, lines), column_shift(value, -1, lines)
+def swapped(first, second, lines):
+    return column_swap(first, 0, lines), column_swap(second, 1, lines)
 
 
 def from_rows(value):
@@ -424,9 +423,9 @@
     pair = simple(pair_kernel, "pair", [shape(2, 2, TILE, HD)], kv_mine, xf_got)[0]
     row = lax.ppermute(pair, "zr", SWAP)
     third = lax.ppermute(row, ("xr", "zr"), [(0, 2), (3, 1)])
-    own_windows = (pair, *beside(pair, ALL_LINES))
-    row_windows = (row, *beside(row, ALL_LINES))
-    third_windows = (third, *beside(third, MIDDLE_LINES))
+    own_windows = (pair, *swapped(pair, pair, ALL_LINES))
+    row_windows = (row, *swapped(row, row, ALL_LINES))
+    third_windows = (third, *swapped(third, third, MIDDLE_LINES))
 
     weight_heads = out_weight.reshape(2, HD, 8 * TILE)
     first_head = jnp.where(xf == 0, weight_heads[0], weight_heads[1])
@@ -456,11 +455,8 @@
     before = jnp.zeros((2, HD, TILE), jnp.float32)
     before, far, far_left, far_right = backward(common_third, before, third_weights, third_windows)
     before, part, part_left, part_right = backward(common, before, row_weights, row_windows)
-    def returned(left, right, lines):
-        return column_shift(left, -1, lines), column_shift(right, 1, lines)
-
     far_sum = simple(
-        far_kernel, "far_sum", [shape(2, 2, TILE, HD)], far, *returned(far_left, far_right, MIDDLE_LINES)
+        far_kernel, "far_sum", [shape(2, 2, TILE, HD)], far, *swapped(far_left, far_right, MIDDLE_LINES)
     )[0]
     third_back = lax.ppermute(far_sum, ("xr", "zr"), [(2, 0), (1, 3)])
     row_sum = simple(
@@ -468,14 +464,14 @@
         "merge",
         [shape(2, 2, TILE, HD)],
         part,
-        *returned(part_left, part_right, ALL_LINES),
+        *swapped(part_left, part_right, ALL_LINES),
         third_back,
     )[0]
     row_back = lax.ppermute(row_sum, "zr", SWAP)
     row_back = simple(widen_kernel, "widen", [shape(2, 2, TILE, HD, dtype=jnp.float32)], row_back, flops=30_000_000_000)[0]
     before, _ = lax.optimization_barrier((before, row_sum))
     grad_query, near, near_left, near_right = backward(common, before, own_weights, own_windows, last=True)
-    from_right, from_left = returned(near_left, near_right, ALL_LINES)
+    from_right, from_left = swapped(near_left, near_right, ALL_LINES)
     sums = (near, from_right, from_left, row_back, grad_query)
     frame_sum = simple(frame_kernel, "frame_sum", [shape(3, TILE, HD)], *sums)[0]
     xf_back = lax.ppermute(frame_sum, "xf", SWAP)

time: 193 us -> 194 us (level)
  the two profiles are of different devices: /device:TPU:2 before, /device:TPU:34 now
where the time goes in v5:
time: 194 us; the launch traced here: 193 us
  starting transfers between devices  86.4 us (45%)
  waiting for transfers between devices  60.2 us (31%)
  Pallas kernels  24 us (12%)
  blocking collectives  15.7 us (8%)
  local copies, waits for them, and re-layouts  3.62 us (2%)
    ppermute x12, starting transfers between devices, column_swap(): return lax.ppermute(value, ('xr', 'zr', 'zc'), pairs)  38.1 us
    all_to_all x1, blocking collectives, body(): lax.all_to_all(spread.reshape(8, TILE, HD), ('xf', 'y'), 0, 0, tiled=True)  15.7 us
    ppermute x1, waiting for transfers between devices, body(): row_back = lax.ppermute(row_sum, 'zr', SWAP)  15.4 us
    ppermute x1, starting transfers between devices, body(): row = lax.ppermute(pair, 'zr', SWAP)  14.8 us
    ppermute x12, waiting for transfers between devices, column_swap(): return lax.ppermute(value, ('xr', 'zr', 'zc'), pairs)  11.7 us
    ppermute x1, starting transfers between devices, body(): row_back = lax.ppermute(row_sum, 'zr', SWAP)  9.37 us
    pallas_call x3, Pallas kernels, backward(): pl.pallas_call(functools.partial(backward_kernel, len(windows), last), ou...  8.53 us
    ppermute x1, waiting for transfers between devices, body(): xf_back = lax.ppermute(frame_sum, 'xf', SWAP)  8.2 us
  transfers between devices with their start and end apart: 24, of which 15 were waited for; matrix products, arithmetic and copies ran while one was open for 1% of the time, Pallas kernels for 7%

profile of v5, /device:TPU:34, one launch (start us, length us, event | category | flops | bytes accessed | tf_op | source)
XLA Modules:
  0.0 192.9 jit_solution(18253873685396398045)
XLA Ops:
  5.7 4.0 %collective-permute-start = (bf16[784,128]{1,0:T(8,128)(2,1)S(1)}, bf16[784,128]{1,0:T(8,128)(2,1)S(1)}, u32[]{:S(2)}, u32[]{:S(2)}) collective-permute-start(bf16[784,128]{1,0:T(8,128)(2,1)S(1)} %pad_maximum_fusion.1), channel_id=1, source_target_pairs={{0,256},{256,0},{1,257},{257,1},{2,258},{258,2},{3,259},{259,3},{4... | collective-permute-start | bytes 602120 | tf_op jit(solution)/shard_map/ppermute | solution.py:419
  12.9 2.9 %collective-permute-done.frame_ref = bf16[784,128]{1,0:T(8,128)(2,1)S(1)} collective-permute-done((bf16[784,128]{1,0:T(8,128)(2,1)S(1)}, bf16[784,128]{1,0:T(8,128)(2,1)S(1)}, u32[]{:S(2)}, u32[]{:S(2)}) %collective-permute-start) | collective-permute-done | bytes 200736 | tf_op jit(solution)/shard_map/ppermute | solution.py:419
  15.9 3.5 %collective-permute-start.10 = (bf16[256,2560]{1,0:T(8,128)(2,1)S(1)}, bf16[256,2560]{1,0:T(8,128)(2,1)S(1)}, u32[]{:S(2)}, u32[]{:S(2)}) collective-permute-start(bf16[256,2560]{1,0:T(8,128)(2,1)S(1)} %pad_maximum_fusion.refs_0_.weight_ref), channel_id=1, source_target_pairs={{0,2},{2,4},{4,6},{6,0},{1,3},{3,5},{5,7},{7,1},{8,10},{10,12},{12... | collective-permute-start | bytes 3932168 | tf_op jit(solution)/shard_map/ppermute | solution.py:437
  19.5 14.8 %collective-permute-start.1 = (bf16[2,2,256,128]{3,2,1,0:T(8,128)(2,1)S(1)}, bf16[2,2,256,128]{3,2,1,0:T(8,128)(2,1)}, u32[]{:S(2)}, u32[]{:S(2)}) collective-permute-start(bf16[2,2,256,128]{3,2,1,0:T(8,128)(2,1)S(1)} %pair.1.refs_0_.refs_2_), channel_id=1, source_target_pairs={{0,64},{64,0},{1,65},{65,1},{2,66},{66,2},{3,67},{67,3},{4,68},{68... | collective-permute-start | bytes 786440 | tf_op jit(solution)/shard_map/ppermute | solution.py:424
  34.3 2.9 %collective-permute-start.5 = (bf16[2,2,256,128]{3,2,1,0:T(8,128)(2,1)S(1)}, bf16[2,2,256,128]{3,2,1,0:T(8,128)(2,1)S(1)}, u32[]{:S(2)}, u32[]{:S(2)}) collective-permute-start(bf16[2,2,256,128]{3,2,1,0:T(8,128)(2,1)S(1)} %pair.1.refs_0_.refs_2_), channel_id=1, source_target_pairs={{0,8},{8,0},{16,24},{24,16},{32,40},{40,32},{48,56},{56,48},{64,72... | collective-permute-start | bytes 786440 | tf_op jit(solution)/shard_map/ppermute | solution.py:371
  37.2 2.9 %collective-permute-start.6 = (bf16[2,2,256,128]{3,2,1,0:T(8,128)(2,1)S(1)}, bf16[2,2,256,128]{3,2,1,0:T(8,128)(2,1)}, u32[]{:S(2)}, u32[]{:S(2)}) collective-permute-start(bf16[2,2,256,128]{3,2,1,0:T(8,128)(2,1)S(1)} %pair.1.refs_0_.refs_2_), channel_id=1, source_target_pairs={{8,16},{16,8},{24,32},{32,24},{40,48},{48,40},{72,80},{80,72},{88,... | collective-permute-start | bytes 786440 | tf_op jit(solution)/shard_map/ppermute | solution.py:371
  40.2 3.6 %collective-permute-start.12 = (bf16[256,2560]{1,0:T(8,128)(2,1)S(1)}, bf16[256,2560]{1,0:T(8,128)(2,1)}, u32[]{:S(2)}, u32[]{:S(2)}) collective-permute-start(bf16[256,2560]{1,0:T(8,128)(2,1)S(1)} %pad_maximum_fusion.refs_0_.weight_ref), channel_id=1, source_target_pairs={{0,6},{2,0},{4,2},{6,4},{1,7},{3,1},{5,3},{7,5},{8,14},{10,8},{12,... | collective-permute-start | bytes 3932168 | tf_op jit(solution)/shard_map/ppermute | solution.py:438
  43.7 5.0 %collective-permute-done.10.refs_1_ = bf16[256,2560]{1,0:T(8,128)(2,1)S(1)} collective-permute-done((bf16[256,2560]{1,0:T(8,128)(2,1)S(1)}, bf16[256,2560]{1,0:T(8,128)(2,1)S(1)}, u32[]{:S(2)}, u32[]{:S(2)}) %collective-permute-start.10) | collective-permute-done | bytes 1310752 | tf_op jit(solution)/shard_map/ppermute | solution.py:437
  51.1 5.3 %collective-permute-done.1.refs_3_.refs_2_ = bf16[2,2,256,128]{3,2,1,0:T(8,128)(2,1)} collective-permute-done((bf16[2,2,256,128]{3,2,1,0:T(8,128)(2,1)S(1)}, bf16[2,2,256,128]{3,2,1,0:T(8,128)(2,1)}, u32[]{:S(2)}, u32[]{:S(2)}) %collective-permute-start.1) | collective-permute-done | bytes 262176 | tf_op jit(solution)/shard_map/ppermute | solution.py:424
  56.4 2.6 %collective-permute-start.7 = (bf16[2,2,256,128]{3,2,1,0:T(8,128)(2,1)}, bf16[2,2,256,128]{3,2,1,0:T(8,128)(2,1)S(1)}, u32[]{:S(2)}, u32[]{:S(2)}) collective-permute-start(bf16[2,2,256,128]{3,2,1,0:T(8,128)(2,1)} %collective-permute-done.1.refs_3_.refs_2_), channel_id=1, source_target_pairs={{0,8},{8,0},{16,24},{24,16},{32,40},{40,32},{48,56},{56,48},{64,72... | collective-permute-start | bytes 786440 | tf_op jit(solution)/shard_map/ppermute | solution.py:371
  58.9 4.2 %collective-permute-done.5.refs_1_.refs_3_ = bf16[2,2,256,128]{3,2,1,0:T(8,128)(2,1)S(1)} collective-permute-done((bf16[2,2,256,128]{3,2,1,0:T(8,128)(2,1)S(1)}, bf16[2,2,256,128]{3,2,1,0:T(8,128)(2,1)S(1)}, u32[]{:S(2)}, u32[]{:S(2)}) %collective-permute-start.5) | collective-permute-done | bytes 262176 | tf_op jit(solution)/shard_map/ppermute | solution.py:371
  64.6 3.7 %collective-permute-start.8 = (bf16[2,2,256,128]{3,2,1,0:T(8,128)(2,1)}, bf16[2,2,256,128]{3,2,1,0:T(8,128)(2,1)S(1)}, u32[]{:S(2)}, u32[]{:S(2)}) collective-permute-start(bf16[2,2,256,128]{3,2,1,0:T(8,128)(2,1)} %collective-permute-done.1.refs_3_.refs_2_), channel_id=1, source_target_pairs={{8,16},{16,8},{24,32},{32,24},{40,48},{48,40},{72,80},{80,72},{88,... | collective-permute-start | bytes 786440 | tf_op jit(solution)/shard_map/ppermute | solution.py:371
  68.3 3.2 %collective-permute-done.2.refs_0_.refs_2_ = bf16[2,2,256,128]{3,2,1,0:T(8,128)(2,1)S(1)} collective-permute-done((bf16[2,2,256,128]{3,2,1,0:T(8,128)(2,1)}, bf16[2,2,256,128]{3,2,1,0:T(8,128)(2,1)S(1)}, u32[]{:S(2)}, u32[]{:S(2)}) %collective-permute-start.2) | collective-permute-done | bytes 262176 | tf_op jit(solution)/shard_map/ppermute | solution.py:425
  71.6 3.5 %collective-permute-start.3 = (bf16[2,2,256,128]{3,2,1,0:T(8,128)(2,1)S(1)}, bf16[2,2,256,128]{3,2,1,0:T(8,128)(2,1)S(1)}, u32[]{:S(2)}, u32[]{:S(2)}) collective-permute-start(bf16[2,2,256,128]{3,2,1,0:T(8,128)(2,1)S(1)} %collective-permute-done.2.refs_0_.refs_2_), channel_id=1, source_target_pairs={{64,72},{72,64},{80,88},{88,80},{96,104},{104,96},{112,120},{120,1... | collective-permute-start | bytes 786440 | tf_op jit(solution)/shard_map/ppermute | solution.py:371
  77.4 4.7 %attend.2 = (bf16[2,6,256,256]{3,2,1,0:T(8,128)(2,1)S(1)}, bf16[2,6,256,256]{3,2,1,0:T(8,128)(2,1)S(1)}, f32[8,512]{1,0:T(8,128)S(1)}, f32[8,512]{1,0:T(8,128)S(1)}, f32[2,128,256]{2,1,0:T(8,128)S(1)}) custom-call(s32[2,19]{1,0:T(2,128)S(1)} %concatenate.13.allowed_ref, bf16[256,128]{1,0:T(8,128)(2,1)S(1)} %get-tuple-element.41.q_mine_ref, ...), custom_call_target="tpu_custom_call" | custom-call | flops 2000000000 | bytes 5400000 | tf_op jit(solution)/shard_map/attend/pallas_call | solution.py:291
  83.4 2.5 %attend.3 = (bf16[2,6,256,256]{3,2,1,0:T(8,128)(2,1)S(1)}, bf16[256,128]{1,0:T(8,128)(2,1)S(1)}, bf16[256,128]{1,0:T(8,128)(2,1)S(1)}, bf16[2,4,256,128]{3,2,1,0...) custom-call(s32[2,19]{1,0:T(2,128)S(1)} %concatenate.13.allowed_ref, ...), custom_call_target="tpu_custom_call" | custom-call | flops 1000000000 | bytes 2700000 | tf_op jit(solution)/shard_map/attend/pallas_call | solution.py:291
  85.9 15.7 %all_to_all.5 = bf16[8,256,128]{2,1,0:T(8,128)(2,1)S(1)} all-to-all(bf16[8,256,128]{2,1,0:T(8,128)(2,1)S(1)} %bitcast.30), channel_id=1, replica_groups=mesh['xf'=2,'xr'=2,'zr'=2,'zc'=8,'y'=4,'core'=2] {'xf','y'}, dimensions={0} | all-to-all | bytes 1048576 | tf_op jit(solution)/shard_map/all_to_all | solution.py:447
  101.6 3.0 %project.1.mine_ref = bf16[256,2048]{1,0:T(8,128)(2,1)S(1)} custom-call(s32[3]{0:T(128)S(1)} %pad_add_fusion.place_ref, bf16[2,4,256,128]{3,2,1,0:T(8,128)(2,1)S(1)} %bitcast.29, bf16[256,2560]{1,0:T(8,128)(2,1)S(1)} %pad_maximum_fusion.refs_0_.weight_ref, bf16[256,2560]{1,0:T(8,128)(2,1)S(1)} %collective-permute-done.10.refs_1_, ...), custom_call_target="tpu_custom_call" | custom-call | flops 1100000000 | bytes 6000000 | tf_op jit(solution)/shard_map/project/pallas_call | solution.py:337
  106.6 2.6 %collective-permute-done.13.other_ref = bf16[256,2048]{1,0:T(8,128)(2,1)S(1)} collective-permute-done((bf16[256,2048]{1,0:T(8,128)(2,1)S(1)}, bf16[256,2048]{1,0:T(8,128)(2,1)S(1)}, u32[]{:S(2)}, u32[]{:S(2)}) %collective-permute-start.13) | collective-permute-done | bytes 1048608 | tf_op jit(solution)/shard_map/ppermute | solution.py:449
  109.2 2.4 %residue.1 = (bf16[256,256]{1,0:T(8,128)(2,1)}, bf16[256,128]{1,0:T(8,128)(2,1)S(1)}, bf16[256,128]{1,0:T(8,128)(2,1)S(1)}) custom-call(s32[3]{0:T(128)S(1)} %pad_add_fusion.place_ref, bf16[256,2048]{1,0:T(8,128)(2,1)S(1)} %project.1.mine_ref, bf16[256,2048]{1,0:T(8,128)(2,1)S(1)} %collective-permute-done.13.other_ref, ...), custom_call_target="tpu_custom_call" | custom-call | flops 300000000 | bytes 5000000 | tf_op jit(solution)/shard_map/residue/pallas_call | solution.py:350
  111.6 2.5 %collective-permute-start.14 = (bf16[256,128]{1,0:T(8,128)(2,1)S(1)}, bf16[256,128]{1,0:T(8,128)(2,1)S(1)}, u32[]{:S(2)}, u32[]{:S(2)}) collective-permute-start(bf16[256,128]{1,0:T(8,128)(2,1)S(1)} %get-tuple-element.50), channel_id=1, source_target_pairs={{0,256},{256,0},{1,257},{257,1},{2,258},{258,2},{3,259},{259,3},{4... | collective-permute-start | bytes 196616 | tf_op jit(solution)/shard_map/ppermute | solution.py:451
  114.1 5.1 %collective-permute-done.14.grad_got_ref = bf16[256,128]{1,0:T(8,128)(2,1)S(1)} collective-permute-done((bf16[256,128]{1,0:T(8,128)(2,1)S(1)}, bf16[256,128]{1,0:T(8,128)(2,1)S(1)}, u32[]{:S(2)}, u32[]{:S(2)}) %collective-permute-start.14) | collective-permute-done | bytes 65568 | tf_op jit(solution)/shard_map/ppermute | solution.py:451
  119.2 2.3 %attend_back.3 = (f32[2,128,256]{2,1,0:T(8,128)S(1)}, bf16[2,2,256,128]{3,2,1,0:T(8,128)(2,1)S(1)}, bf16[2,2,256,128]{3,2,1,0:T(8,128)(2,1)S(1)}, bf16[2,2,256,128]{3,2,1,0:T(8,128)(2,1)S(1)}) custom-call(bf16[256,128]{1,0:T(8,128)(2,1)S(1)} %get-tuple-element.41.q_mine_ref, bf16[784,128]{1,0:T(8,128)(2,1)S(1)} %collective-permute-done.frame_ref, ...), custom_call_target="tpu_custom_call" | custom-call | flops 805306368 | bytes 3600000 | tf_op jit(solution)/shard_map/attend_back/pallas_call | solution.py:318
  123.5 5.5 %collective-permute-start.18 = (bf16[2,2,256,128]{3,2,1,0:T(8,128)(2,1)S(1)}, bf16[2,2,256,128]{3,2,1,0:T(8,128)(2,1)S(1)}, u32[]{:S(2)}, u32[]{:S(2)}) collective-permute-start(bf16[2,2,256,128]{3,2,1,0:T(8,128)(2,1)S(1)} %get-tuple-element.64), channel_id=1, source_target_pairs={{72,80},{80,72},{88,96},{96,88},{104,112},{112,104},{136,144},{144... | collective-permute-start | bytes 786440 | tf_op jit(solution)/shard_map/ppermute | solution.py:371
  129.0 3.1 %attend_back.4 = (f32[2,128,256]{2,1,0:T(8,128)S(1)}, bf16[2,2,256,128]{3,2,1,0:T(8,128)(2,1)S(1)}, bf16[2,2,256,128]{3,2,1,0:T(8,128)(2,1)S(1)}, bf16[2,2,256,128]{3,2,1,0:T(8,128)(2,1)S(1)}) custom-call(bf16[256,128]{1,0:T(8,128)(2,1)S(1)} %get-tuple-element.41.q_mine_ref, bf16[784,128]{1,0:T(8,128)(2,1)S(1)} %collective-permute-done.frame_ref, ...), custom_call_target="tpu_custom_call" | custom-call | flops 805306368 | bytes 3600000 | tf_op jit(solution)/shard_map/attend_back/pallas_call | solution.py:318
  134.0 4.0 %collective-permute-start.16 = (bf16[2,2,256,128]{3,2,1,0:T(8,128)(2,1)S(1)}, bf16[2,2,256,128]{3,2,1,0:T(8,128)(2,1)S(1)}, u32[]{:S(2)}, u32[]{:S(2)}) collective-permute-start(bf16[2,2,256,128]{3,2,1,0:T(8,128)(2,1)S(1)} %get-tuple-element.61), channel_id=1, source_target_pairs={{8,16},{16,8},{24,32},{32,24},{40,48},{48,40},{72,80},{80,72},{88,... | collective-permute-start | bytes 786440 | tf_op jit(solution)/shard_map/ppermute | solution.py:371
  140.6 2.3 %collective-permute-done.16.left_ref = bf16[2,2,256,128]{3,2,1,0:T(8,128)(2,1)S(1)} collective-permute-done((bf16[2,2,256,128]{3,2,1,0:T(8,128)(2,1)S(1)}, bf16[2,2,256,128]{3,2,1,0:T(8,128)(2,1)S(1)}, u32[]{:S(2)}, u32[]{:S(2)}) %collective-permute-start.16) | collective-permute-done | bytes 262176 | tf_op jit(solution)/shard_map/ppermute | solution.py:371
  143.7 9.4 %collective-permute-start.22 = (bf16[2,2,256,128]{3,2,1,0:T(8,128)(2,1)S(1)}, bf16[2,2,256,128]{3,2,1,0:T(8,128)(2,1)S(1)}, u32[]{:S(2)}, u32[]{:S(2)}) collective-permute-start(bf16[2,2,256,128]{3,2,1,0:T(8,128)(2,1)S(1)} %merge.1), channel_id=1, source_target_pairs={{0,64},{64,0},{1,65},{65,1},{2,66},{66,2},{3,67},{67,3},{4,68},{68... | collective-permute-start | bytes 786440 | tf_op jit(solution)/shard_map/ppermute | solution.py:470
  153.0 3.2 %attend_back.5 = (bf16[2,256,128]{2,1,0:T(8,128)(2,1)S(1)}, bf16[2,2,256,128]{3,2,1,0:T(8,128)(2,1)S(1)}, bf16[2,2,256,128]{3,2,1,0:T(8,128)(2,1)S(1)}, bf16[2,2,256,128]{3,2,1,0:T(8,128)(2,1)S(1)}) custom-call(bf16[256,128]{1,0:T(8,128)(2,1)S(1)} %get-tuple-element.41.q_mine_ref, bf16[784,128]{1,0:T(8,128)(2,1)S(1)} %collective-permute-done.frame_ref, ...), custom_call_target="tpu_custom_call" | custom-call | flops 805306368 | bytes 3600000 | tf_op jit(solution)/shard_map/attend_back/pallas_call | solution.py:318
  158.4 4.7 %collective-permute-start.21 = (bf16[2,2,256,128]{3,2,1,0:T(8,128)(2,1)S(1)}, bf16[2,2,256,128]{3,2,1,0:T(8,128)(2,1)S(1)}, u32[]{:S(2)}, u32[]{:S(2)}) collective-permute-start(bf16[2,2,256,128]{3,2,1,0:T(8,128)(2,1)S(1)} %get-tuple-element.69), channel_id=1, source_target_pairs={{8,16},{16,8},{24,32},{32,24},{40,48},{48,40},{72,80},{80,72},{88,... | collective-permute-start | bytes 786440 | tf_op jit(solution)/shard_map/ppermute | solution.py:371
  163.1 15.4 %collective-permute-done.22.part_ref = bf16[2,2,256,128]{3,2,1,0:T(8,128)(2,1)S(1)} collective-permute-done((bf16[2,2,256,128]{3,2,1,0:T(8,128)(2,1)S(1)}, bf16[2,2,256,128]{3,2,1,0:T(8,128)(2,1)S(1)}, u32[]{:S(2)}, u32[]{:S(2)}) %collective-permute-start.22) | collective-permute-done | bytes 262176 | tf_op jit(solution)/shard_map/ppermute | solution.py:470
  183.3 8.2 %collective-permute-done.23.frame_ref = bf16[3,256,128]{2,1,0:T(8,128)(2,1)S(1)} collective-permute-done((bf16[3,256,128]{2,1,0:T(8,128)(2,1)S(1)}, bf16[3,256,128]{2,1,0:T(8,128)(2,1)S(1)}, u32[]{:S(2)}, u32[]{:S(2)}) %collective-permute-start.23) | collective-permute-done | bytes 196640 | tf_op jit(solution)/shard_map/ppermute | solution.py:477
  (54 shorter events, 33.1 us)
Async XLA Ops:
  0.6 15.2 %copy-start.3 = (bf16[256,256]{1,0:T(8,128)(2,1)S(1)}, bf16[256,256]{1,0:T(8,128)(2,1)}, u32[]{:S(2)}) copy-start(bf16[256,256]{1,0:T(8,128)(2,1)} %param.10) | copy-start | bytes 393220
  1.8 0.9 copy-start
  2.7 0.9 copy-start.1
  3.6 0.9 copy-start.2
  5.7 10.1 %collective-permute-start = (bf16[784,128]{1,0:T(8,128)(2,1)S(1)}, bf16[784,128]{1,0:T(8,128)(2,1)S(1)}, u32[]{:S(2)}, u32[]{:S(2)}) collective-permute-start(bf16[784,128]{1,0:T(8,128)(2,1)S(1)} %pad_maximum_fusion.1), channel_id=1, source_target_pairs={{0,256},{256,0},{1,257},{257,1},{2,258},{258,2},{3,259},{259,3},{4... | collective-permute-start | bytes 602120 | tf_op jit(solution)/shard_map/ppermute | solution.py:419
  9.7 6.1 %collective-permute-start.9 = (bf16[256,256]{1,0:T(8,128)(2,1)}, bf16[256,256]{1,0:T(8,128)(2,1)S(1)}, u32[]{:S(2)}, u32[]{:S(2)}) collective-permute-start(bf16[256,256]{1,0:T(8,128)(2,1)} %param.10), channel_id=1, source_target_pairs={{0,1},{1,0},{2,3},{3,2},{4,5},{5,4},{6,7},{7,6},{8,9},{9,8},{10,11... | collective-permute-start | bytes 393224 | tf_op jit(solution)/shard_map/ppermute | solution.py:433
  15.9 32.8 %collective-permute-start.10 = (bf16[256,2560]{1,0:T(8,128)(2,1)S(1)}, bf16[256,2560]{1,0:T(8,128)(2,1)S(1)}, u32[]{:S(2)}, u32[]{:S(2)}) collective-permute-start(bf16[256,2560]{1,0:T(8,128)(2,1)S(1)} %pad_maximum_fusion.refs_0_.weight_ref), channel_id=1, source_target_pairs={{0,2},{2,4},{4,6},{6,0},{1,3},{3,5},{5,7},{7,1},{8,10},{10,12},{12... | collective-permute-start | bytes 3932168 | tf_op jit(solution)/shard_map/ppermute | solution.py:437
  19.5 36.9 %collective-permute-start.1 = (bf16[2,2,256,128]{3,2,1,0:T(8,128)(2,1)S(1)}, bf16[2,2,256,128]{3,2,1,0:T(8,128)(2,1)}, u32[]{:S(2)}, u32[]{:S(2)}) collective-permute-start(bf16[2,2,256,128]{3,2,1,0:T(8,128)(2,1)S(1)} %pair.1.refs_0_.refs_2_), channel_id=1, source_target_pairs={{0,64},{64,0},{1,65},{65,1},{2,66},{66,2},{3,67},{67,3},{4,68},{68... | collective-permute-start | bytes 786440 | tf_op jit(solution)/shard_map/ppermute | solution.py:424
  34.3 28.8 %collective-permute-start.5 = (bf16[2,2,256,128]{3,2,1,0:T(8,128)(2,1)S(1)}, bf16[2,2,256,128]{3,2,1,0:T(8,128)(2,1)S(1)}, u32[]{:S(2)}, u32[]{:S(2)}) collective-permute-start(bf16[2,2,256,128]{3,2,1,0:T(8,128)(2,1)S(1)} %pair.1.refs_0_.refs_2_), channel_id=1, source_target_pairs={{0,8},{8,0},{16,24},{24,16},{32,40},{40,32},{48,56},{56,48},{64,72... | collective-permute-start | bytes 786440 | tf_op jit(solution)/shard_map/ppermute | solution.py:371
  37.2 27.4 %collective-permute-start.6 = (bf16[2,2,256,128]{3,2,1,0:T(8,128)(2,1)S(1)}, bf16[2,2,256,128]{3,2,1,0:T(8,128)(2,1)}, u32[]{:S(2)}, u32[]{:S(2)}) collective-permute-start(bf16[2,2,256,128]{3,2,1,0:T(8,128)(2,1)S(1)} %pair.1.refs_0_.refs_2_), channel_id=1, source_target_pairs={{8,16},{16,8},{24,32},{32,24},{40,48},{48,40},{72,80},{80,72},{88,... | collective-permute-start | bytes 786440 | tf_op jit(solution)/shard_map/ppermute | solution.py:371
  40.2 61.5 %collective-permute-start.12 = (bf16[256,2560]{1,0:T(8,128)(2,1)S(1)}, bf16[256,2560]{1,0:T(8,128)(2,1)}, u32[]{:S(2)}, u32[]{:S(2)}) collective-permute-start(bf16[256,2560]{1,0:T(8,128)(2,1)S(1)} %pad_maximum_fusion.refs_0_.weight_ref), channel_id=1, source_target_pairs={{0,6},{2,0},{4,2},{6,4},{1,7},{3,1},{5,3},{7,5},{8,14},{10,8},{12,... | collective-permute-start | bytes 3932168 | tf_op jit(solution)/shard_map/ppermute | solution.py:438
  48.8 52.9 %collective-permute-start.11 = (bf16[256,2560]{1,0:T(8,128)(2,1)S(1)}, bf16[256,2560]{1,0:T(8,128)(2,1)}, u32[]{:S(2)}, u32[]{:S(2)}) collective-permute-start(bf16[256,2560]{1,0:T(8,128)(2,1)S(1)} %collective-permute-done.10.refs_1_), channel_id=1, source_target_pairs={{0,2},{2,4},{4,6},{6,0},{1,3},{3,5},{5,7},{7,1},{8,10},{10,12},{12... | collective-permute-start | bytes 3932168 | tf_op jit(solution)/shard_map/ppermute | solution.py:439
  56.4 18.8 %collective-permute-start.7 = (bf16[2,2,256,128]{3,2,1,0:T(8,128)(2,1)}, bf16[2,2,256,128]{3,2,1,0:T(8,128)(2,1)S(1)}, u32[]{:S(2)}, u32[]{:S(2)}) collective-permute-start(bf16[2,2,256,128]{3,2,1,0:T(8,128)(2,1)} %collective-permute-done.1.refs_3_.refs_2_), channel_id=1, source_target_pairs={{0,8},{8,0},{16,24},{24,16},{32,40},{40,32},{48,56},{56,48},{64,72... | collective-permute-start | bytes 786440 | tf_op jit(solution)/shard_map/ppermute | solution.py:371
  63.1 8.5 %collective-permute-start.2 = (bf16[2,2,256,128]{3,2,1,0:T(8,128)(2,1)}, bf16[2,2,256,128]{3,2,1,0:T(8,128)(2,1)S(1)}, u32[]{:S(2)}, u32[]{:S(2)}) collective-permute-start(bf16[2,2,256,128]{3,2,1,0:T(8,128)(2,1)} %collective-permute-done.1.refs_3_.refs_2_), channel_id=1, source_target_pairs={{0,128},{192,64},{1,129},{193,65},{2,130},{194,66},{3,131},{195,67... | collective-permute-start | bytes 786440 | tf_op jit(solution)/shard_map/ppermute | solution.py:425
  64.6 12.8 %collective-permute-start.8 = (bf16[2,2,256,128]{3,2,1,0:T(8,128)(2,1)}, bf16[2,2,256,128]{3,2,1,0:T(8,128)(2,1)S(1)}, u32[]{:S(2)}, u32[]{:S(2)}) collective-permute-start(bf16[2,2,256,128]{3,2,1,0:T(8,128)(2,1)} %collective-permute-done.1.refs_3_.refs_2_), channel_id=1, source_target_pairs={{8,16},{16,8},{24,32},{32,24},{40,48},{48,40},{72,80},{80,72},{88,... | collective-permute-start | bytes 786440 | tf_op jit(solution)/shard_map/ppermute | solution.py:371
  71.6 10.5 %collective-permute-start.3 = (bf16[2,2,256,128]{3,2,1,0:T(8,128)(2,1)S(1)}, bf16[2,2,256,128]{3,2,1,0:T(8,128)(2,1)S(1)}, u32[]{:S(2)}, u32[]{:S(2)}) collective-permute-start(bf16[2,2,256,128]{3,2,1,0:T(8,128)(2,1)S(1)} %collective-permute-done.2.refs_0_.refs_2_), channel_id=1, source_target_pairs={{64,72},{72,64},{80,88},{88,80},{96,104},{104,96},{112,120},{120,1... | collective-permute-start | bytes 786440 | tf_op jit(solution)/shard_map/ppermute | solution.py:371
  75.1 8.3 %collective-permute-start.4 = (bf16[2,2,256,128]{3,2,1,0:T(8,128)(2,1)S(1)}, bf16[2,2,256,128]{3,2,1,0:T(8,128)(2,1)S(1)}, u32[]{:S(2)}, u32[]{:S(2)}) collective-permute-start(bf16[2,2,256,128]{3,2,1,0:T(8,128)(2,1)S(1)} %collective-permute-done.2.refs_0_.refs_2_), channel_id=1, source_target_pairs={{72,80},{80,72},{88,96},{96,88},{104,112},{112,104},{136,144},{144... | collective-permute-start | bytes 786440 | tf_op jit(solution)/shard_map/ppermute | solution.py:371
  104.6 4.6 %collective-permute-start.13 = (bf16[256,2048]{1,0:T(8,128)(2,1)S(1)}, bf16[256,2048]{1,0:T(8,128)(2,1)S(1)}, u32[]{:S(2)}, u32[]{:S(2)}) collective-permute-start(bf16[256,2048]{1,0:T(8,128)(2,1)S(1)} %project.1.mine_ref), channel_id=1, source_target_pairs={{0,1},{1,0},{2,3},{3,2},{4,5},{5,4},{6,7},{7,6},{8,9},{9,8},{10,11... | collective-permute-start | bytes 3145736 | tf_op jit(solution)/shard_map/ppermute | solution.py:449
  111.6 7.7 %collective-permute-start.14 = (bf16[256,128]{1,0:T(8,128)(2,1)S(1)}, bf16[256,128]{1,0:T(8,128)(2,1)S(1)}, u32[]{:S(2)}, u32[]{:S(2)}) collective-permute-start(bf16[256,128]{1,0:T(8,128)(2,1)S(1)} %get-tuple-element.50), channel_id=1, source_target_pairs={{0,256},{256,0},{1,257},{257,1},{2,258},{258,2},{3,259},{259,3},{4... | collective-permute-start | bytes 196616 | tf_op jit(solution)/shard_map/ppermute | solution.py:451
  121.6 16.4 %collective-permute-start.17 = (bf16[2,2,256,128]{3,2,1,0:T(8,128)(2,1)S(1)}, bf16[2,2,256,128]{3,2,1,0:T(8,128)(2,1)S(1)}, u32[]{:S(2)}, u32[]{:S(2)}) collective-permute-start(bf16[2,2,256,128]{3,2,1,0:T(8,128)(2,1)S(1)} %get-tuple-element.63), channel_id=1, source_target_pairs={{64,72},{72,64},{80,88},{88,80},{96,104},{104,96},{112,120},{120,1... | collective-permute-start | bytes 786440 | tf_op jit(solution)/shard_map/ppermute | solution.py:371
  123.5 14.5 %collective-permute-start.18 = (bf16[2,2,256,128]{3,2,1,0:T(8,128)(2,1)S(1)}, bf16[2,2,256,128]{3,2,1,0:T(8,128)(2,1)S(1)}, u32[]{:S(2)}, u32[]{:S(2)}) collective-permute-start(bf16[2,2,256,128]{3,2,1,0:T(8,128)(2,1)S(1)} %get-tuple-element.64), channel_id=1, source_target_pairs={{72,80},{80,72},{88,96},{96,88},{104,112},{112,104},{136,144},{144... | collective-permute-start | bytes 786440 | tf_op jit(solution)/shard_map/ppermute | solution.py:371
  132.0 8.6 %collective-permute-start.15 = (bf16[2,2,256,128]{3,2,1,0:T(8,128)(2,1)S(1)}, bf16[2,2,256,128]{3,2,1,0:T(8,128)(2,1)S(1)}, u32[]{:S(2)}, u32[]{:S(2)}) collective-permute-start(bf16[2,2,256,128]{3,2,1,0:T(8,128)(2,1)S(1)} %get-tuple-element.60), channel_id=1, source_target_pairs={{0,8},{8,0},{16,24},{24,16},{32,40},{40,32},{48,56},{56,48},{64,72... | collective-permute-start | bytes 786440 | tf_op jit(solution)/shard_map/ppermute | solution.py:371
  134.0 8.9 %collective-permute-start.16 = (bf16[2,2,256,128]{3,2,1,0:T(8,128)(2,1)S(1)}, bf16[2,2,256,128]{3,2,1,0:T(8,128)(2,1)S(1)}, u32[]{:S(2)}, u32[]{:S(2)}) collective-permute-start(bf16[2,2,256,128]{3,2,1,0:T(8,128)(2,1)S(1)} %get-tuple-element.61), channel_id=1, source_target_pairs={{8,16},{16,8},{24,32},{32,24},{40,48},{48,40},{72,80},{80,72},{88,... | collective-permute-start | bytes 786440 | tf_op jit(solution)/shard_map/ppermute | solution.py:371
  138.1 5.5 %collective-permute-start.19 = (bf16[2,2,256,128]{3,2,1,0:T(8,128)(2,1)S(1)}, bf16[2,2,256,128]{3,2,1,0:T(8,128)(2,1)S(1)}, u32[]{:S(2)}, u32[]{:S(2)}) collective-permute-start(bf16[2,2,256,128]{3,2,1,0:T(8,128)(2,1)S(1)} %far_sum.1), channel_id=1, source_target_pairs={{128,0},{64,192},{129,1},{65,193},{130,2},{66,194},{131,3},{67,195... | collective-permute-start | bytes 786440 | tf_op jit(solution)/shard_map/ppermute | solution.py:461
  143.7 34.8 %collective-permute-start.22 = (bf16[2,2,256,128]{3,2,1,0:T(8,128)(2,1)S(1)}, bf16[2,2,256,128]{3,2,1,0:T(8,128)(2,1)S(1)}, u32[]{:S(2)}, u32[]{:S(2)}) collective-permute-start(bf16[2,2,256,128]{3,2,1,0:T(8,128)(2,1)S(1)} %merge.1), channel_id=1, source_target_pairs={{0,64},{64,0},{1,65},{65,1},{2,66},{66,2},{3,67},{67,3},{4,68},{68... | collective-permute-start | bytes 786440 | tf_op jit(solution)/shard_map/ppermute | solution.py:470
  156.2 23.1 %collective-permute-start.20 = (bf16[2,2,256,128]{3,2,1,0:T(8,128)(2,1)S(1)}, bf16[2,2,256,128]{3,2,1,0:T(8,128)(2,1)S(1)}, u32[]{:S(2)}, u32[]{:S(2)}) collective-permute-start(bf16[2,2,256,128]{3,2,1,0:T(8,128)(2,1)S(1)} %get-tuple-element.68), channel_id=1, source_target_pairs={{0,8},{8,0},{16,24},{24,16},{32,40},{40,32},{48,56},{56,48},{64,72... | collective-permute-start | bytes 786440 | tf_op jit(solution)/shard_map/ppermute | solution.py:371
  158.4 22.8 %collective-permute-start.21 = (bf16[2,2,256,128]{3,2,1,0:T(8,128)(2,1)S(1)}, bf16[2,2,256,128]{3,2,1,0:T(8,128)(2,1)S(1)}, u32[]{:S(2)}, u32[]{:S(2)}) collective-permute-start(bf16[2,2,256,128]{3,2,1,0:T(8,128)(2,1)S(1)} %get-tuple-element.69), channel_id=1, source_target_pairs={{8,16},{16,8},{24,32},{32,24},{40,48},{48,40},{72,80},{80,72},{88,... | collective-permute-start | bytes 786440 | tf_op jit(solution)/shard_map/ppermute | solution.py:371
  181.3 10.2 %collective-permute-start.23 = (bf16[3,256,128]{2,1,0:T(8,128)(2,1)S(1)}, bf16[3,256,128]{2,1,0:T(8,128)(2,1)S(1)}, u32[]{:S(2)}, u32[]{:S(2)}) collective-permute-start(bf16[3,256,128]{2,1,0:T(8,128)(2,1)S(1)} %frame_sum.1), channel_id=1, source_target_pairs={{0,256},{256,0},{1,257},{257,1},{2,258},{258,2},{3,259},{259,3},{4... | collective-permute-start | bytes 589832 | tf_op jit(solution)/shard_map/ppermute | solution.py:477
